TPU v7x, 32 devices: a whole 2x2x4 slice. The times are simulated.
32 devices in a mesh: groups: 2 (over y), comp: 4 (over x, core), expert: 4 (over z).
Axes of the slice: x: 2, y: 2, z: 4, core: 2. Of those that a mesh axis runs over, the one named last changes fastest.
Arguments:
- states: bfloat16 [4, 768, 3072], P('comp', ('groups', 'expert')), parts along dimension 1, may hold values from -9 to 9
- routes: int32 [4, 768, 2], P('comp', ('groups', 'expert')), parts along dimension 1, may hold values from 0 to 3, as said below
- slots: int32 [4, 768, 2], P('comp', ('groups', 'expert')), parts along dimension 1, may hold values from 0 to 71, as said below
- timesteps: int32 [8], P(('groups', 'comp')), parts along dimension 0, may hold values from 0 to 49
- router_weight: bfloat16 [4, 3072, 4], P('comp'), may hold values from -0.109375 to 0.109375
- expert_in: bfloat16 [4, 3072, 8192], P('comp', None, 'expert'), may hold values from -0.109375 to 0.109375
- expert_out: bfloat16 [4, 8192, 3072], P('comp', 'expert'), may hold values from -0.125 to 0.125
- modulation: bfloat16 [50, 3, 3072], replicated, may hold values from -2 to 2
Outputs:
- new_states: bfloat16 [4, 768, 3072], P('comp', ('groups', 'expert')), parts along dimension 1
There are 2 independent parts, one for each index of `groups`. A program takes and returns all parts, laid end to end along the dimension named above; an argument that names none is the same for every part. Nothing has to cross between parts.
Inputs may be any that keep to these rules, and one draw needn't show every extreme that they name: `routes`: in every aligned block of 96 tokens a token's two experts differ, each expert is named by at most 72 tokens, and in each component one expert is named by exactly 72 tokens of every block. Within one block and one expert the slots of the routes to it are distinct and numbered from 0 in token order.
All inputs are finite; a program needn't handle non-finite values.
Results may differ from a plain program's by a relative error of at most 0.0043.
Values may be sent and summed in bfloat16 or wider, within the bound.
No kernel may reach another device: no remote copies, remote signals or barrier semaphores. Data moves between devices by JAX's collectives and lax.ppermute only.
A program may use at most 128 MiB of HBM per device.

v0:
```python
import jax
import jax.numpy as jnp
from jax import lax
from jax.sharding import PartitionSpec as P


def shifted(block, axis, distance):
    devices = range(lax.axis_size(axis))
    route = [((i - distance) % len(devices), i) for i in devices]
    return lax.ppermute(block, axis, route)


def modulate(incoming, mod):
    values = incoming.astype(jnp.float32)
    centred = values - jnp.mean(values, axis=-1, keepdims=True)
    spread = jnp.mean(centred * centred, axis=-1, keepdims=True)
    normed = centred * lax.rsqrt(spread + 1e-06)
    return (normed * (1.0 + mod[0]) + mod[1]).astype(jnp.bfloat16)


def gating(modulated, weight, chosen):
    logits = jnp.dot(modulated, weight, preferred_element_type=jnp.float32)
    picks = chosen[..., None] == jnp.arange(weight.shape[1], dtype=jnp.int32)
    selected = jnp.sum(jnp.where(picks, logits[:, None, :], jnp.float32(0.0)), axis=-1)
    sig = jax.nn.sigmoid(selected)
    return sig / jnp.sum(sig, axis=1, keepdims=True)


def body(states, routes, slots, timesteps, router_weight, expert_in, expert_out, modulation):
    devices = lax.axis_size("expert")
    tokens_here = states.shape[1]
    width = states.shape[2]
    experts = router_weight.shape[2]
    shards = devices // experts
    most = 3 * tokens_here // 4
    incoming = shifted(states[0], "comp", 1)
    mod = modulation[timesteps[0]].astype(jnp.float32)
    modulated = modulate(incoming, mod)
    chosen = routes[0]
    gates = gating(modulated, router_weight[0], chosen)
    target = chosen * most + slots[0]
    place = target[..., None] == jnp.arange(experts * most, dtype=jnp.int32)
    occupied = jnp.any(place, axis=1).astype(jnp.bfloat16)
    buffer = jnp.einsum(
        "tr,td->rd", occupied, modulated, preferred_element_type=jnp.float32
    ).astype(jnp.bfloat16)
    mix_weights = jnp.sum(jnp.where(place, gates[..., None], jnp.float32(0.0)), axis=1)
    w_first = expert_in[0]
    w_second = expert_out[0]
    copies = jnp.broadcast_to(
        buffer.reshape(experts, 1, most, width), (experts, shards, most, width)
    )
    outgoing = copies.reshape(devices, most, width)
    received = lax.all_to_all(outgoing, "expert", split_axis=0, concat_axis=0, tiled=True)
    count = received.shape[1]
    hidden = jax.nn.gelu(
        jnp.dot(received.reshape(-1, width), w_first, preferred_element_type=jnp.float32),
        approximate=True,
    )
    partial_value = (
        jnp.dot(hidden.astype(jnp.bfloat16), w_second, preferred_element_type=jnp.float32)
        .astype(jnp.bfloat16)
        .reshape(devices, count, width)
    )
    returned = lax.all_to_all(partial_value, "expert", split_axis=0, concat_axis=0, tiled=True)
    combined = jnp.sum(returned.reshape(experts, shards, most, width).astype(jnp.float32), axis=1)
    mixture = jnp.dot(
        mix_weights,
        combined.reshape(experts * most, width),
        precision=lax.Precision.HIGHEST,
        preferred_element_type=jnp.float32,
    )
    updated = incoming.astype(jnp.float32) + (1.0 + mod[2]) * mixture
    return updated.astype(jnp.bfloat16)[None]


def solution(mesh):
    in_specs = (
        P("comp", ("groups", "expert"), None),
        P("comp", ("groups", "expert"), None),
        P("comp", ("groups", "expert"), None),
        P(("groups", "comp")),
        P("comp", None, None),
        P("comp", None, "expert"),
        P("comp", "expert", None),
        P(),
    )
    out_specs = P("comp", ("groups", "expert"), None)
    return jax.shard_map(body, mesh=mesh, in_specs=in_specs, out_specs=out_specs, check_vma=False)
```

profile of v0, /device:TPU:0, one launch (start us, length us, event | category | flops | bytes accessed | tf_op | source)
XLA Modules:
  0.0 121.2 jit_solution(6010659223060311610)
XLA Ops:
  0.0 0.0 copy-start
  0.0 0.5 collective-permute-start
  1.1 0.7 bitcast_add_fusion
  1.8 0.1 fusion.30
  1.9 0.9 dynamic-slice_convert_fusion
  2.9 7.3 %collective-permute-done = bf16[96,3072]{1,0:T(8,128)(2,1)S(1)} collective-permute-done((bf16[96,3072]{1,0:T(8,128)(2,1)}, bf16[96,3072]{1,0:T(8,128)(2,1)S(1)}, u32[]{:S(2)}, u32[]{:S(2)}) %collective-permute-start) | collective-permute-done | bytes 589856 | tf_op jit(solution)/shard_map/ppermute | solution.py:10
  10.2 0.2 convert_reduce_fusion
  10.3 0.3 fusion.24
  10.7 0.8 convolution_convert_fusion
  11.4 46.1 %all_to_all.10 = bf16[4,72,3072]{2,1,0:T(8,128)(2,1)S(1)} all-to-all(bf16[4,72,3072]{2,1,0:T(8,128)(2,1)S(1)} %bitcast.40), channel_id=1, replica_groups=mesh['groups'=2,'comp'=4,'expert'=4] {'expert'}, dimensions={0} | all-to-all | bytes 3538944 | tf_op jit(solution)/shard_map/all_to_all | solution.py:54
  57.6 17.3 %fusion.4 = bf16[288,3072]{1,0:T(8,128)(2,1)} fusion(bf16[1,2048,3072]{2,1,0:T(8,128)(2,1)} %param.14, bf16[288,3072]{1,0:T(8,128)(2,1)S(1)} %bitcast.42, bf16[1,3072,2048]{2,1,0:T(8,128)(2,1)} %param.13), kind=kOutput, calls=%fused_computation.5 | convolution fusion | flops 7253950464 | bytes 28704768 | tf_op jit(solution)/shard_map/dot_general | solution.py:61
  74.9 0.0 copy-start.1
  74.9 3.7 %all-to-all-start.1 = ((bf16[4,72,3072]{2,1,0:T(8,128)(2,1)}), bf16[4,72,3072]{2,1,0:T(8,128)(2,1)S(1)}, u32[]{:S(2)}, u32[]{:S(2)}) async-start(bf16[4,72,3072]{2,1,0:T(8,128)(2,1)} %bitcast.41), calls=%async_computation.1 | async-start | bytes 3538944 | tf_op jit(solution)/shard_map/all_to_all | solution.py:65
  78.6 0.0 copy-done
  78.6 0.4 fusion.31
  79.0 0.0 copy-done.1
  79.1 0.1 select_reduce_fusion
  79.2 39.8 %all-to-all-done.1 = bf16[4,72,3072]{2,1,0:T(8,128)(2,1)S(1)} async-done(((bf16[4,72,3072]{2,1,0:T(8,128)(2,1)}), bf16[4,72,3072]{2,1,0:T(8,128)(2,1)S(1)}, u32[]{:S(2)}, u32[]{:S(2)}) %all-to-all-start.1) | async-done | bytes 1769504 | tf_op jit(solution)/shard_map/all_to_all | solution.py:65
  119.0 2.2 %fusion.9 = bf16[1,96,3072]{2,1,0:T(8,128)(2,1)} fusion(f32[96,288]{1,0:T(8,128)S(1)} %select_reduce_fusion, bf16[288,3072]{1,0:T(8,128)(2,1)S(1)} %bitcast.39, bf16[96,3072]{1,0:T(8,128)(2,1)S(1)} %collective-permute-done, f32[3072]{0:T(1024)S(1)} %bitcast.43), kind=kOutput, calls=%fused_computation.10 | convolution fusion | flops 1020395520 | bytes 3072000 | tf_op jit(solution)/shard_map/dot_general | solution.py:67
  (6 shorter events, 0.1 us)
Async XLA Ops:
  0.0 78.6 %copy-start = (bf16[1,3072,4]{1,2,0:T(4,128)(2,1)S(1)}, bf16[1,3072,4]{1,2,0:T(4,128)(2,1)}, u32[]{:S(2)}) copy-start(bf16[1,3072,4]{1,2,0:T(4,128)(2,1)} %param.12) | copy-start | bytes 73732
  0.0 10.2 %collective-permute-start = (bf16[96,3072]{1,0:T(8,128)(2,1)}, bf16[96,3072]{1,0:T(8,128)(2,1)S(1)}, u32[]{:S(2)}, u32[]{:S(2)}) collective-permute-start(bf16[96,3072]{1,0:T(8,128)(2,1)} %bitcast.49), channel_id=1, source_target_pairs={{12,0},{0,4},{4,8},{8,12},{13,1},{1,5},{5,9},{9,13},{14,2},{2,6},{... | collective-permute-start | bytes 1769480 | tf_op jit(solution)/shard_map/ppermute | solution.py:10
  74.9 4.1 %copy-start.1 = (s32[1,96,2]{1,2,0:T(2,128)S(1)}, s32[1,96,2]{1,2,0:T(2,128)}, u32[]{:S(2)}) copy-start(s32[1,96,2]{1,2,0:T(2,128)} %param.9) | copy-start | bytes 2308
  74.9 44.1 %all-to-all-start.1 = ((bf16[4,72,3072]{2,1,0:T(8,128)(2,1)}), bf16[4,72,3072]{2,1,0:T(8,128)(2,1)S(1)}, u32[]{:S(2)}, u32[]{:S(2)}) async-start(bf16[4,72,3072]{2,1,0:T(8,128)(2,1)} %bitcast.41), calls=%async_computation.1 | async-start | bytes 3538944 | tf_op jit(solution)/shard_map/all_to_all | solution.py:65
where the time goes:
time: 122 us; the launch traced here: 121 us
  waiting for transfers between devices  47 us (39%)
  blocking collectives  46.1 us (38%)
  matrix products  20.7 us (17%)
  starting transfers between devices  4.16 us (3%)
  other arithmetic  2.47 us (2%)
    all_to_all x1, blocking collectives, body(): lax.all_to_all(outgoing, 'expert', split_axis=0, concat_axis=0, tiled=True)  46.1 us
    all_to_all x1, waiting for transfers between devices, body(): lax.all_to_all(partial_value, 'expert', split_axis=0, concat_axis=0, tile...  39.8 us
    dot_general x1, matrix products, body(): jnp.dot(hidden.astype(jnp.bfloat16), w_second, preferred_element_type=jnp...  17.3 us
    ppermute x1, waiting for transfers between devices, shifted(): return lax.ppermute(block, axis, route)  7.25 us
    all_to_all x1, starting transfers between devices, body(): lax.all_to_all(partial_value, 'expert', split_axis=0, concat_axis=0, tile...  3.71 us
  transfers between devices with their start and end apart: 2, of which 2 were waited for; matrix products, arithmetic and copies ran while one was open for 2% of the time, Pallas kernels for 0%

commit v1 on v0

--- a/solution.py
+++ b/solution.py
@@ -1,7 +1,13 @@
+import functools
+
 import jax
 import jax.numpy as jnp
 from jax import lax
+from jax.experimental import pallas as pl
+from jax.experimental.pallas import tpu as pltpu
 from jax.sharding import PartitionSpec as P
+
+MIB = 1024 * 1024
 
 
 def shifted(block, axis, distance):
@@ -10,23 +16,206 @@
     return lax.ppermute(block, axis, route)
 
 
-def modulate(incoming, mod):
+def swapped(block, mask):
+    return lax.ppermute(block, "expert", [(e, e ^ mask) for e in range(lax.axis_size("expert"))])
+
+
+def advanced(block, mask):
+    comps, experts = lax.axis_size("comp"), lax.axis_size("expert")
+    route = [
+        (c * experts + e, (c + 1) % comps * experts + (e ^ mask))
+        for c in range(comps)
+        for e in range(experts)
+    ]
+    return lax.ppermute(block, ("comp", "expert"), route)
+
+
+def modulate(incoming, scale, shift):
     values = incoming.astype(jnp.float32)
     centred = values - jnp.mean(values, axis=-1, keepdims=True)
     spread = jnp.mean(centred * centred, axis=-1, keepdims=True)
     normed = centred * lax.rsqrt(spread + 1e-06)
-    return (normed * (1.0 + mod[0]) + mod[1]).astype(jnp.bfloat16)
+    return (normed * (1.0 + scale) + shift).astype(jnp.bfloat16)
+
+
+def pick_logits(logits, chosen):
+    picks = chosen[..., None] == jnp.arange(logits.shape[1], dtype=jnp.int32)
+    return jnp.sum(jnp.where(picks, logits[:, None, :], jnp.float32(0.0)), axis=-1)
 
 
 def gating(modulated, weight, chosen):
     logits = jnp.dot(modulated, weight, preferred_element_type=jnp.float32)
-    picks = chosen[..., None] == jnp.arange(weight.shape[1], dtype=jnp.int32)
-    selected = jnp.sum(jnp.where(picks, logits[:, None, :], jnp.float32(0.0)), axis=-1)
-    sig = jax.nn.sigmoid(selected)
+    sig = jax.nn.sigmoid(pick_logits(logits, chosen))
     return sig / jnp.sum(sig, axis=1, keepdims=True)
 
 
-def body(states, routes, slots, timesteps, router_weight, expert_in, expert_out, modulation):
+def slot_rows(chosen, slots, expert, most):
+    taken = jnp.where(chosen == expert, slots, -1)
+    rows = lax.broadcasted_iota(jnp.int32, (most, chosen.shape[0]), 0)
+    return ((rows == taken[None, :, 0]) | (rows == taken[None, :, 1])).astype(jnp.bfloat16)
+
+
+def select(rows, block):
+    return jnp.dot(rows, block, preferred_element_type=jnp.float32).astype(jnp.bfloat16)
+
+
+def spread_back(rows, result):
+    return lax.dot_general(rows, result, (((0,), (0,)), ((), ())), preferred_element_type=jnp.float32)
+
+
+def tiles(size, step):
+    return [(i, min(step, size - i)) for i in range(0, size, step)]
+
+
+def experts_on(x, w1, w2, hidden, store):
+    for start, size in tiles(w1.shape[1], 512):
+        value = jnp.dot(x[...], w1[:, start:start + size], preferred_element_type=jnp.float32)
+        hidden[:, start:start + size] = jax.nn.gelu(value, approximate=True).astype(jnp.bfloat16)
+    for start, size in tiles(w2.shape[1], 512):
+        value = jnp.dot(hidden[...], w2[:, start:start + size], preferred_element_type=jnp.float32)
+        store(start, size, value)
+
+
+def near_kernel(most, own, rows, sib, mod, w1, w2, out_own, out_sib, x, hidden):
+    pad = x.shape[0] // 2
+    x[0:pad, :] = jnp.zeros((pad, x.shape[1]), x.dtype)
+    x[pad:2 * pad, :] = jnp.zeros((pad, x.shape[1]), x.dtype)
+    x[0:most, :] = select(rows[...], own[...])
+    x[pad:pad + most, :] = modulate(sib[...], mod[0:1, :], mod[1:2, :])
+
+    def store(start, size, value):
+        out_own[:, start:start + size] = value[0:most].astype(jnp.bfloat16)
+        out_sib[:, start:start + size] = value[pad:pad + most].astype(jnp.bfloat16)
+
+    experts_on(x, w1, w2, hidden, store)
+
+
+def far_kernel(most, cut, first, second, mod, w1, w2, out, raw, x, hidden):
+    raw[:, 0:cut] = first[...].astype(jnp.float32)
+    raw[:, cut:] = second[...].astype(jnp.float32)
+    x[...] = jnp.zeros_like(x)
+    x[0:most, :] = modulate(raw[...], mod[0:1, :], mod[1:2, :])
+
+    def store(start, size, value):
+        out[:, start:start + size] = value[0:most].astype(jnp.bfloat16)
+
+    experts_on(x, w1, w2, hidden, store)
+
+
+def cost(rows, width, hid):
+    return pl.CostEstimate(
+        flops=4 * rows * width * hid, bytes_accessed=4 * rows * width, transcendentals=rows * hid
+    )
+
+
+def params():
+    return pltpu.CompilerParams(vmem_limit_bytes=16 * MIB)
+
+
+def near(own, rows, sib, mod, w1, w2):
+    most, width = sib.shape
+    pad = -(-most // 16) * 16
+    hid = w1.shape[1]
+    vmem = pl.BlockSpec(memory_space=pltpu.VMEM)
+    shape = jax.ShapeDtypeStruct((most, width), jnp.bfloat16)
+    return pl.pallas_call(
+        functools.partial(near_kernel, most),
+        out_shape=(shape, shape),
+        in_specs=[vmem] * 6,
+        out_specs=(vmem, vmem),
+        scratch_shapes=[
+            pltpu.VMEM((2 * pad, width), jnp.bfloat16),
+            pltpu.VMEM((2 * pad, hid), jnp.bfloat16),
+        ],
+        compiler_params=params(),
+        cost_estimate=cost(2 * most, width, hid),
+    )(own, rows, sib, mod, w1, w2)
+
+
+def far(first, second, mod, w1, w2):
+    most, cut = first.shape
+    width = cut + second.shape[1]
+    pad = -(-most // 16) * 16
+    hid = w1.shape[1]
+    vmem = pl.BlockSpec(memory_space=pltpu.VMEM)
+    return pl.pallas_call(
+        functools.partial(far_kernel, most, cut),
+        out_shape=jax.ShapeDtypeStruct((most, width), jnp.bfloat16),
+        in_specs=[vmem] * 5,
+        out_specs=vmem,
+        scratch_shapes=[
+            pltpu.VMEM((most, width), jnp.float32),
+            pltpu.VMEM((pad, width), jnp.bfloat16),
+            pltpu.VMEM((pad, hid), jnp.bfloat16),
+        ],
+        compiler_params=params(),
+        cost_estimate=cost(most, width, hid),
+    )(first, second, mod, w1, w2)
+
+
+def quad_body(states, routes, slots, timesteps, router_weight, expert_in, expert_out, modulation):
+    source = states[0]
+    width = source.shape[1]
+    most = 3 * source.shape[0] // 4
+    cut = width // 256 * 128
+    here = lax.axis_index("expert")
+    chosen, places = routes[0], slots[0]
+    w1 = pltpu.with_memory_space_constraint(expert_in[0], pltpu.VMEM)
+    w2 = pltpu.with_memory_space_constraint(expert_out[0], pltpu.VMEM)
+
+    crossed = advanced(source[:, :cut], 2)
+    table = jnp.concatenate([chosen, places], axis=1)
+    ahead = shifted(table, "comp", -1)
+    incoming = shifted(source, "comp", 1)
+    mod = modulation[timesteps[0]].astype(jnp.float32)
+
+    def ahead_rows(mask):
+        return slot_rows(ahead[:, :2], ahead[:, 2:], here ^ mask, most)
+
+    sib = advanced(select(ahead_rows(1), source), 1)
+    far_x = advanced(select(ahead_rows(2), source[:, cut:]), 2)
+    far_z = advanced(select(ahead_rows(3), source[:, cut:]), 3)
+
+    modulated = modulate(incoming, mod[0], mod[1])
+    gates = gating(modulated, router_weight[0], chosen)
+    packed = jnp.concatenate([table.astype(jnp.float32), gates], axis=1)
+    other = swapped(packed, 2)
+    x_chosen = other[:, 0:2].astype(jnp.int32)
+    x_places = other[:, 2:4].astype(jnp.int32)
+    x_gates = other[:, 4:6]
+
+    def gate_of(expert, chosen, gates):
+        return jnp.sum(jnp.where(chosen == expert, gates, 0.0), axis=1, keepdims=True)
+
+    rows_x = slot_rows(x_chosen, x_places, here, most)
+    rows_r = slot_rows(x_chosen, x_places, here ^ 1, most)
+    relayed = swapped(select(rows_r, crossed), 1)
+
+    rows_own = slot_rows(chosen, places, here, most)
+    y_own, y_sib = near(modulated, rows_own, sib, mod, w1, w2)
+    back_s = swapped(y_sib, 1)
+    y_x = far(select(rows_x, crossed), far_x, mod, w1, w2)
+    back_x = swapped(y_x[:, cut:], 2)
+    y_z = far(relayed, far_z, mod, w1, w2)
+    lent = swapped(y_z[:, :cut], 1)
+    back_z = swapped(y_z[:, cut:], 3)
+    joint = gate_of(here, x_chosen, x_gates) * spread_back(rows_x, y_x[:, :cut])
+    joint += gate_of(here ^ 1, x_chosen, x_gates) * spread_back(rows_r, lent)
+    back_u = swapped(joint.astype(jnp.bfloat16), 2)
+
+    def mixed(mask, result):
+        rows = slot_rows(chosen, places, here ^ mask, most)
+        return gate_of(here ^ mask, chosen, gates) * spread_back(rows, result)
+
+    base = mixed(0, y_own) + mixed(1, back_s)
+    left = base[:, :cut] + back_u.astype(jnp.float32)
+    right = base[:, cut:] + mixed(2, back_x) + mixed(3, back_z)
+    mixture = jnp.concatenate([left, right], axis=1)
+    updated = incoming.astype(jnp.float32) + (1.0 + mod[2]) * mixture
+    return updated.astype(jnp.bfloat16)[None]
+
+
+def general_body(states, routes, slots, timesteps, router_weight, expert_in, expert_out, modulation):
     devices = lax.axis_size("expert")
     tokens_here = states.shape[1]
     width = states.shape[2]
@@ -35,7 +224,7 @@
     most = 3 * tokens_here // 4
     incoming = shifted(states[0], "comp", 1)
     mod = modulation[timesteps[0]].astype(jnp.float32)
-    modulated = modulate(incoming, mod)
+    modulated = modulate(incoming, mod[0], mod[1])
     chosen = routes[0]
     gates = gating(modulated, router_weight[0], chosen)
     target = chosen * most + slots[0]
@@ -74,6 +263,12 @@
     return updated.astype(jnp.bfloat16)[None]
 
 
+def body(states, routes, slots, timesteps, router_weight, *rest):
+    quad = lax.axis_size("expert") == router_weight.shape[2] == 4
+    chosen_body = quad_body if quad else general_body
+    return chosen_body(states, routes, slots, timesteps, router_weight, *rest)
+
+
 def solution(mesh):
     in_specs = (
         P("comp", ("groups", "expert"), None),

time: 122 us -> 109 us (0.89)
  blocking collectives: 46.1 us -> 0 us
  starting transfers between devices: 4.16 us -> 22.6 us
  matrix products: 20.7 us -> 4.14 us
  Pallas kernels: 0 us -> 14.7 us
  local copies, waits for them, and re-layouts: 0.01 us -> 10.3 us
  waiting for transfers between devices: 47 us -> 52.3 us
    ppermute x0 -> x11, waiting for transfers between devices: none -> 52.3 us  [the longest x7 29.7 us: swapped(): lax.ppermute(block, 'expert', [(e, e ^ mask) for e in range(lax.axis_size...]
    all_to_all x1 -> x0, blocking collectives: 46.1 us -> none  [body(): lax.all_to_all(outgoing, 'expert', split_axis=0, concat_axis=0, tiled=True)]
    all_to_all x1 -> x0, waiting for transfers between devices: 39.8 us -> none  [body(): lax.all_to_all(partial_value, 'expert', split_axis=0, concat_axis=0, tile...]
    ppermute x0 -> x11, starting transfers between devices: none -> 22 us  [the longest x7 12.4 us: swapped(): lax.ppermute(block, 'expert', [(e, e ^ mask) for e in range(lax.axis_size...]
    dot_general x3 -> x11, matrix products: 20.3 us -> 3.89 us  [the longest x5 2.01 us: select(): jnp.dot(rows, block, preferred_element_type=jnp.float32)]
    pallas_call x0 -> x3, Pallas kernels: none -> 14.7 us  [the longest x2 9.82 us: far(): pl.pallas_call(functools.partial(far_kernel, most, cut), out_shape=jax.Sh...]
    unnamed x4 -> x14, local copies, waits for them, and re-layouts: 0.01 us -> 9.17 us
    ppermute x1 -> x2, waiting for transfers between devices: 7.25 us -> 0.01 us  [shifted(): return lax.ppermute(block, axis, route)]
  transfers between devices with their start and end apart: 2 -> 13, of which waited for: 2 -> 5; matrix products, arithmetic and copies ran while one was open for 2% -> 7% of each run, Pallas kernels for 0% -> 14%
where the time goes in v1:
time: 109 us; the launch traced here: 108 us
  waiting for transfers between devices  52.3 us (48%)
  starting transfers between devices  22.6 us (21%)
  Pallas kernels  14.7 us (13%)
  local copies, waits for them, and re-layouts  10.3 us (9%)
  matrix products  4.14 us (4%)
  other arithmetic  3.43 us (3%)
    ppermute x7, waiting for transfers between devices, swapped(): lax.ppermute(block, 'expert', [(e, e ^ mask) for e in range(lax.axis_size...  29.7 us
    ppermute x4, waiting for transfers between devices, advanced(): return lax.ppermute(block, ('comp', 'expert'), route)  22.6 us
    ppermute x7, starting transfers between devices, swapped(): lax.ppermute(block, 'expert', [(e, e ^ mask) for e in range(lax.axis_size...  12.4 us
    pallas_call x2, Pallas kernels, far(): pl.pallas_call(functools.partial(far_kernel, most, cut), out_shape=jax.Sh...  9.82 us
    ppermute x4, starting transfers between devices, advanced(): return lax.ppermute(block, ('comp', 'expert'), route)  9.59 us
    unnamed x14, local copies, waits for them, and re-layouts  9.17 us
    pallas_call x1, Pallas kernels, near(): pl.pallas_call(functools.partial(near_kernel, most), out_shape=(shape, sh...  4.89 us
  transfers between devices with their start and end apart: 13, of which 5 were waited for; matrix products, arithmetic and copies ran while one was open for 7% of the time, Pallas kernels for 14%

profile of v1, /device:TPU:0, one launch (start us, length us, event | category | flops | bytes accessed | tf_op | source)
XLA Modules:
  0.0 108.5 jit_solution(16830203789098873835)
XLA Ops:
  0.0 0.0 copy-start
  0.0 0.0 copy-start.4
  0.0 0.5 collective-permute-start
  0.5 1.0 slice.150
  1.5 4.8 %collective-permute-start.5 = (bf16[96,1536]{1,0:T(8,128)(2,1)S(1)}, bf16[96,1536]{1,0:T(8,128)(2,1)S(1)}, u32[]{:S(2)}, u32[]{:S(2)}) collective-permute-start(bf16[96,1536]{1,0:T(8,128)(2,1)S(1)} %slice.150), channel_id=1, source_target_pairs={{0,6},{1,7},{2,4},{3,5},{4,10},{5,11},{6,8},{7,9},{8,14},{9,15},{1... | collective-permute-start | bytes 884744 | tf_op jit(solution)/shard_map/ppermute | solution.py:30
  6.3 0.7 pad_add_fusion
  7.0 0.1 collective-permute-start.1
  7.8 0.0 copy-done
  7.9 0.7 broadcast_select_fusion
  8.7 0.0 collective-permute-done.1
  8.7 1.2 %convolution_convert_fusion.3 = bf16[72,1536]{1,0:T(8,128)(2,1)S(1)} fusion(bf16[96,3072]{1,0:T(8,128)(2,1)} %bitcast.97, s32[96]{0:T(128)S(1)} %get-tuple-element.54, s32[96]{0:T(128)S(1)} %get-tuple-element.55), kind=kOutput, calls=%fused_computation.8 | convolution fusion | flops 21364992 | bytes 516864 | tf_op jit(solution)/shard_map/dot_general | solution.py:59
  9.9 2.1 %collective-permute-start.6 = (bf16[72,1536]{1,0:T(8,128)(2,1)S(1)}, bf16[72,1536]{1,0:T(8,128)(2,1)S(1)}, u32[]{:S(2)}, u32[]{:S(2)}) collective-permute-start(bf16[72,1536]{1,0:T(8,128)(2,1)S(1)} %convolution_convert_fusion.3), channel_id=1, source_target_pairs={{0,6},{1,7},{2,4},{3,5},{4,10},{5,11},{6,8},{7,9},{8,14},{9,15},{1... | collective-permute-start | bytes 663560 | tf_op jit(solution)/shard_map/ppermute | solution.py:30
  12.0 0.0 copy-done.4
  12.0 0.2 convolution_convert_fusion.1
  12.2 2.6 %collective-permute-start.8 = (bf16[72,1536]{1,0:T(8,128)(2,1)S(1)}, bf16[72,1536]{1,0:T(8,128)(2,1)S(1)}, u32[]{:S(2)}, u32[]{:S(2)}) collective-permute-start(bf16[72,1536]{1,0:T(8,128)(2,1)S(1)} %convolution_convert_fusion.1), channel_id=1, source_target_pairs={{0,7},{1,6},{2,5},{3,4},{4,11},{5,10},{6,9},{7,8},{8,15},{9,14},{1... | collective-permute-start | bytes 663560 | tf_op jit(solution)/shard_map/ppermute | solution.py:30
  14.8 0.3 convolution_convert_fusion
  15.1 0.0 copy-start.5
  15.1 0.1 collective-permute-start.2
  15.1 0.0 collective-permute-done
  15.1 0.2 convert_reduce_fusion
  15.3 0.0 copy-start.6
  15.3 0.3 fusion.3
  15.7 0.3 fusion.6.own
  16.0 0.0 copy-done.5
  16.0 0.2 fusion.38
  16.2 0.0 copy-done.6
  16.3 2.7 %collective-permute-start.4 = (f32[96,6]{0,1:T(8,128)S(1)}, f32[96,6]{0,1:T(8,128)S(1)}, u32[]{:S(2)}, u32[]{:S(2)}) collective-permute-start(f32[96,6]{0,1:T(8,128)S(1)} %pad_maximum_fusion), channel_id=1, source_target_pairs={{0,2},{1,3},{2,0},{3,1},{4,6},{5,7},{6,4},{7,5},{8,10},{9,11},{10,... | collective-permute-start | bytes 6920 | tf_op jit(solution)/shard_map/ppermute | solution.py:20
  19.0 22.5 %collective-permute-done.2.sib = bf16[72,3072]{1,0:T(8,128)(2,1)S(1)} collective-permute-done((bf16[72,3072]{1,0:T(8,128)(2,1)S(1)}, bf16[72,3072]{1,0:T(8,128)(2,1)S(1)}, u32[]{:S(2)}, u32[]{:S(2)}) %collective-permute-start.2) | collective-permute-done | bytes 442400 | tf_op jit(solution)/shard_map/ppermute | solution.py:30
  41.6 0.0 copy-start.1
  41.6 4.6 %copy-done.1 = bf16[1,3072,2048]{2,1,0:T(8,128)(2,1)S(1)} copy-done((bf16[1,3072,2048]{2,1,0:T(8,128)(2,1)S(1)}, bf16[1,3072,2048]{2,1,0:T(8,128)(2,1)}, u32[]{:S(2)}) %copy-start.1) | copy-done | bytes 12582936
  46.2 0.0 copy-start.3
  46.2 4.6 %copy-done.3 = bf16[1,2048,3072]{2,1,0:T(8,128)(2,1)S(1)} copy-done((bf16[1,2048,3072]{2,1,0:T(8,128)(2,1)S(1)}, bf16[1,2048,3072]{2,1,0:T(8,128)(2,1)}, u32[]{:S(2)}) %copy-start.3) | copy-done | bytes 12582936
  50.7 0.0 copy-start.2
  50.8 4.9 %shard_map.82 = (bf16[72,3072]{1,0:T(8,128)(2,1)S(1)}, bf16[72,3072]{1,0:T(8,128)(2,1)S(1)}) custom-call(bf16[96,3072]{1,0:T(8,128)(2,1)S(1)} %fusion.6.own, bf16[72,96]{1,0:T(8,128)(2,1)S(1)} %fusion.37.rows, bf16[72,3072]{1,0:T(8,128)(2,1)S(1)} %collective-permute-done.2.sib, f32[3,3072]{1,0:T(4,128)S(1)} %get-tuple-element.21.mod, ...), custom_call_target="tpu_custom_call" | custom-call | flops 3623878656 | bytes 1769472 | tf_op jit(solution)/shard_map/pallas_call | solution.py:121
  55.6 0.1 collective-permute-start.3
  55.7 0.0 collective-permute-done.4
  55.8 0.0 collective-permute-done.5
  55.8 0.2 convolution_convert_fusion.2
  56.0 2.1 %collective-permute-start.7 = (bf16[72,1536]{1,0:T(8,128)(2,1)S(1)}, bf16[72,1536]{1,0:T(8,128)(2,1)S(1)}, u32[]{:S(2)}, u32[]{:S(2)}) collective-permute-start(bf16[72,1536]{1,0:T(8,128)(2,1)S(1)} %convolution_convert_fusion.2), channel_id=1, source_target_pairs={{0,1},{1,0},{2,3},{3,2},{4,5},{5,4},{6,7},{7,6},{8,9},{9,8},{10,11... | collective-permute-start | bytes 663560 | tf_op jit(solution)/shard_map/ppermute | solution.py:20
  58.0 0.2 convolution_convert_fusion.4.first
  58.2 0.0 collective-permute-done.6.second
  58.3 0.0 copy-done.2
  58.3 4.8 %shard_map.83 = bf16[72,3072]{1,0:T(8,128)(2,1)S(1)} custom-call(bf16[72,1536]{1,0:T(8,128)(2,1)S(1)} %convolution_convert_fusion.4.first, bf16[72,1536]{1,0:T(8,128)(2,1)S(1)} %collective-permute-done.6.second, f32[3,3072]{1,0:T(4,128)S(1)} %get-tuple-element.21.mod, bf16[3072,2048]{1,0:T(8,128)(2,1)S(1)} %bitcast.90, bf16[2048,3072]{1,0:T(8,128)(2,1)S(1)} %bitcast.93), custom_call_target="tpu_custom_call" | custom-call | flops 1811939328 | bytes 884736 | tf_op jit(solution)/shard_map/pallas_call | solution.py:141
  63.1 1.3 %collective-permute-start.11 = (bf16[72,1536]{1,0:T(8,128)(2,1)S(1)}, bf16[72,1536]{1,0:T(8,128)(2,1)S(1)}, u32[]{:S(2)}, u32[]{:S(2)}) collective-permute-start(bf16[72,1536]{1,0:T(8,128)(2,1)S(1)} %slice.155), channel_id=1, source_target_pairs={{0,2},{1,3},{2,0},{3,1},{4,6},{5,7},{6,4},{7,5},{8,10},{9,11},{10,... | collective-permute-start | bytes 663560 | tf_op jit(solution)/shard_map/ppermute | solution.py:20
  64.4 0.3 fusion.12
  64.7 0.0 collective-permute-done.8.second
  64.7 12.6 %collective-permute-done.7.first = bf16[72,1536]{1,0:T(8,128)(2,1)S(1)} collective-permute-done((bf16[72,1536]{1,0:T(8,128)(2,1)S(1)}, bf16[72,1536]{1,0:T(8,128)(2,1)S(1)}, u32[]{:S(2)}, u32[]{:S(2)}) %collective-permute-start.7) | collective-permute-done | bytes 221216 | tf_op jit(solution)/shard_map/ppermute | solution.py:20
  77.3 5.0 %shard_map.84 = bf16[72,3072]{1,0:T(8,128)(2,1)S(1)} custom-call(bf16[72,1536]{1,0:T(8,128)(2,1)S(1)} %collective-permute-done.7.first, bf16[72,1536]{1,0:T(8,128)(2,1)S(1)} %collective-permute-done.8.second, f32[3,3072]{1,0:T(4,128)S(1)} %get-tuple-element.21.mod, bf16[3072,2048]{1,0:T(8,128)(2,1)S(1)} %bitcast.91, bf16[2048,3072]{1,0:T(8,128)(2,1)S(1)} %bitcast.94), custom_call_target="tpu_custom_call" | custom-call | flops 1811939328 | bytes 884736 | tf_op jit(solution)/shard_map/pallas_call | solution.py:141
  82.3 0.1 collective-permute-start.9
  82.4 2.7 %collective-permute-start.12 = (bf16[72,1536]{1,0:T(8,128)(2,1)S(1)}, bf16[72,1536]{1,0:T(8,128)(2,1)S(1)}, u32[]{:S(2)}, u32[]{:S(2)}) collective-permute-start(bf16[72,1536]{1,0:T(8,128)(2,1)S(1)} %get-tuple-element.17), channel_id=1, source_target_pairs={{0,3},{1,2},{2,1},{3,0},{4,7},{5,6},{6,5},{7,4},{8,11},{9,10},{10,... | collective-permute-start | bytes 663560 | tf_op jit(solution)/shard_map/ppermute | solution.py:20
  85.1 0.0 collective-permute-done.11
  85.1 0.3 convolution_multiply_fusion.3
  85.4 0.0 collective-permute-done.3
  85.4 0.4 convolution_multiply_fusion
  85.8 3.8 %collective-permute-done.9 = bf16[72,1536]{1,0:T(8,128)(2,1)S(1)} collective-permute-done((bf16[72,1536]{1,0:T(8,128)(2,1)S(1)}, bf16[72,1536]{1,0:T(8,128)(2,1)S(1)}, u32[]{:S(2)}, u32[]{:S(2)}) %collective-permute-start.9) | collective-permute-done | bytes 221216 | tf_op jit(solution)/shard_map/ppermute | solution.py:20
  89.6 0.3 add_convert_fusion
  89.9 3.5 %collective-permute-start.10 = (bf16[96,1536]{1,0:T(8,128)(2,1)S(1)}, bf16[96,1536]{1,0:T(8,128)(2,1)S(1)}, u32[]{:S(2)}, u32[]{:S(2)}) collective-permute-start(bf16[96,1536]{1,0:T(8,128)(2,1)S(1)} %add_convert_fusion), channel_id=1, source_target_pairs={{0,2},{1,3},{2,0},{3,1},{4,6},{5,7},{6,4},{7,5},{8,10},{9,11},{10,... | collective-permute-start | bytes 884744 | tf_op jit(solution)/shard_map/ppermute | solution.py:20
  93.4 0.4 fusion
  93.7 2.4 %collective-permute-done.12 = bf16[72,1536]{1,0:T(8,128)(2,1)S(1)} collective-permute-done((bf16[72,1536]{1,0:T(8,128)(2,1)S(1)}, bf16[72,1536]{1,0:T(8,128)(2,1)S(1)}, u32[]{:S(2)}, u32[]{:S(2)}) %collective-permute-start.12) | collective-permute-done | bytes 221216 | tf_op jit(solution)/shard_map/ppermute | solution.py:20
  96.2 0.3 fusion.9
  96.5 10.9 %collective-permute-done.10 = bf16[96,1536]{1,0:T(8,128)(2,1)S(1)} collective-permute-done((bf16[96,1536]{1,0:T(8,128)(2,1)S(1)}, bf16[96,1536]{1,0:T(8,128)(2,1)S(1)}, u32[]{:S(2)}, u32[]{:S(2)}) %collective-permute-start.10) | collective-permute-done | bytes 294944 | tf_op jit(solution)/shard_map/ppermute | solution.py:20
  107.4 0.1 slice_add_fusion.1
  107.5 1.0 fusion.8
  (22 shorter events, 0.3 us)
Async XLA Ops:
  0.0 7.8 %copy-start = (bf16[50,3,3072]{2,0,1:T(8,128)(2,1)S(1)}, bf16[50,3,3072]{2,0,1:T(8,128)(2,1)}, u32[]{:S(2)}) copy-start(bf16[50,3,3072]{2,0,1:T(8,128)(2,1)} %param.15) | copy-start | bytes 2764804
  0.0 12.0 %copy-start.4 = (bf16[1,96,3072]{2,1,0:T(8,128)(2,1)S(1)}, bf16[1,96,3072]{2,1,0:T(8,128)(2,1)}, u32[]{:S(2)}) copy-start(bf16[1,96,3072]{2,1,0:T(8,128)(2,1)} %param.8) | copy-start | bytes 1769476
  0.0 15.1 %collective-permute-start = (bf16[96,3072]{1,0:T(8,128)(2,1)}, bf16[96,3072]{1,0:T(8,128)(2,1)S(1)}, u32[]{:S(2)}, u32[]{:S(2)}) collective-permute-start(bf16[96,3072]{1,0:T(8,128)(2,1)} %bitcast.95), channel_id=1, source_target_pairs={{12,0},{0,4},{4,8},{8,12},{13,1},{1,5},{5,9},{9,13},{14,2},{2,6},{... | collective-permute-start | bytes 1769480 | tf_op jit(solution)/shard_map/ppermute | solution.py:16
  1.5 54.3 %collective-permute-start.5 = (bf16[96,1536]{1,0:T(8,128)(2,1)S(1)}, bf16[96,1536]{1,0:T(8,128)(2,1)S(1)}, u32[]{:S(2)}, u32[]{:S(2)}) collective-permute-start(bf16[96,1536]{1,0:T(8,128)(2,1)S(1)} %slice.150), channel_id=1, source_target_pairs={{0,6},{1,7},{2,4},{3,5},{4,10},{5,11},{6,8},{7,9},{8,14},{9,15},{1... | collective-permute-start | bytes 884744 | tf_op jit(solution)/shard_map/ppermute | solution.py:30
  7.0 1.7 %collective-permute-start.1 = (s32[96,4]{0,1:T(4,128)S(1)}, s32[96,4]{0,1:T(4,128)S(1)}, u32[]{:S(2)}, u32[]{:S(2)}) collective-permute-start(s32[96,4]{0,1:T(4,128)S(1)} %get-tuple-element.32), channel_id=1, source_target_pairs={{4,0},{8,4},{12,8},{0,12},{5,1},{9,5},{13,9},{1,13},{6,2},{10,6},{... | collective-permute-start | bytes 4616 | tf_op jit(solution)/shard_map/ppermute | solution.py:16
  9.9 48.4 %collective-permute-start.6 = (bf16[72,1536]{1,0:T(8,128)(2,1)S(1)}, bf16[72,1536]{1,0:T(8,128)(2,1)S(1)}, u32[]{:S(2)}, u32[]{:S(2)}) collective-permute-start(bf16[72,1536]{1,0:T(8,128)(2,1)S(1)} %convolution_convert_fusion.3), channel_id=1, source_target_pairs={{0,6},{1,7},{2,4},{3,5},{4,10},{5,11},{6,8},{7,9},{8,14},{9,15},{1... | collective-permute-start | bytes 663560 | tf_op jit(solution)/shard_map/ppermute | solution.py:30
  12.2 52.5 %collective-permute-start.8 = (bf16[72,1536]{1,0:T(8,128)(2,1)S(1)}, bf16[72,1536]{1,0:T(8,128)(2,1)S(1)}, u32[]{:S(2)}, u32[]{:S(2)}) collective-permute-start(bf16[72,1536]{1,0:T(8,128)(2,1)S(1)} %convolution_convert_fusion.1), channel_id=1, source_target_pairs={{0,7},{1,6},{2,5},{3,4},{4,11},{5,10},{6,9},{7,8},{8,15},{9,14},{1... | collective-permute-start | bytes 663560 | tf_op jit(solution)/shard_map/ppermute | solution.py:30
  15.1 0.9 copy-start.5
  15.1 26.5 %collective-permute-start.2 = (bf16[72,3072]{1,0:T(8,128)(2,1)S(1)}, bf16[72,3072]{1,0:T(8,128)(2,1)S(1)}, u32[]{:S(2)}, u32[]{:S(2)}) collective-permute-start(bf16[72,3072]{1,0:T(8,128)(2,1)S(1)} %convolution_convert_fusion), channel_id=1, source_target_pairs={{0,5},{1,4},{2,7},{3,6},{4,9},{5,8},{6,11},{7,10},{8,13},{9,12},{1... | collective-permute-start | bytes 1327112 | tf_op jit(solution)/shard_map/ppermute | solution.py:30
  15.3 0.9 copy-start.6
  16.3 39.4 %collective-permute-start.4 = (f32[96,6]{0,1:T(8,128)S(1)}, f32[96,6]{0,1:T(8,128)S(1)}, u32[]{:S(2)}, u32[]{:S(2)}) collective-permute-start(f32[96,6]{0,1:T(8,128)S(1)} %pad_maximum_fusion), channel_id=1, source_target_pairs={{0,2},{1,3},{2,0},{3,1},{4,6},{5,7},{6,4},{7,5},{8,10},{9,11},{10,... | collective-permute-start | bytes 6920 | tf_op jit(solution)/shard_map/ppermute | solution.py:20
  41.6 4.6 %copy-start.1 = (bf16[1,3072,2048]{2,1,0:T(8,128)(2,1)S(1)}, bf16[1,3072,2048]{2,1,0:T(8,128)(2,1)}, u32[]{:S(2)}) copy-start(bf16[1,3072,2048]{2,1,0:T(8,128)(2,1)} %param.13) | copy-start | bytes 37748740
  46.2 4.6 %copy-start.3 = (bf16[1,2048,3072]{2,1,0:T(8,128)(2,1)S(1)}, bf16[1,2048,3072]{2,1,0:T(8,128)(2,1)}, u32[]{:S(2)}) copy-start(bf16[1,2048,3072]{2,1,0:T(8,128)(2,1)} %param.14) | copy-start | bytes 37748740
  50.7 7.5 %copy-start.2 = (bf16[1,3072,2048]{2,1,0:T(8,128)(2,1)S(1)}, bf16[1,3072,2048]{2,1,0:T(8,128)(2,1)}, u32[]{:S(2)}) copy-start(bf16[1,3072,2048]{2,1,0:T(8,128)(2,1)} %param.13) | copy-start | bytes 37748740
  55.6 29.7 %collective-permute-start.3 = (bf16[72,3072]{1,0:T(8,128)(2,1)S(1)}, bf16[72,3072]{1,0:T(8,128)(2,1)S(1)}, u32[]{:S(2)}, u32[]{:S(2)}) collective-permute-start(bf16[72,3072]{1,0:T(8,128)(2,1)S(1)} %get-tuple-element.8), channel_id=1, source_target_pairs={{0,1},{1,0},{2,3},{3,2},{4,5},{5,4},{6,7},{7,6},{8,9},{9,8},{10,11... | collective-permute-start | bytes 1327112 | tf_op jit(solution)/shard_map/ppermute | solution.py:20
  56.0 21.3 %collective-permute-start.7 = (bf16[72,1536]{1,0:T(8,128)(2,1)S(1)}, bf16[72,1536]{1,0:T(8,128)(2,1)S(1)}, u32[]{:S(2)}, u32[]{:S(2)}) collective-permute-start(bf16[72,1536]{1,0:T(8,128)(2,1)S(1)} %convolution_convert_fusion.2), channel_id=1, source_target_pairs={{0,1},{1,0},{2,3},{3,2},{4,5},{5,4},{6,7},{7,6},{8,9},{9,8},{10,11... | collective-permute-start | bytes 663560 | tf_op jit(solution)/shard_map/ppermute | solution.py:20
  63.1 22.0 %collective-permute-start.11 = (bf16[72,1536]{1,0:T(8,128)(2,1)S(1)}, bf16[72,1536]{1,0:T(8,128)(2,1)S(1)}, u32[]{:S(2)}, u32[]{:S(2)}) collective-permute-start(bf16[72,1536]{1,0:T(8,128)(2,1)S(1)} %slice.155), channel_id=1, source_target_pairs={{0,2},{1,3},{2,0},{3,1},{4,6},{5,7},{6,4},{7,5},{8,10},{9,11},{10,... | collective-permute-start | bytes 663560 | tf_op jit(solution)/shard_map/ppermute | solution.py:20
  82.3 7.3 %collective-permute-start.9 = (bf16[72,1536]{1,0:T(8,128)(2,1)S(1)}, bf16[72,1536]{1,0:T(8,128)(2,1)S(1)}, u32[]{:S(2)}, u32[]{:S(2)}) collective-permute-start(bf16[72,1536]{1,0:T(8,128)(2,1)S(1)} %get-tuple-element.16), channel_id=1, source_target_pairs={{0,1},{1,0},{2,3},{3,2},{4,5},{5,4},{6,7},{7,6},{8,9},{9,8},{10,11... | collective-permute-start | bytes 663560 | tf_op jit(solution)/shard_map/ppermute | solution.py:20
  82.4 13.8 %collective-permute-start.12 = (bf16[72,1536]{1,0:T(8,128)(2,1)S(1)}, bf16[72,1536]{1,0:T(8,128)(2,1)S(1)}, u32[]{:S(2)}, u32[]{:S(2)}) collective-permute-start(bf16[72,1536]{1,0:T(8,128)(2,1)S(1)} %get-tuple-element.17), channel_id=1, source_target_pairs={{0,3},{1,2},{2,1},{3,0},{4,7},{5,6},{6,5},{7,4},{8,11},{9,10},{10,... | collective-permute-start | bytes 663560 | tf_op jit(solution)/shard_map/ppermute | solution.py:20
  89.9 17.6 %collective-permute-start.10 = (bf16[96,1536]{1,0:T(8,128)(2,1)S(1)}, bf16[96,1536]{1,0:T(8,128)(2,1)S(1)}, u32[]{:S(2)}, u32[]{:S(2)}) collective-permute-start(bf16[96,1536]{1,0:T(8,128)(2,1)S(1)} %add_convert_fusion), channel_id=1, source_target_pairs={{0,2},{1,3},{2,0},{3,1},{4,6},{5,7},{6,4},{7,5},{8,10},{9,11},{10,... | collective-permute-start | bytes 884744 | tf_op jit(solution)/shard_map/ppermute | solution.py:20

commit v2 on v0

--- a/solution.py
+++ b/solution.py
@@ -1,7 +1,15 @@
 import jax
 import jax.numpy as jnp
 from jax import lax
+from jax.experimental import pallas as pl
+from jax.experimental.pallas import tpu as pltpu
 from jax.sharding import PartitionSpec as P
+
+MIB = 1024 * 1024
+VMEM = pl.BlockSpec(memory_space=pltpu.VMEM)
+ANY = pl.BlockSpec(memory_space=pl.ANY)
+HBM = pl.BlockSpec(memory_space=pltpu.HBM)
+PARAMS = pltpu.CompilerParams(vmem_limit_bytes=10 * MIB)
 
 
 def shifted(block, axis, distance):
@@ -10,12 +18,388 @@
     return lax.ppermute(block, axis, route)
 
 
-def modulate(incoming, mod):
+def swapped(block, mask):
+    return lax.ppermute(block, "expert", [(e, e ^ mask) for e in range(lax.axis_size("expert"))])
+
+
+def advanced(block, mask):
+    comps, experts = lax.axis_size("comp"), lax.axis_size("expert")
+    route = [
+        (c * experts + e, (c + 1) % comps * experts + (e ^ mask))
+        for c in range(comps)
+        for e in range(experts)
+    ]
+    return lax.ppermute(block, ("comp", "expert"), route)
+
+
+def modulate(incoming, scale, shift):
     values = incoming.astype(jnp.float32)
     centred = values - jnp.mean(values, axis=-1, keepdims=True)
     spread = jnp.mean(centred * centred, axis=-1, keepdims=True)
     normed = centred * lax.rsqrt(spread + 1e-06)
-    return (normed * (1.0 + mod[0]) + mod[1]).astype(jnp.bfloat16)
+    return (normed * (1.0 + scale) + shift).astype(jnp.bfloat16)
+
+
+def slot_rows(target, mask, most):
+    rows = lax.broadcasted_iota(jnp.int32, (most, target.shape[1]), 0) + mask * most
+    hit = (rows == target[0:1, :]) | (rows == target[1:2, :])
+    return jnp.where(hit, 1.0, 0.0).astype(jnp.bfloat16)
+
+
+def select(rows, block):
+    return jnp.dot(rows, block, preferred_element_type=jnp.float32).astype(jnp.bfloat16)
+
+
+def gate_column(target, gates, mask, most):
+    picked = (target >= mask * most) & (target < (mask + 1) * most)
+    row = jnp.sum(jnp.where(picked, gates, 0.0), axis=0, keepdims=True)
+    size = target.shape[1]
+    places = (size, size)
+    same = lax.broadcasted_iota(jnp.int32, places, 0) == lax.broadcasted_iota(jnp.int32, places, 1)
+    return jnp.sum(jnp.where(same, row, 0.0), axis=1, keepdims=True)
+
+
+def mixed(target, gates, mask, result):
+    rows = slot_rows(target, mask, result.shape[0])
+    spread = lax.dot_general(
+        rows, result, (((0,), (0,)), ((), ())), preferred_element_type=jnp.float32
+    )
+    return gate_column(target, gates, mask, result.shape[0]) * spread
+
+
+def tiles(size, step):
+    return [(i, min(step, size - i)) for i in range(0, size, step)]
+
+
+def first_layer(x, w1, hidden, ready=lambda index: None):
+    for index, (start, size) in enumerate(tiles(w1.shape[1], 512)):
+        ready(index)
+        value = jnp.dot(x[...], w1[:, start:start + size], preferred_element_type=jnp.float32)
+        hidden[:, start:start + size] = jax.nn.gelu(value, approximate=True).astype(jnp.bfloat16)
+
+
+def second_layer(hidden, w2, columns, outs, ready=lambda index: None):
+    pad = hidden.shape[0] // len(outs)
+    for index, (start, size) in enumerate(tiles(columns[1] - columns[0], 512)):
+        ready(index)
+        part = w2[:, columns[0] + start:columns[0] + start + size]
+        value = jnp.dot(hidden[...], part, preferred_element_type=jnp.float32)
+        for i, out in enumerate(outs):
+            rows = value[i * pad:i * pad + out.shape[0]]
+            out[:, start:start + size] = rows.astype(jnp.bfloat16)
+
+
+def source_kernel(source, ahead, out_x, out_z, out_s):
+    most = out_s.shape[0]
+    cut = source.shape[1] - out_x.shape[1]
+    out_x[...] = select(slot_rows(ahead[...], 2, most), source[:, cut:])
+    out_z[...] = select(slot_rows(ahead[...], 3, most), source[:, cut:])
+    out_s[...] = select(slot_rows(ahead[...], 1, most), source[...])
+
+
+def relay_kernel(crossed, target, after, out_here, out_there):
+    del after
+    most = out_here.shape[0]
+    out_here[...] = select(slot_rows(target[...], 2, most), crossed[...])
+    out_there[...] = select(slot_rows(target[...], 3, most), crossed[...])
+
+
+def own_kernel(
+    own, target, chosen, mod, router, w1, w2, after, out, gates, w1v, w2v, x, hidden, sems1, sems2
+):
+    del after
+
+    def copies(source, target, sems):
+        return [
+            pltpu.make_async_copy(
+                source.at[:, pl.ds(start, size)], target.at[:, pl.ds(start, size)], sems.at[index]
+            )
+            for index, (start, size) in enumerate(tiles(source.shape[1], 512))
+        ]
+
+    first, second = copies(w1, w1v, sems1), copies(w2, w2v, sems2)
+    for copy in first + second:
+        copy.start()
+    most = out.shape[0]
+    modulated = modulate(own[...], mod[0:1, :], mod[1:2, :])
+    logits = lax.dot_general(
+        router[...], modulated, (((1,), (1,)), ((), ())), preferred_element_type=jnp.float32
+    )
+    picked = jnp.zeros(chosen.shape, jnp.float32)
+    for expert in range(router.shape[0]):
+        picked += jnp.where(chosen[...] == expert, logits[expert:expert + 1, :], 0.0)
+    sig = jax.nn.sigmoid(picked)
+    gates[...] = sig / jnp.sum(sig, axis=0, keepdims=True)
+    x[...] = jnp.zeros_like(x)
+    x[0:most, :] = select(slot_rows(target[...], 0, most), modulated)
+    first_layer(x, w1v, hidden, lambda index: first[index].wait())
+    second_layer(hidden, w2v, (0, w2.shape[1]), (out,), lambda index: second[index].wait())
+
+
+def far_kernel(near_x, far_x, near_z, far_z, mod, w1, w2, after, out_x, out_z, hidden, raw, x):
+    del after
+    most, cut = near_x.shape
+    pad = x.shape[0] // 2
+    x[...] = jnp.zeros_like(x)
+    for i, (left, right) in enumerate(((near_x, far_x), (near_z, far_z))):
+        raw[:, 0:cut] = left[...].astype(jnp.float32)
+        raw[:, cut:] = right[...].astype(jnp.float32)
+        x[i * pad:i * pad + most, :] = modulate(raw[...], mod[0:1, :], mod[1:2, :])
+    first_layer(x, w1, hidden)
+    second_layer(hidden, w2, (cut, w2.shape[1]), (out_x, out_z))
+
+
+def rest_kernel(hidden, w2, after, out_x, out_z):
+    del after
+    second_layer(hidden, w2, (0, out_x.shape[1]), (out_x, out_z))
+
+
+def sibling_kernel(sib, mod, w1, w2, after, out, x, hidden):
+    del after
+    x[...] = jnp.zeros_like(x)
+    x[0:out.shape[0], :] = modulate(sib[...], mod[0:1, :], mod[1:2, :])
+    first_layer(x, w1, hidden)
+    second_layer(hidden, w2, (0, w2.shape[1]), (out,))
+
+
+def joint_kernel(target, gates, here, there, out):
+    value = mixed(target[...], gates[...], 2, here[...])
+    value += mixed(target[...], gates[...], 3, there[...])
+    out[...] = value.astype(jnp.bfloat16)
+
+
+def home_kernel(target, gates, y_own, y_x, y_z, out):
+    cut = y_own.shape[1] - y_x.shape[1]
+    place, weight = target[...], gates[...]
+    own = mixed(place, weight, 0, y_own[...])
+    far = mixed(place, weight, 2, y_x[...]) + mixed(place, weight, 3, y_z[...])
+    out[:, 0:cut] = own[:, 0:cut]
+    out[:, cut:] = own[:, cut:] + far
+
+
+def near_kernel(target, gates, mixture, y_sib, out):
+    out[...] = mixture[...] + mixed(target[...], gates[...], 1, y_sib[...])
+
+
+def last_kernel(incoming, mod, mixture, joint, out):
+    cut = joint.shape[1]
+    left = mixture[:, 0:cut] + joint[...].astype(jnp.float32)
+    left = incoming[:, 0:cut].astype(jnp.float32) + (1.0 + mod[2:3, 0:cut]) * left
+    right = incoming[:, cut:].astype(jnp.float32) + (1.0 + mod[2:3, cut:]) * mixture[:, cut:]
+    out[:, 0:cut] = left.astype(jnp.bfloat16)
+    out[:, cut:] = right.astype(jnp.bfloat16)
+
+
+def cost(flops):
+    return pl.CostEstimate(flops=flops, bytes_accessed=flops // 1024, transcendentals=0)
+
+
+SHORT, LONG = cost(1 << 20), cost(1 << 37)
+
+
+def padded(most):
+    return -(-most // 16) * 16
+
+
+def array(rows, columns, dtype=jnp.bfloat16):
+    return jax.ShapeDtypeStruct((rows, columns), dtype)
+
+
+def source_pass(source, ahead, most, cut):
+    width = source.shape[1]
+    return pl.pallas_call(
+        source_kernel,
+        out_shape=(array(most, width - cut), array(most, width - cut), array(most, width)),
+        in_specs=[VMEM] * 2,
+        out_specs=(VMEM,) * 3,
+        compiler_params=PARAMS,
+        cost_estimate=SHORT,
+    )(source, ahead)
+
+
+def relay_pass(crossed, target, after, most):
+    cut = crossed.shape[1]
+    return pl.pallas_call(
+        relay_kernel,
+        out_shape=(array(most, cut), array(most, cut)),
+        in_specs=[VMEM] * 2 + [ANY],
+        out_specs=(VMEM,) * 2,
+        compiler_params=PARAMS,
+        cost_estimate=SHORT,
+    )(crossed, target, after)
+
+
+def own_pass(own, target, chosen, mod, router, w1, w2, after, most):
+    width, hid = w1.shape
+    return pl.pallas_call(
+        own_kernel,
+        out_shape=(
+            array(most, width),
+            array(*chosen.shape, jnp.float32),
+            pltpu.VMEM(w1.shape, w1.dtype),
+            pltpu.VMEM(w2.shape, w2.dtype),
+        ),
+        in_specs=[VMEM] * 5 + [HBM] * 2 + [ANY],
+        out_specs=(VMEM,) * 4,
+        scratch_shapes=[
+            pltpu.VMEM((padded(most), width), jnp.bfloat16),
+            pltpu.VMEM((padded(most), hid), jnp.bfloat16),
+            pltpu.SemaphoreType.DMA((len(tiles(w1.shape[1], 512)),)),
+            pltpu.SemaphoreType.DMA((len(tiles(w2.shape[1], 512)),)),
+        ],
+        compiler_params=PARAMS,
+        cost_estimate=SHORT,
+    )(
+        own,
+        target,
+        chosen,
+        mod,
+        router,
+        pltpu.with_memory_space_constraint(w1, pltpu.HBM),
+        pltpu.with_memory_space_constraint(w2, pltpu.HBM),
+        after,
+    )
+
+
+def far_pass(near_x, far_x, near_z, far_z, mod, w1, w2, after):
+    most = near_x.shape[0]
+    width, hid = w1.shape
+    out = array(*far_x.shape)
+    return pl.pallas_call(
+        far_kernel,
+        out_shape=(out, out, array(2 * padded(most), hid)),
+        in_specs=[VMEM] * 7 + [ANY],
+        out_specs=(VMEM,) * 3,
+        scratch_shapes=[
+            pltpu.VMEM((most, width), jnp.float32),
+            pltpu.VMEM((2 * padded(most), width), jnp.bfloat16),
+        ],
+        compiler_params=PARAMS,
+        cost_estimate=SHORT,
+    )(near_x, far_x, near_z, far_z, mod, w1, w2, after)
+
+
+def rest_pass(hidden, w2, after, most, cut):
+    return pl.pallas_call(
+        rest_kernel,
+        out_shape=(array(most, cut), array(most, cut)),
+        in_specs=[VMEM] * 2 + [ANY],
+        out_specs=(VMEM,) * 2,
+        compiler_params=PARAMS,
+        cost_estimate=SHORT,
+    )(hidden, w2, after)
+
+
+def sibling_pass(sib, mod, w1, w2, after):
+    most, width = sib.shape
+    hid = w1.shape[1]
+    return pl.pallas_call(
+        sibling_kernel,
+        out_shape=array(most, width),
+        in_specs=[VMEM] * 4 + [ANY],
+        out_specs=VMEM,
+        scratch_shapes=[
+            pltpu.VMEM((padded(most), width), jnp.bfloat16),
+            pltpu.VMEM((padded(most), hid), jnp.bfloat16),
+        ],
+        compiler_params=PARAMS,
+        cost_estimate=SHORT,
+    )(sib, mod, w1, w2, after)
+
+
+def joint_pass(target, gates, here, there):
+    tokens, cut = target.shape[1], here.shape[1]
+    return pl.pallas_call(
+        joint_kernel,
+        out_shape=array(tokens, cut),
+        in_specs=[VMEM] * 4,
+        out_specs=VMEM,
+        compiler_params=PARAMS,
+        cost_estimate=SHORT,
+    )(target, gates, here, there)
+
+
+def home_pass(target, gates, y_own, y_x, y_z):
+    return pl.pallas_call(
+        home_kernel,
+        out_shape=array(target.shape[1], y_own.shape[1], jnp.float32),
+        in_specs=[VMEM] * 5,
+        out_specs=VMEM,
+        compiler_params=PARAMS,
+        cost_estimate=LONG,
+    )(target, gates, y_own, y_x, y_z)
+
+
+def near_pass(target, gates, mixture, y_sib):
+    return pl.pallas_call(
+        near_kernel,
+        out_shape=array(*mixture.shape, jnp.float32),
+        in_specs=[VMEM] * 4,
+        out_specs=VMEM,
+        compiler_params=PARAMS,
+        cost_estimate=SHORT,
+    )(target, gates, mixture, y_sib)
+
+
+def last_pass(incoming, mod, mixture, joint):
+    return pl.pallas_call(
+        last_kernel,
+        out_shape=array(*incoming.shape),
+        in_specs=[VMEM] * 4,
+        out_specs=VMEM,
+        compiler_params=PARAMS,
+        cost_estimate=SHORT,
+    )(incoming, mod, mixture, joint)
+
+
+def quad_body(states, routes, slots, timesteps, router_weight, expert_in, expert_out, modulation):
+    source = states[0]
+    width = source.shape[1]
+    most = 3 * source.shape[0] // 4
+    cut = width // 256 * 128
+    here = lax.axis_index("expert")
+    chosen = routes[0].T
+    target = (chosen ^ here) * most + slots[0].T
+    x_target = swapped(target, 2)
+    ahead = shifted(target, "comp", -1)
+    crossed = advanced(source[:, :cut], 2)
+    incoming = shifted(source, "comp", 1)
+    mod = modulation[timesteps[0]].astype(jnp.float32)
+
+    x_source, z_source, s_source = source_pass(source, ahead, most, cut)
+    sib = advanced(s_source, 1)
+    far_x = advanced(x_source, 2)
+    far_z = advanced(z_source, 3)
+
+    y_own, gates, w1, w2 = own_pass(
+        incoming,
+        target,
+        chosen,
+        mod,
+        router_weight[0].T,
+        expert_in[0],
+        expert_out[0],
+        z_source,
+        most,
+    )
+    x_gates = swapped(gates, 2)
+    w1 = pltpu.with_memory_space_constraint(w1, pltpu.VMEM)
+    w2 = pltpu.with_memory_space_constraint(w2, pltpu.VMEM)
+    near_x, passed = relay_pass(crossed, x_target, gates, most)
+    near_z = swapped(passed, 1)
+    y_sib = sibling_pass(sib, mod, w1, w2, passed)
+    back_s = swapped(y_sib, 1)
+    x_right, z_right, hidden = far_pass(
+        near_x, far_x, near_z, far_z, mod, w1, w2, y_sib
+    )
+    back_z = swapped(z_right, 3)
+    back_x = swapped(x_right, 2)
+    x_left, z_left = rest_pass(hidden, w2, x_gates, most, cut)
+    lent = swapped(z_left, 1)
+    joint = swapped(joint_pass(x_target, x_gates, x_left, lent), 2)
+    mixture = home_pass(target, gates, y_own, back_x, back_z)
+    mixture = near_pass(target, gates, mixture, back_s)
+    return last_pass(incoming, mod, mixture, joint)[None]
 
 
 def gating(modulated, weight, chosen):
@@ -26,7 +410,7 @@
     return sig / jnp.sum(sig, axis=1, keepdims=True)
 
 
-def body(states, routes, slots, timesteps, router_weight, expert_in, expert_out, modulation):
+def general_body(states, routes, slots, timesteps, router_weight, expert_in, expert_out, modulation):
     devices = lax.axis_size("expert")
     tokens_here = states.shape[1]
     width = states.shape[2]
@@ -35,7 +419,7 @@
     most = 3 * tokens_here // 4
     incoming = shifted(states[0], "comp", 1)
     mod = modulation[timesteps[0]].astype(jnp.float32)
-    modulated = modulate(incoming, mod)
+    modulated = modulate(incoming, mod[0], mod[1])
     chosen = routes[0]
     gates = gating(modulated, router_weight[0], chosen)
     target = chosen * most + slots[0]
@@ -74,6 +458,12 @@
     return updated.astype(jnp.bfloat16)[None]
 
 
+def body(states, routes, slots, timesteps, router_weight, *rest):
+    quad = lax.axis_size("expert") == router_weight.shape[2] == 4
+    chosen_body = quad_body if quad else general_body
+    return chosen_body(states, routes, slots, timesteps, router_weight, *rest)
+
+
 def solution(mesh):
     in_specs = (
         P("comp", ("groups", "expert"), None),

time: 122 us -> 85.9 us (0.70)
  blocking collectives: 46.1 us -> 0 us
  Pallas kernels: 0 us -> 24.6 us
  matrix products: 20.7 us -> 0 us
  starting transfers between devices: 4.16 us -> 21.5 us
  waiting for transfers between devices: 47 us -> 34.4 us
  local copies, waits for them, and re-layouts: 0.01 us -> 3.51 us
  other arithmetic: 2.47 us -> 0.8 us
    all_to_all x1 -> x0, blocking collectives: 46.1 us -> none  [body(): lax.all_to_all(outgoing, 'expert', split_axis=0, concat_axis=0, tiled=True)]
    all_to_all x1 -> x0, waiting for transfers between devices: 39.8 us -> none  [body(): lax.all_to_all(partial_value, 'expert', split_axis=0, concat_axis=0, tile...]
    ppermute x0 -> x12, waiting for transfers between devices: none -> 29.7 us  [the longest x8 29.7 us: swapped(): lax.ppermute(block, 'expert', [(e, e ^ mask) for e in range(lax.axis_size...]
    pallas_call x0 -> x10, Pallas kernels: none -> 24.6 us  [the longest x1 11.6 us: own_pass(): pl.pallas_call(own_kernel, out_shape=(array(most, width), array(*chosen.s...]
    dot_general x4 -> x0, matrix products: 20.7 us -> none  [the longest x1 17.3 us: body(): jnp.dot(hidden.astype(jnp.bfloat16), w_second, preferred_element_type=jnp...]
    ppermute x0 -> x12, starting transfers between devices: none -> 19.1 us  [the longest x8 13.5 us: swapped(): lax.ppermute(block, 'expert', [(e, e ^ mask) for e in range(lax.axis_size...]
    all_to_all x1 -> x0, starting transfers between devices: 3.71 us -> none  [body(): lax.all_to_all(partial_value, 'expert', split_axis=0, concat_axis=0, tile...]
    ppermute x1 -> x2, waiting for transfers between devices: 7.25 us -> 4.64 us  [shifted(): return lax.ppermute(block, axis, route)]
  transfers between devices with their start and end apart: 2 -> 14, of which waited for: 2 -> 6; matrix products, arithmetic and copies ran while one was open for 2% -> 1% of each run, Pallas kernels for 0% -> 26%
where the time goes in v2:
time: 85.9 us; the launch traced here: 85.6 us
  waiting for transfers between devices  34.4 us (40%)
  Pallas kernels  24.6 us (29%)
  starting transfers between devices  21.5 us (25%)
  local copies, waits for them, and re-layouts  3.51 us (4%)
    ppermute x8, waiting for transfers between devices, swapped(): lax.ppermute(block, 'expert', [(e, e ^ mask) for e in range(lax.axis_size...  29.7 us
    ppermute x8, starting transfers between devices, swapped(): lax.ppermute(block, 'expert', [(e, e ^ mask) for e in range(lax.axis_size...  13.5 us
    pallas_call x1, Pallas kernels, own_pass(): pl.pallas_call(own_kernel, out_shape=(array(most, width), array(*chosen.s...  11.6 us
    ppermute x4, starting transfers between devices, advanced(): return lax.ppermute(block, ('comp', 'expert'), route)  5.59 us
    pallas_call x1, Pallas kernels, sibling_pass(): pl.pallas_call(sibling_kernel, out_shape=array(most, width), in_specs=[VM...  4.78 us
    ppermute x2, waiting for transfers between devices, shifted(): return lax.ppermute(block, axis, route)  4.64 us
    pallas_call x1, Pallas kernels, far_pass(): pl.pallas_call(far_kernel, out_shape=(out, out, array(2 * padded(most), h...  3.92 us
    unnamed x8, local copies, waits for them, and re-layouts  2.48 us
  transfers between devices with their start and end apart: 14, of which 6 were waited for; matrix products, arithmetic and copies ran while one was open for 1% of the time, Pallas kernels for 26%

profile of v2, /device:TPU:0, one launch (start us, length us, event | category | flops | bytes accessed | tf_op | source)
XLA Modules:
  0.0 85.6 jit_solution(3208955129378225993)
XLA Ops:
  0.0 0.0 copy-start
  0.0 0.8 bitcast_add_fusion.target
  0.8 2.4 %collective-permute-start.1 = (s32[2,96]{1,0:T(2,128)S(1)}, s32[2,96]{1,0:T(2,128)S(1)}, u32[]{:S(2)}, u32[]{:S(2)}) collective-permute-start(s32[2,96]{1,0:T(2,128)S(1)} %bitcast_add_fusion.target), channel_id=1, source_target_pairs={{4,0},{8,4},{12,8},{0,12},{5,1},{9,5},{13,9},{1,13},{6,2},{10,6},{... | collective-permute-start | bytes 2312 | tf_op jit(solution)/shard_map/ppermute | solution.py:18
  3.2 2.6 %collective-permute-start.3 = (s32[2,96]{1,0:T(2,128)S(1)}, s32[2,96]{1,0:T(2,128)S(1)}, u32[]{:S(2)}, u32[]{:S(2)}) collective-permute-start(s32[2,96]{1,0:T(2,128)S(1)} %bitcast_add_fusion.target), channel_id=1, source_target_pairs={{0,2},{1,3},{2,0},{3,1},{4,6},{5,7},{6,4},{7,5},{8,10},{9,11},{10,... | collective-permute-start | bytes 2312 | tf_op jit(solution)/shard_map/ppermute | solution.py:22
  5.8 0.0 collective-permute-start
  5.8 1.0 %slice.4 = bf16[96,1536]{1,0:T(8,128)(2,1)S(1)} slice(bf16[96,3072]{1,0:T(8,128)(2,1)} %bitcast.25), slice={[0:96], [0:1536]} | slice | bytes 589824 | tf_op jit(solution)/shard_map/slice | solution.py:365
  6.7 0.7 collective-permute-start.2
  8.1 0.0 copy-done
  8.2 0.0 collective-permute-done.1.ahead
  8.2 0.0 copy-start.1
  8.2 1.1 %copy-done.1 = bf16[1,96,3072]{2,1,0:T(8,128)(2,1)S(1)} copy-done((bf16[1,96,3072]{2,1,0:T(8,128)(2,1)S(1)}, bf16[1,96,3072]{2,1,0:T(8,128)(2,1)}, u32[]{:S(2)}) %copy-start.1) | copy-done | bytes 589848
  9.2 0.4 shard_map.82
  9.7 1.3 %collective-permute-start.7 = (bf16[72,3072]{1,0:T(8,128)(2,1)S(1)}, bf16[72,3072]{1,0:T(8,128)(2,1)S(1)}, u32[]{:S(2)}, u32[]{:S(2)}) collective-permute-start(bf16[72,3072]{1,0:T(8,128)(2,1)S(1)} %get-tuple-element.27), channel_id=1, source_target_pairs={{0,5},{1,4},{2,7},{3,6},{4,9},{5,8},{6,11},{7,10},{8,13},{9,12},{1... | collective-permute-start | bytes 1327112 | tf_op jit(solution)/shard_map/ppermute | solution.py:32
  11.0 3.6 %collective-permute-start.4 = (bf16[72,1536]{1,0:T(8,128)(2,1)S(1)}, bf16[72,1536]{1,0:T(8,128)(2,1)S(1)}, u32[]{:S(2)}, u32[]{:S(2)}) collective-permute-start(bf16[72,1536]{1,0:T(8,128)(2,1)S(1)} %get-tuple-element.23), channel_id=1, source_target_pairs={{0,6},{1,7},{2,4},{3,5},{4,10},{5,11},{6,8},{7,9},{8,14},{9,15},{1... | collective-permute-start | bytes 663560 | tf_op jit(solution)/shard_map/ppermute | solution.py:32
  14.6 4.6 %collective-permute-done.own.incoming = bf16[96,3072]{1,0:T(8,128)(2,1)S(1)} collective-permute-done((bf16[96,3072]{1,0:T(8,128)(2,1)}, bf16[96,3072]{1,0:T(8,128)(2,1)S(1)}, u32[]{:S(2)}, u32[]{:S(2)}) %collective-permute-start) | collective-permute-done | bytes 589856 | tf_op jit(solution)/shard_map/ppermute | solution.py:18
  19.2 0.0 collective-permute-start.6
  19.2 0.0 copy-start.2
  19.2 0.7 copy-done.2
  19.9 0.0 copy-start.3
  19.9 0.7 copy-done.3
  20.6 11.6 %shard_map.83 = (bf16[72,3072]{1,0:T(8,128)(2,1)S(1)}, f32[2,96]{1,0:T(2,128)S(1)}, bf16[3072,2048]{1,0:T(8,128)(2,1)S(1)}, bf16[2048,3072]{1,0:T(8,128)(2,1)S(1)}) custom-call(bf16[96,3072]{1,0:T(8,128)(2,1)S(1)} %collective-permute-done.own.incoming, s32[2,96]{1,0:T(2,128)S(1)} %bitcast_add_fusion.target, s32[2,96]{1,0:T(2,128)S(1)} %bitcast.28, ...), custom_call_target="tpu_custom_call" | custom-call | flops 1048576 | bytes 1024 | tf_op jit(solution)/shard_map/pallas_call | solution.py:234
  32.3 0.0 collective-permute-done.3.target
  32.3 0.0 collective-permute-done.2.crossed
  32.3 0.3 shard_map.84
  32.6 3.8 %collective-permute-start.5 = (bf16[72,1536]{1,0:T(8,128)(2,1)S(1)}, bf16[72,1536]{1,0:T(8,128)(2,1)S(1)}, u32[]{:S(2)}, u32[]{:S(2)}) collective-permute-start(bf16[72,1536]{1,0:T(8,128)(2,1)S(1)} %get-tuple-element.24.after), channel_id=1, source_target_pairs={{0,1},{1,0},{2,3},{3,2},{4,5},{5,4},{6,7},{7,6},{8,9},{9,8},{10,11... | collective-permute-start | bytes 663560 | tf_op jit(solution)/shard_map/ppermute | solution.py:22
  36.4 0.0 collective-permute-start.11
  36.4 0.0 collective-permute-done.7.sib
  36.4 4.8 %shard_map.85.after = bf16[72,3072]{1,0:T(8,128)(2,1)S(1)} custom-call(bf16[72,3072]{1,0:T(8,128)(2,1)S(1)} %collective-permute-done.7.sib, f32[3,3072]{1,0:T(4,128)S(1)} %fusion.mod, bf16[3072,2048]{1,0:T(8,128)(2,1)S(1)} %get-tuple-element.25.w1, bf16[2048,3072]{1,0:T(8,128)(2,1)S(1)} %get-tuple-element.26.w2, bf16[72,1536]{1,0:T(8,128)(2,1)S(1)} %get-tuple-element.24.after), custom_call_target="tpu_custom_call" | custom-call | flops 1048576 | bytes 1024 | tf_op jit(solution)/shard_map/pallas_call | solution.py:296
  41.2 0.0 collective-permute-done.4.far_x
  41.2 0.0 collective-permute-done.6.far_z
  41.2 1.5 %collective-permute-done.5.near_z = bf16[72,1536]{1,0:T(8,128)(2,1)S(1)} collective-permute-done((bf16[72,1536]{1,0:T(8,128)(2,1)S(1)}, bf16[72,1536]{1,0:T(8,128)(2,1)S(1)}, u32[]{:S(2)}, u32[]{:S(2)}) %collective-permute-start.5) | collective-permute-done | bytes 221216 | tf_op jit(solution)/shard_map/ppermute | solution.py:22
  42.7 3.9 %shard_map.86 = (bf16[72,1536]{1,0:T(8,128)(2,1)S(1)}, bf16[72,1536]{1,0:T(8,128)(2,1)S(1)}, bf16[160,2048]{1,0:T(8,128)(2,1)S(1)}) custom-call(bf16[72,1536]{1,0:T(8,128)(2,1)S(1)} %get-tuple-element.22.near_x, bf16[72,1536]{1,0:T(8,128)(2,1)S(1)} %collective-permute-done.4.far_x, bf16[72,1536]{1,0:T(8,128)(2,1)S(1)} %collective-permute-done.5.near_z, ...), custom_call_target="tpu_custom_call" | custom-call | flops 1048576 | bytes 1024 | tf_op jit(solution)/shard_map/pallas_call | solution.py:268
  46.6 0.0 collective-permute-done.11.after.gates
  46.6 1.4 %shard_map.89 = (bf16[72,1536]{1,0:T(8,128)(2,1)S(1)}, bf16[72,1536]{1,0:T(8,128)(2,1)S(1)}) custom-call(bf16[160,2048]{1,0:T(8,128)(2,1)S(1)} %get-tuple-element.30.hidden, bf16[2048,3072]{1,0:T(8,128)(2,1)S(1)} %get-tuple-element.26.w2, f32[2,96]{1,0:T(2,128)S(1)} %collective-permute-done.11.after.gates), custom_call_target="tpu_custom_call" | custom-call | flops 1048576 | bytes 1024 | tf_op jit(solution)/shard_map/pallas_call | solution.py:283
  48.0 0.4 collective-permute-start.12
  48.3 4.8 %collective-permute-start.8 = (bf16[72,1536]{1,0:T(8,128)(2,1)S(1)}, bf16[72,1536]{1,0:T(8,128)(2,1)S(1)}, u32[]{:S(2)}, u32[]{:S(2)}) collective-permute-start(bf16[72,1536]{1,0:T(8,128)(2,1)S(1)} %get-tuple-element.28), channel_id=1, source_target_pairs={{0,2},{1,3},{2,0},{3,1},{4,6},{5,7},{6,4},{7,5},{8,10},{9,11},{10,... | collective-permute-start | bytes 663560 | tf_op jit(solution)/shard_map/ppermute | solution.py:22
  53.1 0.0 collective-permute-start.9
  53.1 0.6 collective-permute-start.10
  53.7 6.4 %collective-permute-done.12.there = bf16[72,1536]{1,0:T(8,128)(2,1)S(1)} collective-permute-done((bf16[72,1536]{1,0:T(8,128)(2,1)S(1)}, bf16[72,1536]{1,0:T(8,128)(2,1)S(1)}, u32[]{:S(2)}, u32[]{:S(2)}) %collective-permute-start.12) | collective-permute-done | bytes 221216 | tf_op jit(solution)/shard_map/ppermute | solution.py:22
  60.1 0.3 shard_map.90
  60.5 1.4 %collective-permute-start.13 = (bf16[96,1536]{1,0:T(8,128)(2,1)S(1)}, bf16[96,1536]{1,0:T(8,128)(2,1)S(1)}, u32[]{:S(2)}, u32[]{:S(2)}) collective-permute-start(bf16[96,1536]{1,0:T(8,128)(2,1)S(1)} %shard_map.90), channel_id=1, source_target_pairs={{0,2},{1,3},{2,0},{3,1},{4,6},{5,7},{6,4},{7,5},{8,10},{9,11},{10,... | collective-permute-start | bytes 884744 | tf_op jit(solution)/shard_map/ppermute | solution.py:22
  61.8 7.2 %collective-permute-done.8.y_x = bf16[72,1536]{1,0:T(8,128)(2,1)S(1)} collective-permute-done((bf16[72,1536]{1,0:T(8,128)(2,1)S(1)}, bf16[72,1536]{1,0:T(8,128)(2,1)S(1)}, u32[]{:S(2)}, u32[]{:S(2)}) %collective-permute-start.8) | collective-permute-done | bytes 221216 | tf_op jit(solution)/shard_map/ppermute | solution.py:22
  69.0 0.0 collective-permute-done.9.y_z
  69.0 0.5 shard_map.87.mixture
  69.6 9.4 %collective-permute-done.10.y_sib = bf16[72,3072]{1,0:T(8,128)(2,1)S(1)} collective-permute-done((bf16[72,3072]{1,0:T(8,128)(2,1)S(1)}, bf16[72,3072]{1,0:T(8,128)(2,1)S(1)}, u32[]{:S(2)}, u32[]{:S(2)}) %collective-permute-start.10) | collective-permute-done | bytes 442400 | tf_op jit(solution)/shard_map/ppermute | solution.py:22
  78.9 0.3 shard_map.88.mixture
  79.3 5.3 %collective-permute-done.13.joint = bf16[96,1536]{1,0:T(8,128)(2,1)S(1)} collective-permute-done((bf16[96,1536]{1,0:T(8,128)(2,1)S(1)}, bf16[96,1536]{1,0:T(8,128)(2,1)S(1)}, u32[]{:S(2)}, u32[]{:S(2)}) %collective-permute-start.13) | collective-permute-done | bytes 294944 | tf_op jit(solution)/shard_map/ppermute | solution.py:22
  84.6 1.0 %shard_map.91 = bf16[96,3072]{1,0:T(8,128)(2,1)} custom-call(bf16[96,3072]{1,0:T(8,128)(2,1)S(1)} %collective-permute-done.own.incoming, f32[3,3072]{1,0:T(4,128)S(1)} %fusion.mod, f32[96,3072]{1,0:T(8,128)S(1)} %shard_map.88.mixture, bf16[96,1536]{1,0:T(8,128)(2,1)S(1)} %collective-permute-done.13.joint), custom_call_target="tpu_custom_call" | custom-call | flops 1048576 | bytes 1024 | tf_op jit(solution)/shard_map/pallas_call | solution.py:345
  (2 shorter events, 0.1 us)
Async XLA Ops:
  0.0 8.1 %copy-start = (bf16[50,3,3072]{2,0,1:T(8,128)(2,1)S(1)}, bf16[50,3,3072]{2,0,1:T(8,128)(2,1)}, u32[]{:S(2)}) copy-start(bf16[50,3,3072]{2,0,1:T(8,128)(2,1)} %param.15) | copy-start | bytes 2764804
  0.8 7.4 %collective-permute-start.1 = (s32[2,96]{1,0:T(2,128)S(1)}, s32[2,96]{1,0:T(2,128)S(1)}, u32[]{:S(2)}, u32[]{:S(2)}) collective-permute-start(s32[2,96]{1,0:T(2,128)S(1)} %bitcast_add_fusion.target), channel_id=1, source_target_pairs={{4,0},{8,4},{12,8},{0,12},{5,1},{9,5},{13,9},{1,13},{6,2},{10,6},{... | collective-permute-start | bytes 2312 | tf_op jit(solution)/shard_map/ppermute | solution.py:18
  3.2 29.1 %collective-permute-start.3 = (s32[2,96]{1,0:T(2,128)S(1)}, s32[2,96]{1,0:T(2,128)S(1)}, u32[]{:S(2)}, u32[]{:S(2)}) collective-permute-start(s32[2,96]{1,0:T(2,128)S(1)} %bitcast_add_fusion.target), channel_id=1, source_target_pairs={{0,2},{1,3},{2,0},{3,1},{4,6},{5,7},{6,4},{7,5},{8,10},{9,11},{10,... | collective-permute-start | bytes 2312 | tf_op jit(solution)/shard_map/ppermute | solution.py:22
  5.8 13.4 %collective-permute-start = (bf16[96,3072]{1,0:T(8,128)(2,1)}, bf16[96,3072]{1,0:T(8,128)(2,1)S(1)}, u32[]{:S(2)}, u32[]{:S(2)}) collective-permute-start(bf16[96,3072]{1,0:T(8,128)(2,1)} %bitcast.24), channel_id=1, source_target_pairs={{12,0},{0,4},{4,8},{8,12},{13,1},{1,5},{5,9},{9,13},{14,2},{2,6},{... | collective-permute-start | bytes 1769480 | tf_op jit(solution)/shard_map/ppermute | solution.py:18
  6.7 25.5 %collective-permute-start.2 = (bf16[96,1536]{1,0:T(8,128)(2,1)S(1)}, bf16[96,1536]{1,0:T(8,128)(2,1)S(1)}, u32[]{:S(2)}, u32[]{:S(2)}) collective-permute-start(bf16[96,1536]{1,0:T(8,128)(2,1)S(1)} %slice.4), channel_id=1, source_target_pairs={{0,6},{1,7},{2,4},{3,5},{4,10},{5,11},{6,8},{7,9},{8,14},{9,15},{1... | collective-permute-start | bytes 884744 | tf_op jit(solution)/shard_map/ppermute | solution.py:32
  8.2 1.1 %copy-start.1 = (bf16[1,96,3072]{2,1,0:T(8,128)(2,1)S(1)}, bf16[1,96,3072]{2,1,0:T(8,128)(2,1)}, u32[]{:S(2)}) copy-start(bf16[1,96,3072]{2,1,0:T(8,128)(2,1)} %param.8) | copy-start | bytes 1769476
  9.7 26.7 %collective-permute-start.7 = (bf16[72,3072]{1,0:T(8,128)(2,1)S(1)}, bf16[72,3072]{1,0:T(8,128)(2,1)S(1)}, u32[]{:S(2)}, u32[]{:S(2)}) collective-permute-start(bf16[72,3072]{1,0:T(8,128)(2,1)S(1)} %get-tuple-element.27), channel_id=1, source_target_pairs={{0,5},{1,4},{2,7},{3,6},{4,9},{5,8},{6,11},{7,10},{8,13},{9,12},{1... | collective-permute-start | bytes 1327112 | tf_op jit(solution)/shard_map/ppermute | solution.py:32
  11.0 30.2 %collective-permute-start.4 = (bf16[72,1536]{1,0:T(8,128)(2,1)S(1)}, bf16[72,1536]{1,0:T(8,128)(2,1)S(1)}, u32[]{:S(2)}, u32[]{:S(2)}) collective-permute-start(bf16[72,1536]{1,0:T(8,128)(2,1)S(1)} %get-tuple-element.23), channel_id=1, source_target_pairs={{0,6},{1,7},{2,4},{3,5},{4,10},{5,11},{6,8},{7,9},{8,14},{9,15},{1... | collective-permute-start | bytes 663560 | tf_op jit(solution)/shard_map/ppermute | solution.py:32
  19.2 22.0 %collective-permute-start.6 = (bf16[72,1536]{1,0:T(8,128)(2,1)S(1)}, bf16[72,1536]{1,0:T(8,128)(2,1)S(1)}, u32[]{:S(2)}, u32[]{:S(2)}) collective-permute-start(bf16[72,1536]{1,0:T(8,128)(2,1)S(1)} %get-tuple-element.19.after), channel_id=1, source_target_pairs={{0,7},{1,6},{2,5},{3,4},{4,11},{5,10},{6,9},{7,8},{8,15},{9,14},{1... | collective-permute-start | bytes 663560 | tf_op jit(solution)/shard_map/ppermute | solution.py:32
  19.2 0.7 copy-start.2
  19.9 0.7 copy-start.3
  32.6 10.1 %collective-permute-start.5 = (bf16[72,1536]{1,0:T(8,128)(2,1)S(1)}, bf16[72,1536]{1,0:T(8,128)(2,1)S(1)}, u32[]{:S(2)}, u32[]{:S(2)}) collective-permute-start(bf16[72,1536]{1,0:T(8,128)(2,1)S(1)} %get-tuple-element.24.after), channel_id=1, source_target_pairs={{0,1},{1,0},{2,3},{3,2},{4,5},{5,4},{6,7},{7,6},{8,9},{9,8},{10,11... | collective-permute-start | bytes 663560 | tf_op jit(solution)/shard_map/ppermute | solution.py:22
  36.4 10.2 %collective-permute-start.11 = (f32[2,96]{1,0:T(2,128)S(1)}, f32[2,96]{1,0:T(2,128)S(1)}, u32[]{:S(2)}, u32[]{:S(2)}) collective-permute-start(f32[2,96]{1,0:T(2,128)S(1)} %get-tuple-element.20.after.gates), channel_id=1, source_target_pairs={{0,2},{1,3},{2,0},{3,1},{4,6},{5,7},{6,4},{7,5},{8,10},{9,11},{10,... | collective-permute-start | bytes 2312 | tf_op jit(solution)/shard_map/ppermute | solution.py:22
  48.0 12.2 %collective-permute-start.12 = (bf16[72,1536]{1,0:T(8,128)(2,1)S(1)}, bf16[72,1536]{1,0:T(8,128)(2,1)S(1)}, u32[]{:S(2)}, u32[]{:S(2)}) collective-permute-start(bf16[72,1536]{1,0:T(8,128)(2,1)S(1)} %get-tuple-element.32), channel_id=1, source_target_pairs={{0,1},{1,0},{2,3},{3,2},{4,5},{5,4},{6,7},{7,6},{8,9},{9,8},{10,11... | collective-permute-start | bytes 663560 | tf_op jit(solution)/shard_map/ppermute | solution.py:22
  48.3 20.7 %collective-permute-start.8 = (bf16[72,1536]{1,0:T(8,128)(2,1)S(1)}, bf16[72,1536]{1,0:T(8,128)(2,1)S(1)}, u32[]{:S(2)}, u32[]{:S(2)}) collective-permute-start(bf16[72,1536]{1,0:T(8,128)(2,1)S(1)} %get-tuple-element.28), channel_id=1, source_target_pairs={{0,2},{1,3},{2,0},{3,1},{4,6},{5,7},{6,4},{7,5},{8,10},{9,11},{10,... | collective-permute-start | bytes 663560 | tf_op jit(solution)/shard_map/ppermute | solution.py:22
  53.1 15.9 %collective-permute-start.9 = (bf16[72,1536]{1,0:T(8,128)(2,1)S(1)}, bf16[72,1536]{1,0:T(8,128)(2,1)S(1)}, u32[]{:S(2)}, u32[]{:S(2)}) collective-permute-start(bf16[72,1536]{1,0:T(8,128)(2,1)S(1)} %get-tuple-element.29), channel_id=1, source_target_pairs={{0,3},{1,2},{2,1},{3,0},{4,7},{5,6},{6,5},{7,4},{8,11},{9,10},{10,... | collective-permute-start | bytes 663560 | tf_op jit(solution)/shard_map/ppermute | solution.py:22
  53.1 25.8 %collective-permute-start.10 = (bf16[72,3072]{1,0:T(8,128)(2,1)S(1)}, bf16[72,3072]{1,0:T(8,128)(2,1)S(1)}, u32[]{:S(2)}, u32[]{:S(2)}) collective-permute-start(bf16[72,3072]{1,0:T(8,128)(2,1)S(1)} %shard_map.85.after), channel_id=1, source_target_pairs={{0,1},{1,0},{2,3},{3,2},{4,5},{5,4},{6,7},{7,6},{8,9},{9,8},{10,11... | collective-permute-start | bytes 1327112 | tf_op jit(solution)/shard_map/ppermute | solution.py:22
  60.5 24.1 %collective-permute-start.13 = (bf16[96,1536]{1,0:T(8,128)(2,1)S(1)}, bf16[96,1536]{1,0:T(8,128)(2,1)S(1)}, u32[]{:S(2)}, u32[]{:S(2)}) collective-permute-start(bf16[96,1536]{1,0:T(8,128)(2,1)S(1)} %shard_map.90), channel_id=1, source_target_pairs={{0,2},{1,3},{2,0},{3,1},{4,6},{5,7},{6,4},{7,5},{8,10},{9,11},{10,... | collective-permute-start | bytes 884744 | tf_op jit(solution)/shard_map/ppermute | solution.py:22

commit v3 on v2

--- a/solution.py
+++ b/solution.py
@@ -1,3 +1,5 @@
+import functools
+
 import jax
 import jax.numpy as jnp
 from jax import lax
@@ -89,12 +91,29 @@
             out[:, start:start + size] = rows.astype(jnp.bfloat16)
 
 
-def source_kernel(source, ahead, out_x, out_z, out_s):
-    most = out_s.shape[0]
-    cut = source.shape[1] - out_x.shape[1]
-    out_x[...] = select(slot_rows(ahead[...], 2, most), source[:, cut:])
-    out_z[...] = select(slot_rows(ahead[...], 3, most), source[:, cut:])
-    out_s[...] = select(slot_rows(ahead[...], 1, most), source[...])
+def sibling_kernel(source, ahead, out, out_source):
+    out[...] = select(slot_rows(ahead[...], 1, out.shape[0]), source[...])
+    out_source[...] = source[...]
+
+
+def source_kernel(mask, source, ahead, after, out):
+    del after
+    first = source.shape[1] - out.shape[1]
+    out[...] = select(slot_rows(ahead[...], mask, out.shape[0]), source[:, first:])
+
+
+def load_kernel(weight, after, out, sems):
+    del after
+    copies = [
+        pltpu.make_async_copy(
+            weight.at[:, pl.ds(start, size)], out.at[:, pl.ds(start, size)], sems.at[index]
+        )
+        for index, (start, size) in enumerate(tiles(weight.shape[1], 512))
+    ]
+    for copy in copies:
+        copy.start()
+    for copy in copies:
+        copy.wait()
 
 
 def relay_kernel(crossed, target, after, out_here, out_there):
@@ -104,23 +123,7 @@
     out_there[...] = select(slot_rows(target[...], 3, most), crossed[...])
 
 
-def own_kernel(
-    own, target, chosen, mod, router, w1, w2, after, out, gates, w1v, w2v, x, hidden, sems1, sems2
-):
-    del after
-
-    def copies(source, target, sems):
-        return [
-            pltpu.make_async_copy(
-                source.at[:, pl.ds(start, size)], target.at[:, pl.ds(start, size)], sems.at[index]
-            )
-            for index, (start, size) in enumerate(tiles(source.shape[1], 512))
-        ]
-
-    first, second = copies(w1, w1v, sems1), copies(w2, w2v, sems2)
-    for copy in first + second:
-        copy.start()
-    most = out.shape[0]
+def gate_kernel(own, target, chosen, mod, router, out, gates):
     modulated = modulate(own[...], mod[0:1, :], mod[1:2, :])
     logits = lax.dot_general(
         router[...], modulated, (((1,), (1,)), ((), ())), preferred_element_type=jnp.float32
@@ -130,55 +133,91 @@
         picked += jnp.where(chosen[...] == expert, logits[expert:expert + 1, :], 0.0)
     sig = jax.nn.sigmoid(picked)
     gates[...] = sig / jnp.sum(sig, axis=0, keepdims=True)
+    out[...] = select(slot_rows(target[...], 0, out.shape[0]), modulated)
+
+
+def pack_gates(gates, rows):
+    row = lax.broadcasted_iota(jnp.int32, (rows, gates.shape[1]), 0)
+    packed = jnp.zeros(row.shape, jnp.float32)
+    for index in range(3):
+        piece = gates.astype(jnp.bfloat16).astype(jnp.float32)
+        gates = gates - piece
+        for k in range(2):
+            packed = jnp.where(row == 2 * index + k, piece[k:k + 1, :], packed)
+    return packed.astype(jnp.bfloat16)
+
+
+def unpack_gates(packed):
+    pieces = packed[0:16, :].astype(jnp.float32)
+    return (pieces[0:2, :] + pieces[2:4, :]) + pieces[4:6, :]
+
+
+def far_hidden(left, right, mod, w1, hidden, raw, x):
+    most, cut = left.shape
+    raw[:, 0:cut] = left[...].astype(jnp.float32)
+    raw[:, cut:] = right[...].astype(jnp.float32)
+    for start, size in tiles(most, 16):
+        x[start:start + size, :] = modulate(raw[start:start + size, :], mod[0:1, :], mod[1:2, :])
+    first_layer(x, w1, hidden)
+
+
+def cross_kernel(left, right, mod, gates, w1, w2, out, hidden, raw, x):
+    width = w2.shape[1]
+    part = out.shape[1] - gates.shape[1]
+    out[:, part:] = pack_gates(gates[...], out.shape[0])
+    far_hidden(left, right, mod, w1, hidden, raw, x)
+    second_layer(hidden, w2, (width - part, width), (out.at[:, 0:part],))
+
+
+def far_kernel(left, right, mod, w1, w2, after, out_left, out_right, hidden, raw, x):
+    del after
+    cut = out_left.shape[1]
+    far_hidden(left, right, mod, w1, hidden, raw, x)
+    second_layer(hidden, w2, (0, cut), (out_left,))
+    second_layer(hidden, w2, (cut, w2.shape[1]), (out_right,))
+
+
+def rest_kernel(hidden, w2, after, out):
+    del after
+    second_layer(hidden, w2, (0, out.shape[1]), (out,))
+
+
+def near_kernel(own, sib, mod, w1, w2, after, out_own, out_first, out_second, x, hidden):
+    del after
+    most, pad = own.shape[0], x.shape[0] // 2
     x[...] = jnp.zeros_like(x)
-    x[0:most, :] = select(slot_rows(target[...], 0, most), modulated)
-    first_layer(x, w1v, hidden, lambda index: first[index].wait())
-    second_layer(hidden, w2v, (0, w2.shape[1]), (out,), lambda index: second[index].wait())
-
-
-def far_kernel(near_x, far_x, near_z, far_z, mod, w1, w2, after, out_x, out_z, hidden, raw, x):
-    del after
-    most, cut = near_x.shape
-    pad = x.shape[0] // 2
-    x[...] = jnp.zeros_like(x)
-    for i, (left, right) in enumerate(((near_x, far_x), (near_z, far_z))):
-        raw[:, 0:cut] = left[...].astype(jnp.float32)
-        raw[:, cut:] = right[...].astype(jnp.float32)
-        x[i * pad:i * pad + most, :] = modulate(raw[...], mod[0:1, :], mod[1:2, :])
+    x[0:most, :] = own[...]
+    x[pad:pad + most, :] = modulate(sib[...], mod[0:1, :], mod[1:2, :])
     first_layer(x, w1, hidden)
-    second_layer(hidden, w2, (cut, w2.shape[1]), (out_x, out_z))
-
-
-def rest_kernel(hidden, w2, after, out_x, out_z):
-    del after
-    second_layer(hidden, w2, (0, out_x.shape[1]), (out_x, out_z))
-
-
-def sibling_kernel(sib, mod, w1, w2, after, out, x, hidden):
-    del after
-    x[...] = jnp.zeros_like(x)
-    x[0:out.shape[0], :] = modulate(sib[...], mod[0:1, :], mod[1:2, :])
-    first_layer(x, w1, hidden)
-    second_layer(hidden, w2, (0, w2.shape[1]), (out,))
-
-
-def joint_kernel(target, gates, here, there, out):
-    value = mixed(target[...], gates[...], 2, here[...])
-    value += mixed(target[...], gates[...], 3, there[...])
+    cut = out_first.shape[1]
+    second_layer(hidden, w2, (0, cut), (out_own.at[:, 0:cut], out_first))
+    second_layer(hidden, w2, (cut, w2.shape[1]), (out_own.at[:, cut:], out_second))
+
+
+def joint_kernel(target, carried, here, there, later, after, out, out_later):
+    del after
+    out_later[...] = later[...]
+    gates = unpack_gates(carried[:, carried.shape[1] - target.shape[1]:])
+    value = mixed(target[...], gates, 2, here[...])
+    value += mixed(target[...], gates, 3, there[...])
     out[...] = value.astype(jnp.bfloat16)
 
 
 def home_kernel(target, gates, y_own, y_x, y_z, out):
-    cut = y_own.shape[1] - y_x.shape[1]
+    part = y_z.shape[1]
+    cut = y_own.shape[1] - part
     place, weight = target[...], gates[...]
     own = mixed(place, weight, 0, y_own[...])
-    far = mixed(place, weight, 2, y_x[...]) + mixed(place, weight, 3, y_z[...])
+    far = mixed(place, weight, 2, y_x[:, 0:part]) + mixed(place, weight, 3, y_z[...])
     out[:, 0:cut] = own[:, 0:cut]
     out[:, cut:] = own[:, cut:] + far
 
 
-def near_kernel(target, gates, mixture, y_sib, out):
-    out[...] = mixture[...] + mixed(target[...], gates[...], 1, y_sib[...])
+def add_kernel(target, gates, mixture, y_first, y_second, out):
+    cut = y_first.shape[1]
+    place, weight = target[...], gates[...]
+    out[:, 0:cut] = mixture[:, 0:cut] + mixed(place, weight, 1, y_first[...])
+    out[:, cut:] = mixture[:, cut:] + mixed(place, weight, 1, y_second[...])
 
 
 def last_kernel(incoming, mod, mixture, joint, out):
@@ -205,23 +244,46 @@
     return jax.ShapeDtypeStruct((rows, columns), dtype)
 
 
-def source_pass(source, ahead, most, cut):
-    width = source.shape[1]
-    return pl.pallas_call(
-        source_kernel,
-        out_shape=(array(most, width - cut), array(most, width - cut), array(most, width)),
+def sibling_pass(source, ahead, most):
+    return pl.pallas_call(
+        sibling_kernel,
+        out_shape=(array(most, source.shape[1]), array(*source.shape)),
         in_specs=[VMEM] * 2,
-        out_specs=(VMEM,) * 3,
+        out_specs=(VMEM,) * 2,
         compiler_params=PARAMS,
         cost_estimate=SHORT,
     )(source, ahead)
 
 
+def source_pass(mask, source, ahead, after, most, first):
+    return pl.pallas_call(
+        functools.partial(source_kernel, mask),
+        out_shape=array(most, source.shape[1] - first),
+        in_specs=[VMEM] * 2 + [ANY],
+        out_specs=VMEM,
+        compiler_params=PARAMS,
+        cost_estimate=SHORT,
+    )(source, ahead, after)
+
+
+def load_pass(weight, after):
+    loaded = pl.pallas_call(
+        load_kernel,
+        out_shape=pltpu.VMEM(weight.shape, weight.dtype),
+        in_specs=[HBM, ANY],
+        out_specs=VMEM,
+        scratch_shapes=[pltpu.SemaphoreType.DMA((len(tiles(weight.shape[1], 512)),))],
+        compiler_params=PARAMS,
+        cost_estimate=SHORT,
+    )(pltpu.with_memory_space_constraint(weight, pltpu.HBM), after)
+    return pltpu.with_memory_space_constraint(loaded, pltpu.VMEM)
+
+
 def relay_pass(crossed, target, after, most):
-    cut = crossed.shape[1]
+    part = array(most, crossed.shape[1])
     return pl.pallas_call(
         relay_kernel,
-        out_shape=(array(most, cut), array(most, cut)),
+        out_shape=(part, part),
         in_specs=[VMEM] * 2 + [ANY],
         out_specs=(VMEM,) * 2,
         compiler_params=PARAMS,
@@ -229,94 +291,88 @@
     )(crossed, target, after)
 
 
-def own_pass(own, target, chosen, mod, router, w1, w2, after, most):
+def gate_pass(own, target, chosen, mod, router, most):
+    return pl.pallas_call(
+        gate_kernel,
+        out_shape=(array(most, own.shape[1]), array(*chosen.shape, jnp.float32)),
+        in_specs=[VMEM] * 5,
+        out_specs=(VMEM,) * 2,
+        compiler_params=PARAMS,
+        cost_estimate=SHORT,
+    )(own, target, chosen, mod, router)
+
+
+def cross_pass(left, right, mod, gates, w1, w2, cut):
+    most = left.shape[0]
     width, hid = w1.shape
     return pl.pallas_call(
-        own_kernel,
-        out_shape=(
-            array(most, width),
-            array(*chosen.shape, jnp.float32),
-            pltpu.VMEM(w1.shape, w1.dtype),
-            pltpu.VMEM(w2.shape, w2.dtype),
-        ),
-        in_specs=[VMEM] * 5 + [HBM] * 2 + [ANY],
-        out_specs=(VMEM,) * 4,
+        cross_kernel,
+        out_shape=(array(most, width - cut + gates.shape[1]), array(most, hid)),
+        in_specs=[VMEM] * 6,
+        out_specs=(VMEM,) * 2,
         scratch_shapes=[
-            pltpu.VMEM((padded(most), width), jnp.bfloat16),
-            pltpu.VMEM((padded(most), hid), jnp.bfloat16),
-            pltpu.SemaphoreType.DMA((len(tiles(w1.shape[1], 512)),)),
-            pltpu.SemaphoreType.DMA((len(tiles(w2.shape[1], 512)),)),
+            pltpu.VMEM((most, width), jnp.float32),
+            pltpu.VMEM((most, width), jnp.bfloat16),
         ],
         compiler_params=PARAMS,
         cost_estimate=SHORT,
-    )(
-        own,
-        target,
-        chosen,
-        mod,
-        router,
-        pltpu.with_memory_space_constraint(w1, pltpu.HBM),
-        pltpu.with_memory_space_constraint(w2, pltpu.HBM),
-        after,
-    )
-
-
-def far_pass(near_x, far_x, near_z, far_z, mod, w1, w2, after):
-    most = near_x.shape[0]
+    )(left, right, mod, gates, w1, w2)
+
+
+def far_pass(left, right, mod, w1, w2, after, cut):
+    most = left.shape[0]
     width, hid = w1.shape
-    out = array(*far_x.shape)
     return pl.pallas_call(
         far_kernel,
-        out_shape=(out, out, array(2 * padded(most), hid)),
-        in_specs=[VMEM] * 7 + [ANY],
+        out_shape=(array(most, cut), array(most, width - cut)),
+        in_specs=[VMEM] * 5 + [ANY],
+        out_specs=(VMEM,) * 2,
+        scratch_shapes=[
+            pltpu.VMEM((most, hid), jnp.bfloat16),
+            pltpu.VMEM((most, width), jnp.float32),
+            pltpu.VMEM((most, width), jnp.bfloat16),
+        ],
+        compiler_params=PARAMS,
+        cost_estimate=SHORT,
+    )(left, right, mod, w1, w2, after)
+
+
+def rest_pass(hidden, w2, after, cut):
+    return pl.pallas_call(
+        rest_kernel,
+        out_shape=array(hidden.shape[0], cut),
+        in_specs=[VMEM] * 2 + [ANY],
+        out_specs=VMEM,
+        compiler_params=PARAMS,
+        cost_estimate=SHORT,
+    )(hidden, w2, after)
+
+
+def near_pass(own, sib, mod, w1, w2, after, cut):
+    most, width = sib.shape
+    return pl.pallas_call(
+        near_kernel,
+        out_shape=(array(most, width), array(most, cut), array(most, width - cut)),
+        in_specs=[VMEM] * 5 + [ANY],
         out_specs=(VMEM,) * 3,
         scratch_shapes=[
-            pltpu.VMEM((most, width), jnp.float32),
             pltpu.VMEM((2 * padded(most), width), jnp.bfloat16),
+            pltpu.VMEM((2 * padded(most), w1.shape[1]), jnp.bfloat16),
         ],
         compiler_params=PARAMS,
         cost_estimate=SHORT,
-    )(near_x, far_x, near_z, far_z, mod, w1, w2, after)
-
-
-def rest_pass(hidden, w2, after, most, cut):
-    return pl.pallas_call(
-        rest_kernel,
-        out_shape=(array(most, cut), array(most, cut)),
-        in_specs=[VMEM] * 2 + [ANY],
+    )(own, sib, mod, w1, w2, after)
+
+
+def joint_pass(target, carried, here, there, later, after):
+    return pl.pallas_call(
+        joint_kernel,
+        out_shape=(array(target.shape[1], here.shape[1]), array(*later.shape)),
+        in_specs=[VMEM] * 5 + [ANY],
         out_specs=(VMEM,) * 2,
         compiler_params=PARAMS,
         cost_estimate=SHORT,
-    )(hidden, w2, after)
-
-
-def sibling_pass(sib, mod, w1, w2, after):
-    most, width = sib.shape
-    hid = w1.shape[1]
-    return pl.pallas_call(
-        sibling_kernel,
-        out_shape=array(most, width),
-        in_specs=[VMEM] * 4 + [ANY],
-        out_specs=VMEM,
-        scratch_shapes=[
-            pltpu.VMEM((padded(most), width), jnp.bfloat16),
-            pltpu.VMEM((padded(most), hid), jnp.bfloat16),
-        ],
-        compiler_params=PARAMS,
-        cost_estimate=SHORT,
-    )(sib, mod, w1, w2, after)
-
-
-def joint_pass(target, gates, here, there):
-    tokens, cut = target.shape[1], here.shape[1]
-    return pl.pallas_call(
-        joint_kernel,
-        out_shape=array(tokens, cut),
-        in_specs=[VMEM] * 4,
-        out_specs=VMEM,
-        compiler_params=PARAMS,
-        cost_estimate=SHORT,
-    )(target, gates, here, there)
+    )(target, carried, here, there, later, after)
 
 
 def home_pass(target, gates, y_own, y_x, y_z):
@@ -330,15 +386,15 @@
     )(target, gates, y_own, y_x, y_z)
 
 
-def near_pass(target, gates, mixture, y_sib):
-    return pl.pallas_call(
-        near_kernel,
+def add_pass(target, gates, mixture, y_first, y_second):
+    return pl.pallas_call(
+        add_kernel,
         out_shape=array(*mixture.shape, jnp.float32),
-        in_specs=[VMEM] * 4,
+        in_specs=[VMEM] * 5,
         out_specs=VMEM,
         compiler_params=PARAMS,
         cost_estimate=SHORT,
-    )(target, gates, mixture, y_sib)
+    )(target, gates, mixture, y_first, y_second)
 
 
 def last_pass(incoming, mod, mixture, joint):
@@ -357,48 +413,40 @@
     width = source.shape[1]
     most = 3 * source.shape[0] // 4
     cut = width // 256 * 128
+    back_cut = cut
     here = lax.axis_index("expert")
     chosen = routes[0].T
     target = (chosen ^ here) * most + slots[0].T
     x_target = swapped(target, 2)
     ahead = shifted(target, "comp", -1)
     crossed = advanced(source[:, :cut], 2)
-    incoming = shifted(source, "comp", 1)
     mod = modulation[timesteps[0]].astype(jnp.float32)
 
-    x_source, z_source, s_source = source_pass(source, ahead, most, cut)
+    s_source, same = sibling_pass(source, ahead, most)
+    incoming = shifted(same, "comp", 1)
     sib = advanced(s_source, 1)
-    far_x = advanced(x_source, 2)
+    w1 = load_pass(expert_in[0], s_source)
+    far_x = advanced(source_pass(2, source, ahead, w1, most, cut), 2)
+    own, gates = gate_pass(incoming, target, chosen, mod, router_weight[0].T, most)
+
+    near_x, passed = relay_pass(crossed, x_target, w1, most)
+    near_z = swapped(passed, 1)
+    z_source = source_pass(3, source, ahead, passed, most, cut)
     far_z = advanced(z_source, 3)
-
-    y_own, gates, w1, w2 = own_pass(
-        incoming,
-        target,
-        chosen,
-        mod,
-        router_weight[0].T,
-        expert_in[0],
-        expert_out[0],
-        z_source,
-        most,
-    )
-    x_gates = swapped(gates, 2)
-    w1 = pltpu.with_memory_space_constraint(w1, pltpu.VMEM)
-    w2 = pltpu.with_memory_space_constraint(w2, pltpu.VMEM)
-    near_x, passed = relay_pass(crossed, x_target, gates, most)
-    near_z = swapped(passed, 1)
-    y_sib = sibling_pass(sib, mod, w1, w2, passed)
-    back_s = swapped(y_sib, 1)
-    x_right, z_right, hidden = far_pass(
-        near_x, far_x, near_z, far_z, mod, w1, w2, y_sib
-    )
+    w2 = load_pass(expert_out[0], z_source)
+    x_right, x_hidden = cross_pass(near_x, far_x, mod, gates, w1, w2, back_cut)
+    back_x = swapped(x_right, 2)
+    y_own, s_first, s_second = near_pass(own, sib, mod, w1, w2, x_right, cut + 256)
+    back_first = swapped(s_first, 1)
+    z_left, z_right = far_pass(near_z, far_z, mod, w1, w2, s_first, back_cut)
+    lent = swapped(z_left, 1)
     back_z = swapped(z_right, 3)
-    back_x = swapped(x_right, 2)
-    x_left, z_left = rest_pass(hidden, w2, x_gates, most, cut)
-    lent = swapped(z_left, 1)
-    joint = swapped(joint_pass(x_target, x_gates, x_left, lent), 2)
+    x_left = rest_pass(x_hidden, w2, z_left, back_cut)
+    joint, later = joint_pass(x_target, back_x, x_left, lent, s_second, back_first)
+    joint = swapped(joint, 2)
+    back_second = swapped(later, 1)
     mixture = home_pass(target, gates, y_own, back_x, back_z)
-    mixture = near_pass(target, gates, mixture, back_s)
+    mixture = add_pass(target, gates, mixture, back_first, back_second)
     return last_pass(incoming, mod, mixture, joint)[None]
 
 

time: 85.9 us -> 79.1 us (0.921)
  waiting for transfers between devices: 34.4 us -> 27.7 us
  Pallas kernels: 24.6 us -> 28.3 us
  starting transfers between devices: 21.5 us -> 19.1 us
  local copies, waits for them, and re-layouts: 3.51 us -> 2.11 us
    ppermute x8, waiting for transfers between devices: 29.7 us -> 19.9 us  [swapped(): lax.ppermute(block, 'expert', [(e, e ^ mask) for e in range(lax.axis_size...]
    ppermute x4, waiting for transfers between devices: 0.01 us -> 7.81 us  [advanced(): return lax.ppermute(block, ('comp', 'expert'), route)]
    ppermute x2, waiting for transfers between devices: 4.64 us -> 0.01 us  [shifted(): return lax.ppermute(block, axis, route)]
    pallas_call x8 -> x13, Pallas kernels: 23.1 us -> 26.8 us  [the longest x2 9.59 us: load_pass(): pl.pallas_call(load_kernel, out_shape=pltpu.VMEM(weight.shape, weight.dty...]
    unnamed x8 -> x10, local copies, waits for them, and re-layouts: 2.48 us -> 1.08 us
    ppermute x2, starting transfers between devices: 2.38 us -> 1.16 us  [shifted(): return lax.ppermute(block, axis, route)]
    ppermute x8, starting transfers between devices: 13.5 us -> 12.6 us  [swapped(): lax.ppermute(block, 'expert', [(e, e ^ mask) for e in range(lax.axis_size...]
  transfers between devices with their start and end apart: 14 -> 14, of which waited for: 6 -> 6; matrix products, arithmetic and copies ran while one was open for 1% -> 1% of each run, Pallas kernels for 26% -> 35%
where the time goes in v3:
time: 79.1 us; the launch traced here: 78.9 us
  Pallas kernels  28.3 us (36%)
  waiting for transfers between devices  27.7 us (35%)
  starting transfers between devices  19.1 us (24%)
  local copies, waits for them, and re-layouts  2.11 us (3%)
  between operations  0.87 us (1%)
  other arithmetic  0.8 us (1%)
    ppermute x8, waiting for transfers between devices, swapped(): lax.ppermute(block, 'expert', [(e, e ^ mask) for e in range(lax.axis_size...  19.9 us
    ppermute x8, starting transfers between devices, swapped(): lax.ppermute(block, 'expert', [(e, e ^ mask) for e in range(lax.axis_size...  12.6 us
    pallas_call x2, Pallas kernels, load_pass(): pl.pallas_call(load_kernel, out_shape=pltpu.VMEM(weight.shape, weight.dty...  9.59 us
    ppermute x4, waiting for transfers between devices, advanced(): return lax.ppermute(block, ('comp', 'expert'), route)  7.81 us
    ppermute x4, starting transfers between devices, advanced(): return lax.ppermute(block, ('comp', 'expert'), route)  5.41 us
    pallas_call x1, Pallas kernels, near_pass(): pl.pallas_call(near_kernel, out_shape=(array(most, width), array(most, cu...  4.98 us
    pallas_call x1, Pallas kernels, far_pass(): pl.pallas_call(far_kernel, out_shape=(array(most, cut), array(most, width...  4.86 us
    pallas_call x1, Pallas kernels, cross_pass(): pl.pallas_call(cross_kernel, out_shape=(array(most, width - cut + gates.s...  3.75 us
  transfers between devices with their start and end apart: 14, of which 6 were waited for; matrix products, arithmetic and copies ran while one was open for 1% of the time, Pallas kernels for 35%

profile of v3, /device:TPU:0, one launch (start us, length us, event | category | flops | bytes accessed | tf_op | source)
XLA Modules:
  0.0 78.9 jit_solution(2367200556290900097)
XLA Ops:
  0.0 0.0 copy-start
  0.0 0.8 bitcast_add_fusion.target
  0.8 4.0 %collective-permute-start.4 = (s32[2,96]{1,0:T(2,128)S(1)}, s32[2,96]{1,0:T(2,128)S(1)}, u32[]{:S(2)}, u32[]{:S(2)}) collective-permute-start(s32[2,96]{1,0:T(2,128)S(1)} %bitcast_add_fusion.target), channel_id=1, source_target_pairs={{0,2},{1,3},{2,0},{3,1},{4,6},{5,7},{6,4},{7,5},{8,10},{9,11},{10,... | collective-permute-start | bytes 2312 | tf_op jit(solution)/shard_map/ppermute | solution.py:24
  4.8 0.7 collective-permute-start
  5.5 1.0 %slice.4 = bf16[96,1536]{1,0:T(8,128)(2,1)S(1)} slice(bf16[96,3072]{1,0:T(8,128)(2,1)} %bitcast.24), slice={[0:96], [0:1536]} | slice | bytes 589824 | tf_op jit(solution)/shard_map/slice | solution.py:422
  6.5 0.1 collective-permute-start.3
  7.2 0.0 copy-done
  7.2 0.0 collective-permute-done.ahead
  7.3 0.0 copy-start.1
  7.3 1.1 %copy-done.1 = bf16[1,96,3072]{2,1,0:T(8,128)(2,1)S(1)} copy-done((bf16[1,96,3072]{2,1,0:T(8,128)(2,1)S(1)}, bf16[1,96,3072]{2,1,0:T(8,128)(2,1)}, u32[]{:S(2)}) %copy-start.1) | copy-done | bytes 589848
  8.3 0.3 shard_map.82
  8.6 2.0 %collective-permute-start.2 = (bf16[72,3072]{1,0:T(8,128)(2,1)S(1)}, bf16[72,3072]{1,0:T(8,128)(2,1)S(1)}, u32[]{:S(2)}, u32[]{:S(2)}) collective-permute-start(bf16[72,3072]{1,0:T(8,128)(2,1)S(1)} %get-tuple-element.23.after), channel_id=1, source_target_pairs={{0,5},{1,4},{2,7},{3,6},{4,9},{5,8},{6,11},{7,10},{8,13},{9,12},{1... | collective-permute-start | bytes 1327112 | tf_op jit(solution)/shard_map/ppermute | solution.py:34
  10.6 0.5 collective-permute-start.1
  11.1 0.0 copy-start.2
  11.1 4.8 %shard_map.84.after.w1 = bf16[3072,2048]{1,0:T(8,128)(2,1)S(1)} custom-call(bf16[3072,2048]{1,0:T(8,128)(2,1)} %bitcast.31, bf16[72,3072]{1,0:T(8,128)(2,1)S(1)} %get-tuple-element.23.after), custom_call_target="tpu_custom_call" | custom-call | flops 1048576 | bytes 1024 | tf_op jit(solution)/shard_map/pallas_call | solution.py:270
  15.9 0.0 copy-done.2
  15.9 0.2 shard_map.88
  16.1 3.0 %collective-permute-start.5 = (bf16[72,1536]{1,0:T(8,128)(2,1)S(1)}, bf16[72,1536]{1,0:T(8,128)(2,1)S(1)}, u32[]{:S(2)}, u32[]{:S(2)}) collective-permute-start(bf16[72,1536]{1,0:T(8,128)(2,1)S(1)} %shard_map.88), channel_id=1, source_target_pairs={{0,6},{1,7},{2,4},{3,5},{4,10},{5,11},{6,8},{7,9},{8,14},{9,15},{1... | collective-permute-start | bytes 663560 | tf_op jit(solution)/shard_map/ppermute | solution.py:34
  19.1 0.0 collective-permute-done.4.target
  19.1 4.9 %collective-permute-done.3.crossed = bf16[96,1536]{1,0:T(8,128)(2,1)S(1)} collective-permute-done((bf16[96,1536]{1,0:T(8,128)(2,1)S(1)}, bf16[96,1536]{1,0:T(8,128)(2,1)S(1)}, u32[]{:S(2)}, u32[]{:S(2)}) %collective-permute-start.3) | collective-permute-done | bytes 294944 | tf_op jit(solution)/shard_map/ppermute | solution.py:34
  24.0 0.3 shard_map.85
  24.2 0.1 collective-permute-start.7
  24.3 0.2 shard_map.86.after
  24.5 0.4 collective-permute-start.8
  24.9 0.0 copy-start.3
  24.9 0.0 copy-start.4
  24.9 4.8 %shard_map.87.w2 = bf16[2048,3072]{1,0:T(8,128)(2,1)S(1)} custom-call(bf16[2048,3072]{1,0:T(8,128)(2,1)} %bitcast.30, bf16[72,1536]{1,0:T(8,128)(2,1)S(1)} %shard_map.86.after), custom_call_target="tpu_custom_call" | custom-call | flops 1048576 | bytes 1024 | tf_op jit(solution)/shard_map/pallas_call | solution.py:270
  29.7 0.0 collective-permute-done.1.own.incoming
  29.8 0.0 copy-done.3
  29.8 0.0 copy-done.4
  29.8 0.8 shard_map.83
  30.5 2.9 %collective-permute-done.5.right = bf16[72,1536]{1,0:T(8,128)(2,1)S(1)} collective-permute-done((bf16[72,1536]{1,0:T(8,128)(2,1)S(1)}, bf16[72,1536]{1,0:T(8,128)(2,1)S(1)}, u32[]{:S(2)}, u32[]{:S(2)}) %collective-permute-start.5) | collective-permute-done | bytes 221216 | tf_op jit(solution)/shard_map/ppermute | solution.py:34
  33.5 3.8 %shard_map.89 = (bf16[72,1632]{1,0:T(8,128)(2,1)S(1)}, bf16[72,2048]{1,0:T(8,128)(2,1)S(1)}) custom-call(bf16[72,1536]{1,0:T(8,128)(2,1)S(1)} %get-tuple-element.25.left, bf16[72,1536]{1,0:T(8,128)(2,1)S(1)} %collective-permute-done.5.right, f32[3,3072]{1,0:T(4,128)S(1)} %fusion.mod, f32[2,96]{1,0:T(2,128)S(1)} %get-tuple-element.21.gates, ...), custom_call_target="tpu_custom_call" | custom-call | flops 1048576 | bytes 1024 | tf_op jit(solution)/shard_map/pallas_call | solution.py:308
  37.2 0.0 collective-permute-done.2.sib
  37.3 5.0 %shard_map.90 = (bf16[72,3072]{1,0:T(8,128)(2,1)S(1)}, bf16[72,1792]{1,0:T(8,128)(2,1)S(1)}, bf16[72,1280]{1,0:T(8,128)(2,1)S(1)}) custom-call(bf16[72,3072]{1,0:T(8,128)(2,1)S(1)} %get-tuple-element.22.own, bf16[72,3072]{1,0:T(8,128)(2,1)S(1)} %collective-permute-done.2.sib, f32[3,3072]{1,0:T(4,128)S(1)} %fusion.mod, ...), custom_call_target="tpu_custom_call" | custom-call | flops 1048576 | bytes 1024 | tf_op jit(solution)/shard_map/pallas_call | solution.py:353
  42.2 0.1 collective-permute-start.10
  42.3 1.8 %collective-permute-start.6 = (bf16[72,1632]{1,0:T(8,128)(2,1)S(1)}, bf16[72,1632]{1,0:T(8,128)(2,1)S(1)}, u32[]{:S(2)}, u32[]{:S(2)}) collective-permute-start(bf16[72,1632]{1,0:T(8,128)(2,1)S(1)} %get-tuple-element.26.after), channel_id=1, source_target_pairs={{0,2},{1,3},{2,0},{3,1},{4,6},{5,7},{6,4},{7,5},{8,10},{9,11},{10,... | collective-permute-start | bytes 705032 | tf_op jit(solution)/shard_map/ppermute | solution.py:24
  44.2 0.0 collective-permute-done.8.right
  44.2 0.0 collective-permute-done.7.left
  44.2 4.9 %shard_map.91 = (bf16[72,1536]{1,0:T(8,128)(2,1)S(1)}, bf16[72,1536]{1,0:T(8,128)(2,1)S(1)}) custom-call(bf16[72,1536]{1,0:T(8,128)(2,1)S(1)} %collective-permute-done.7.left, bf16[72,1536]{1,0:T(8,128)(2,1)S(1)} %collective-permute-done.8.right, f32[3,3072]{1,0:T(4,128)S(1)} %fusion.mod, bf16[3072,2048]{1,0:T(8,128)(2,1)S(1)} %shard_map.84.after.w1, ...), custom_call_target="tpu_custom_call" | custom-call | flops 1048576 | bytes 1024 | tf_op jit(solution)/shard_map/pallas_call | solution.py:325
  49.0 0.2 collective-permute-start.11
  49.3 2.4 %collective-permute-start.9 = (bf16[72,1536]{1,0:T(8,128)(2,1)S(1)}, bf16[72,1536]{1,0:T(8,128)(2,1)S(1)}, u32[]{:S(2)}, u32[]{:S(2)}) collective-permute-start(bf16[72,1536]{1,0:T(8,128)(2,1)S(1)} %get-tuple-element.29), channel_id=1, source_target_pairs={{0,3},{1,2},{2,1},{3,0},{4,7},{5,6},{6,5},{7,4},{8,11},{9,10},{10,... | collective-permute-start | bytes 663560 | tf_op jit(solution)/shard_map/ppermute | solution.py:24
  51.7 1.2 %shard_map.93.here = bf16[72,1536]{1,0:T(8,128)(2,1)S(1)} custom-call(bf16[72,2048]{1,0:T(8,128)(2,1)S(1)} %get-tuple-element.30.hidden, bf16[2048,3072]{1,0:T(8,128)(2,1)S(1)} %shard_map.87.w2, bf16[72,1536]{1,0:T(8,128)(2,1)S(1)} %get-tuple-element.31.after), custom_call_target="tpu_custom_call" | custom-call | flops 1048576 | bytes 1024 | tf_op jit(solution)/shard_map/pallas_call | solution.py:341
  52.9 6.4 %collective-permute-done.11.there = bf16[72,1536]{1,0:T(8,128)(2,1)S(1)} collective-permute-done((bf16[72,1536]{1,0:T(8,128)(2,1)S(1)}, bf16[72,1536]{1,0:T(8,128)(2,1)S(1)}, u32[]{:S(2)}, u32[]{:S(2)}) %collective-permute-start.11) | collective-permute-done | bytes 221216 | tf_op jit(solution)/shard_map/ppermute | solution.py:24
  59.3 0.0 collective-permute-done.6.y_x.carried
  59.3 0.0 collective-permute-done.10.after.y_first
  59.3 0.4 shard_map.94
  59.7 2.2 %collective-permute-start.12 = (bf16[72,1280]{1,0:T(8,128)(2,1)S(1)}, bf16[72,1280]{1,0:T(8,128)(2,1)S(1)}, u32[]{:S(2)}, u32[]{:S(2)}) collective-permute-start(bf16[72,1280]{1,0:T(8,128)(2,1)S(1)} %get-tuple-element.33), channel_id=1, source_target_pairs={{0,1},{1,0},{2,3},{3,2},{4,5},{5,4},{6,7},{7,6},{8,9},{9,8},{10,11... | collective-permute-start | bytes 552968 | tf_op jit(solution)/shard_map/ppermute | solution.py:24
  61.8 1.7 %collective-permute-start.13 = (bf16[96,1536]{1,0:T(8,128)(2,1)S(1)}, bf16[96,1536]{1,0:T(8,128)(2,1)S(1)}, u32[]{:S(2)}, u32[]{:S(2)}) collective-permute-start(bf16[96,1536]{1,0:T(8,128)(2,1)S(1)} %get-tuple-element.34), channel_id=1, source_target_pairs={{0,2},{1,3},{2,0},{3,1},{4,6},{5,7},{6,4},{7,5},{8,10},{9,11},{10,... | collective-permute-start | bytes 884744 | tf_op jit(solution)/shard_map/ppermute | solution.py:24
  63.5 1.9 %collective-permute-done.9.y_z = bf16[72,1536]{1,0:T(8,128)(2,1)S(1)} collective-permute-done((bf16[72,1536]{1,0:T(8,128)(2,1)S(1)}, bf16[72,1536]{1,0:T(8,128)(2,1)S(1)}, u32[]{:S(2)}, u32[]{:S(2)}) %collective-permute-start.9) | collective-permute-done | bytes 221216 | tf_op jit(solution)/shard_map/ppermute | solution.py:24
  65.5 0.5 shard_map.92.mixture
  66.0 7.2 %collective-permute-done.12.y_second = bf16[72,1280]{1,0:T(8,128)(2,1)S(1)} collective-permute-done((bf16[72,1280]{1,0:T(8,128)(2,1)S(1)}, bf16[72,1280]{1,0:T(8,128)(2,1)S(1)}, u32[]{:S(2)}, u32[]{:S(2)}) %collective-permute-start.12) | collective-permute-done | bytes 184352 | tf_op jit(solution)/shard_map/ppermute | solution.py:24
  73.3 0.3 shard_map.95.mixture
  73.6 4.3 %collective-permute-done.13.joint = bf16[96,1536]{1,0:T(8,128)(2,1)S(1)} collective-permute-done((bf16[96,1536]{1,0:T(8,128)(2,1)S(1)}, bf16[96,1536]{1,0:T(8,128)(2,1)S(1)}, u32[]{:S(2)}, u32[]{:S(2)}) %collective-permute-start.13) | collective-permute-done | bytes 294944 | tf_op jit(solution)/shard_map/ppermute | solution.py:24
  77.9 1.0 %shard_map.96 = bf16[96,3072]{1,0:T(8,128)(2,1)} custom-call(bf16[96,3072]{1,0:T(8,128)(2,1)S(1)} %collective-permute-done.1.own.incoming, f32[3,3072]{1,0:T(4,128)S(1)} %fusion.mod, f32[96,3072]{1,0:T(8,128)S(1)} %shard_map.95.mixture, bf16[96,1536]{1,0:T(8,128)(2,1)S(1)} %collective-permute-done.13.joint), custom_call_target="tpu_custom_call" | custom-call | flops 1048576 | bytes 1024 | tf_op jit(solution)/shard_map/pallas_call | solution.py:401
  (2 shorter events, 0.1 us)
Async XLA Ops:
  0.0 7.2 %copy-start = (bf16[50,3,3072]{2,0,1:T(8,128)(2,1)S(1)}, bf16[50,3,3072]{2,0,1:T(8,128)(2,1)}, u32[]{:S(2)}) copy-start(bf16[50,3,3072]{2,0,1:T(8,128)(2,1)} %param.15) | copy-start | bytes 2764804
  0.8 18.3 %collective-permute-start.4 = (s32[2,96]{1,0:T(2,128)S(1)}, s32[2,96]{1,0:T(2,128)S(1)}, u32[]{:S(2)}, u32[]{:S(2)}) collective-permute-start(s32[2,96]{1,0:T(2,128)S(1)} %bitcast_add_fusion.target), channel_id=1, source_target_pairs={{0,2},{1,3},{2,0},{3,1},{4,6},{5,7},{6,4},{7,5},{8,10},{9,11},{10,... | collective-permute-start | bytes 2312 | tf_op jit(solution)/shard_map/ppermute | solution.py:24
  4.8 2.4 %collective-permute-start = (s32[2,96]{1,0:T(2,128)S(1)}, s32[2,96]{1,0:T(2,128)S(1)}, u32[]{:S(2)}, u32[]{:S(2)}) collective-permute-start(s32[2,96]{1,0:T(2,128)S(1)} %bitcast_add_fusion.target), channel_id=1, source_target_pairs={{4,0},{8,4},{12,8},{0,12},{5,1},{9,5},{13,9},{1,13},{6,2},{10,6},{... | collective-permute-start | bytes 2312 | tf_op jit(solution)/shard_map/ppermute | solution.py:20
  6.5 17.5 %collective-permute-start.3 = (bf16[96,1536]{1,0:T(8,128)(2,1)S(1)}, bf16[96,1536]{1,0:T(8,128)(2,1)S(1)}, u32[]{:S(2)}, u32[]{:S(2)}) collective-permute-start(bf16[96,1536]{1,0:T(8,128)(2,1)S(1)} %slice.4), channel_id=1, source_target_pairs={{0,6},{1,7},{2,4},{3,5},{4,10},{5,11},{6,8},{7,9},{8,14},{9,15},{1... | collective-permute-start | bytes 884744 | tf_op jit(solution)/shard_map/ppermute | solution.py:34
  7.3 1.1 %copy-start.1 = (bf16[1,96,3072]{2,1,0:T(8,128)(2,1)S(1)}, bf16[1,96,3072]{2,1,0:T(8,128)(2,1)}, u32[]{:S(2)}) copy-start(bf16[1,96,3072]{2,1,0:T(8,128)(2,1)} %param.8) | copy-start | bytes 1769476
  8.6 28.7 %collective-permute-start.2 = (bf16[72,3072]{1,0:T(8,128)(2,1)S(1)}, bf16[72,3072]{1,0:T(8,128)(2,1)S(1)}, u32[]{:S(2)}, u32[]{:S(2)}) collective-permute-start(bf16[72,3072]{1,0:T(8,128)(2,1)S(1)} %get-tuple-element.23.after), channel_id=1, source_target_pairs={{0,5},{1,4},{2,7},{3,6},{4,9},{5,8},{6,11},{7,10},{8,13},{9,12},{1... | collective-permute-start | bytes 1327112 | tf_op jit(solution)/shard_map/ppermute | solution.py:34
  10.6 19.2 %collective-permute-start.1 = (bf16[96,3072]{1,0:T(8,128)(2,1)S(1)}, bf16[96,3072]{1,0:T(8,128)(2,1)S(1)}, u32[]{:S(2)}, u32[]{:S(2)}) collective-permute-start(bf16[96,3072]{1,0:T(8,128)(2,1)S(1)} %get-tuple-element.20), channel_id=1, source_target_pairs={{12,0},{0,4},{4,8},{8,12},{13,1},{1,5},{5,9},{9,13},{14,2},{2,6},{... | collective-permute-start | bytes 1769480 | tf_op jit(solution)/shard_map/ppermute | solution.py:20
  11.1 4.8 %copy-start.2 = (bf16[1,96,3072]{2,1,0:T(8,128)(2,1)S(1)}, bf16[1,96,3072]{2,1,0:T(8,128)(2,1)}, u32[]{:S(2)}) copy-start(bf16[1,96,3072]{2,1,0:T(8,128)(2,1)} %param.8) | copy-start | bytes 1769476
  16.1 17.4 %collective-permute-start.5 = (bf16[72,1536]{1,0:T(8,128)(2,1)S(1)}, bf16[72,1536]{1,0:T(8,128)(2,1)S(1)}, u32[]{:S(2)}, u32[]{:S(2)}) collective-permute-start(bf16[72,1536]{1,0:T(8,128)(2,1)S(1)} %shard_map.88), channel_id=1, source_target_pairs={{0,6},{1,7},{2,4},{3,5},{4,10},{5,11},{6,8},{7,9},{8,14},{9,15},{1... | collective-permute-start | bytes 663560 | tf_op jit(solution)/shard_map/ppermute | solution.py:34
  24.2 19.9 %collective-permute-start.7 = (bf16[72,1536]{1,0:T(8,128)(2,1)S(1)}, bf16[72,1536]{1,0:T(8,128)(2,1)S(1)}, u32[]{:S(2)}, u32[]{:S(2)}) collective-permute-start(bf16[72,1536]{1,0:T(8,128)(2,1)S(1)} %get-tuple-element.24.after), channel_id=1, source_target_pairs={{0,1},{1,0},{2,3},{3,2},{4,5},{5,4},{6,7},{7,6},{8,9},{9,8},{10,11... | collective-permute-start | bytes 663560 | tf_op jit(solution)/shard_map/ppermute | solution.py:24
  24.5 19.6 %collective-permute-start.8 = (bf16[72,1536]{1,0:T(8,128)(2,1)S(1)}, bf16[72,1536]{1,0:T(8,128)(2,1)S(1)}, u32[]{:S(2)}, u32[]{:S(2)}) collective-permute-start(bf16[72,1536]{1,0:T(8,128)(2,1)S(1)} %shard_map.86.after), channel_id=1, source_target_pairs={{0,7},{1,6},{2,5},{3,4},{4,11},{5,10},{6,9},{7,8},{8,15},{9,14},{1... | collective-permute-start | bytes 663560 | tf_op jit(solution)/shard_map/ppermute | solution.py:34
  24.9 4.8 %copy-start.3 = (bf16[1,3072,4]{1,2,0:T(4,128)(2,1)S(1)}, bf16[1,3072,4]{1,2,0:T(4,128)(2,1)}, u32[]{:S(2)}) copy-start(bf16[1,3072,4]{1,2,0:T(4,128)(2,1)} %param.12) | copy-start | bytes 73732
  24.9 4.8 %copy-start.4 = (s32[1,96,2]{1,2,0:T(2,128)S(1)}, s32[1,96,2]{1,2,0:T(2,128)}, u32[]{:S(2)}) copy-start(s32[1,96,2]{1,2,0:T(2,128)} %param.9) | copy-start | bytes 2308
  42.2 17.0 %collective-permute-start.10 = (bf16[72,1792]{1,0:T(8,128)(2,1)S(1)}, bf16[72,1792]{1,0:T(8,128)(2,1)S(1)}, u32[]{:S(2)}, u32[]{:S(2)}) collective-permute-start(bf16[72,1792]{1,0:T(8,128)(2,1)S(1)} %get-tuple-element.28.after), channel_id=1, source_target_pairs={{0,1},{1,0},{2,3},{3,2},{4,5},{5,4},{6,7},{7,6},{8,9},{9,8},{10,11... | collective-permute-start | bytes 774152 | tf_op jit(solution)/shard_map/ppermute | solution.py:24
  42.3 17.0 %collective-permute-start.6 = (bf16[72,1632]{1,0:T(8,128)(2,1)S(1)}, bf16[72,1632]{1,0:T(8,128)(2,1)S(1)}, u32[]{:S(2)}, u32[]{:S(2)}) collective-permute-start(bf16[72,1632]{1,0:T(8,128)(2,1)S(1)} %get-tuple-element.26.after), channel_id=1, source_target_pairs={{0,2},{1,3},{2,0},{3,1},{4,6},{5,7},{6,4},{7,5},{8,10},{9,11},{10,... | collective-permute-start | bytes 705032 | tf_op jit(solution)/shard_map/ppermute | solution.py:24
  49.0 10.3 %collective-permute-start.11 = (bf16[72,1536]{1,0:T(8,128)(2,1)S(1)}, bf16[72,1536]{1,0:T(8,128)(2,1)S(1)}, u32[]{:S(2)}, u32[]{:S(2)}) collective-permute-start(bf16[72,1536]{1,0:T(8,128)(2,1)S(1)} %get-tuple-element.31.after), channel_id=1, source_target_pairs={{0,1},{1,0},{2,3},{3,2},{4,5},{5,4},{6,7},{7,6},{8,9},{9,8},{10,11... | collective-permute-start | bytes 663560 | tf_op jit(solution)/shard_map/ppermute | solution.py:24
  49.3 16.2 %collective-permute-start.9 = (bf16[72,1536]{1,0:T(8,128)(2,1)S(1)}, bf16[72,1536]{1,0:T(8,128)(2,1)S(1)}, u32[]{:S(2)}, u32[]{:S(2)}) collective-permute-start(bf16[72,1536]{1,0:T(8,128)(2,1)S(1)} %get-tuple-element.29), channel_id=1, source_target_pairs={{0,3},{1,2},{2,1},{3,0},{4,7},{5,6},{6,5},{7,4},{8,11},{9,10},{10,... | collective-permute-start | bytes 663560 | tf_op jit(solution)/shard_map/ppermute | solution.py:24
  59.7 13.6 %collective-permute-start.12 = (bf16[72,1280]{1,0:T(8,128)(2,1)S(1)}, bf16[72,1280]{1,0:T(8,128)(2,1)S(1)}, u32[]{:S(2)}, u32[]{:S(2)}) collective-permute-start(bf16[72,1280]{1,0:T(8,128)(2,1)S(1)} %get-tuple-element.33), channel_id=1, source_target_pairs={{0,1},{1,0},{2,3},{3,2},{4,5},{5,4},{6,7},{7,6},{8,9},{9,8},{10,11... | collective-permute-start | bytes 552968 | tf_op jit(solution)/shard_map/ppermute | solution.py:24
  61.8 16.1 %collective-permute-start.13 = (bf16[96,1536]{1,0:T(8,128)(2,1)S(1)}, bf16[96,1536]{1,0:T(8,128)(2,1)S(1)}, u32[]{:S(2)}, u32[]{:S(2)}) collective-permute-start(bf16[96,1536]{1,0:T(8,128)(2,1)S(1)} %get-tuple-element.34), channel_id=1, source_target_pairs={{0,2},{1,3},{2,0},{3,1},{4,6},{5,7},{6,4},{7,5},{8,10},{9,11},{10,... | collective-permute-start | bytes 884744 | tf_op jit(solution)/shard_map/ppermute | solution.py:24

commit v4 on v3

--- a/solution.py
+++ b/solution.py
@@ -91,7 +91,8 @@
             out[:, start:start + size] = rows.astype(jnp.bfloat16)
 
 
-def sibling_kernel(source, ahead, out, out_source):
+def sibling_kernel(source, ahead, target, out, out_source, out_target):
+    out_target[...] = target[...]
     out[...] = select(slot_rows(ahead[...], 1, out.shape[0]), source[...])
     out_source[...] = source[...]
 
@@ -169,34 +170,44 @@
     second_layer(hidden, w2, (width - part, width), (out.at[:, 0:part],))
 
 
-def far_kernel(left, right, mod, w1, w2, after, out_left, out_right, hidden, raw, x):
-    del after
-    cut = out_left.shape[1]
-    far_hidden(left, right, mod, w1, hidden, raw, x)
-    second_layer(hidden, w2, (0, cut), (out_left,))
-    second_layer(hidden, w2, (cut, w2.shape[1]), (out_right,))
-
-
-def rest_kernel(hidden, w2, after, out):
-    del after
-    second_layer(hidden, w2, (0, out.shape[1]), (out,))
-
-
-def near_kernel(own, sib, mod, w1, w2, after, out_own, out_first, out_second, x, hidden):
-    del after
-    most, pad = own.shape[0], x.shape[0] // 2
-    x[...] = jnp.zeros_like(x)
-    x[0:most, :] = own[...]
-    x[pad:pad + most, :] = modulate(sib[...], mod[0:1, :], mod[1:2, :])
+def far_kernel(
+    left, right, mod, w1, w2, x_hidden, after, out_x, out_z, z_hidden, hidden, raw, x
+):
+    del after
+    most, cut = left.shape
+    pad = hidden.shape[0] // 2
+    hidden[...] = jnp.zeros_like(hidden)
+    hidden[0:most, :] = x_hidden[...]
+    far_hidden(left, right, mod, w1, hidden.at[pad:pad + most, :], raw, x)
+    z_hidden[...] = hidden[pad:pad + most, :]
+    second_layer(hidden, w2, (0, out_x.shape[1]), (out_x, out_z))
+
+
+def rest_kernel(hidden, w2, out):
+    second_layer(hidden, w2, (w2.shape[1] - out.shape[1], w2.shape[1]), (out,))
+
+
+def near_kernel(own, sib, mod, w1, w2, after, out_own, out_first, out_second, raw, x, hidden):
+    del after
+    most = own.shape[0]
+    raw[0:most, :] = own[...].astype(jnp.float32)
+    for start, size in tiles(most, 16):
+        rows = modulate(sib[start:start + size, :], mod[0:1, :], mod[1:2, :])
+        raw[most + start:most + start + size, :] = rows.astype(jnp.float32)
+    x[...] = raw[...].astype(jnp.bfloat16)
     first_layer(x, w1, hidden)
     cut = out_first.shape[1]
     second_layer(hidden, w2, (0, cut), (out_own.at[:, 0:cut], out_first))
     second_layer(hidden, w2, (cut, w2.shape[1]), (out_own.at[:, cut:], out_second))
 
 
-def joint_kernel(target, carried, here, there, later, after, out, out_later):
-    del after
-    out_later[...] = later[...]
+def copy_kernel(source, after, out):
+    del after
+    out[...] = source[...]
+
+
+def joint_kernel(target, carried, here, there, after, out):
+    del after
     gates = unpack_gates(carried[:, carried.shape[1] - target.shape[1]:])
     value = mixed(target[...], gates, 2, here[...])
     value += mixed(target[...], gates, 3, there[...])
@@ -244,15 +255,19 @@
     return jax.ShapeDtypeStruct((rows, columns), dtype)
 
 
-def sibling_pass(source, ahead, most):
+def sibling_pass(source, ahead, target, most):
     return pl.pallas_call(
         sibling_kernel,
-        out_shape=(array(most, source.shape[1]), array(*source.shape)),
-        in_specs=[VMEM] * 2,
-        out_specs=(VMEM,) * 2,
-        compiler_params=PARAMS,
-        cost_estimate=SHORT,
-    )(source, ahead)
+        out_shape=(
+            array(most, source.shape[1]),
+            array(*source.shape),
+            array(*target.shape, target.dtype),
+        ),
+        in_specs=[VMEM] * 3,
+        out_specs=(VMEM,) * 3,
+        compiler_params=PARAMS,
+        cost_estimate=SHORT,
+    )(source, ahead, target)
 
 
 def source_pass(mask, source, ahead, after, most, first):
@@ -319,33 +334,33 @@
     )(left, right, mod, gates, w1, w2)
 
 
-def far_pass(left, right, mod, w1, w2, after, cut):
+def far_pass(left, right, mod, w1, w2, x_hidden, after, cut):
     most = left.shape[0]
     width, hid = w1.shape
     return pl.pallas_call(
         far_kernel,
-        out_shape=(array(most, cut), array(most, width - cut)),
-        in_specs=[VMEM] * 5 + [ANY],
-        out_specs=(VMEM,) * 2,
+        out_shape=(array(most, cut), array(most, cut), array(most, hid)),
+        in_specs=[VMEM] * 6 + [ANY],
+        out_specs=(VMEM,) * 3,
         scratch_shapes=[
-            pltpu.VMEM((most, hid), jnp.bfloat16),
+            pltpu.VMEM((2 * padded(most), hid), jnp.bfloat16),
             pltpu.VMEM((most, width), jnp.float32),
             pltpu.VMEM((most, width), jnp.bfloat16),
         ],
         compiler_params=PARAMS,
         cost_estimate=SHORT,
-    )(left, right, mod, w1, w2, after)
-
-
-def rest_pass(hidden, w2, after, cut):
+    )(left, right, mod, w1, w2, x_hidden, after)
+
+
+def rest_pass(hidden, w2, part):
     return pl.pallas_call(
         rest_kernel,
-        out_shape=array(hidden.shape[0], cut),
-        in_specs=[VMEM] * 2 + [ANY],
-        out_specs=VMEM,
-        compiler_params=PARAMS,
-        cost_estimate=SHORT,
-    )(hidden, w2, after)
+        out_shape=array(hidden.shape[0], part),
+        in_specs=[VMEM] * 2,
+        out_specs=VMEM,
+        compiler_params=PARAMS,
+        cost_estimate=SHORT,
+    )(hidden, w2)
 
 
 def near_pass(own, sib, mod, w1, w2, after, cut):
@@ -356,23 +371,35 @@
         in_specs=[VMEM] * 5 + [ANY],
         out_specs=(VMEM,) * 3,
         scratch_shapes=[
-            pltpu.VMEM((2 * padded(most), width), jnp.bfloat16),
-            pltpu.VMEM((2 * padded(most), w1.shape[1]), jnp.bfloat16),
+            pltpu.VMEM((2 * most, width), jnp.float32),
+            pltpu.VMEM((2 * most, width), jnp.bfloat16),
+            pltpu.VMEM((2 * most, w1.shape[1]), jnp.bfloat16),
         ],
         compiler_params=PARAMS,
         cost_estimate=SHORT,
     )(own, sib, mod, w1, w2, after)
 
 
-def joint_pass(target, carried, here, there, later, after):
+def copy_pass(source, after):
+    return pl.pallas_call(
+        copy_kernel,
+        out_shape=array(*source.shape),
+        in_specs=[VMEM, ANY],
+        out_specs=VMEM,
+        compiler_params=PARAMS,
+        cost_estimate=SHORT,
+    )(source, after)
+
+
+def joint_pass(target, carried, here, there, after):
     return pl.pallas_call(
         joint_kernel,
-        out_shape=(array(target.shape[1], here.shape[1]), array(*later.shape)),
-        in_specs=[VMEM] * 5 + [ANY],
-        out_specs=(VMEM,) * 2,
-        compiler_params=PARAMS,
-        cost_estimate=SHORT,
-    )(target, carried, here, there, later, after)
+        out_shape=array(target.shape[1], here.shape[1]),
+        in_specs=[VMEM] * 4 + [ANY],
+        out_specs=VMEM,
+        compiler_params=PARAMS,
+        cost_estimate=SHORT,
+    )(target, carried, here, there, after)
 
 
 def home_pass(target, gates, y_own, y_x, y_z):
@@ -414,15 +441,16 @@
     most = 3 * source.shape[0] // 4
     cut = width // 256 * 128
     back_cut = cut
+    sib_cut = cut + 256
     here = lax.axis_index("expert")
     chosen = routes[0].T
     target = (chosen ^ here) * most + slots[0].T
-    x_target = swapped(target, 2)
     ahead = shifted(target, "comp", -1)
     crossed = advanced(source[:, :cut], 2)
     mod = modulation[timesteps[0]].astype(jnp.float32)
 
-    s_source, same = sibling_pass(source, ahead, most)
+    s_source, same, same_target = sibling_pass(source, ahead, target, most)
+    x_target = swapped(same_target, 2)
     incoming = shifted(same, "comp", 1)
     sib = advanced(s_source, 1)
     w1 = load_pass(expert_in[0], s_source)
@@ -436,15 +464,16 @@
     w2 = load_pass(expert_out[0], z_source)
     x_right, x_hidden = cross_pass(near_x, far_x, mod, gates, w1, w2, back_cut)
     back_x = swapped(x_right, 2)
-    y_own, s_first, s_second = near_pass(own, sib, mod, w1, w2, x_right, cut + 256)
+    y_own, s_first, s_second = near_pass(own, sib, mod, w1, w2, x_right, sib_cut)
     back_first = swapped(s_first, 1)
-    z_left, z_right = far_pass(near_z, far_z, mod, w1, w2, s_first, back_cut)
+    x_left, z_left, z_hidden = far_pass(
+        near_z, far_z, mod, w1, w2, x_hidden, x_hidden, back_cut
+    )
     lent = swapped(z_left, 1)
-    back_z = swapped(z_right, 3)
-    x_left = rest_pass(x_hidden, w2, z_left, back_cut)
-    joint, later = joint_pass(x_target, back_x, x_left, lent, s_second, back_first)
+    back_z = swapped(rest_pass(z_hidden, w2, width - back_cut), 3)
+    joint = joint_pass(x_target, back_x, x_left, lent, back_first)
+    back_second = swapped(copy_pass(s_second, joint), 1)
     joint = swapped(joint, 2)
-    back_second = swapped(later, 1)
     mixture = home_pass(target, gates, y_own, back_x, back_z)
     mixture = add_pass(target, gates, mixture, back_first, back_second)
     return last_pass(incoming, mod, mixture, joint)[None]

time: 79.1 us -> 77.3 us (0.977); the launches traced: 78.9 us -> 76.1 us
  waiting for transfers between devices: 27.7 us -> 19.6 us
  starting transfers between devices: 19.1 us -> 25.8 us
  Pallas kernels: 28.3 us -> 26.9 us
    ppermute x4, waiting for transfers between devices: 7.81 us -> 1.77 us  [advanced(): return lax.ppermute(block, ('comp', 'expert'), route)]
    ppermute x4, starting transfers between devices: 5.41 us -> 8.35 us  [advanced(): return lax.ppermute(block, ('comp', 'expert'), route)]
    ppermute x2, starting transfers between devices: 1.16 us -> 3.16 us  [shifted(): return lax.ppermute(block, axis, route)]
    ppermute x8, waiting for transfers between devices: 19.9 us -> 17.9 us  [swapped(): lax.ppermute(block, 'expert', [(e, e ^ mask) for e in range(lax.axis_size...]
    ppermute x8, starting transfers between devices: 12.6 us -> 14.3 us  [swapped(): lax.ppermute(block, 'expert', [(e, e ^ mask) for e in range(lax.axis_size...]
    pallas_call x3 -> x4, Pallas kernels: 6.42 us -> 5.31 us  [the longest x1 3.73 us: far_pass(): pl.pallas_call(far_kernel, out_shape=(array(most, cut), array(most, cut),...]
  transfers between devices with their start and end apart: 14 -> 14, of which waited for: 6 -> 6; matrix products, arithmetic and copies ran while one was open for 1% -> 1% of each run, Pallas kernels for 35% -> 34%
where the time goes in v4:
time: 77.3 us; the launch traced here: 76.1 us
  Pallas kernels  26.9 us (35%)
  starting transfers between devices  25.8 us (33%)
  waiting for transfers between devices  19.6 us (25%)
  local copies, waits for them, and re-layouts  2.1 us (3%)
  between operations  0.87 us (1%)
  other arithmetic  0.8 us (1%)
    ppermute x8, waiting for transfers between devices, swapped(): lax.ppermute(block, 'expert', [(e, e ^ mask) for e in range(lax.axis_size...  17.9 us
    ppermute x8, starting transfers between devices, swapped(): lax.ppermute(block, 'expert', [(e, e ^ mask) for e in range(lax.axis_size...  14.3 us
    pallas_call x2, Pallas kernels, load_pass(): pl.pallas_call(load_kernel, out_shape=pltpu.VMEM(weight.shape, weight.dty...  9.59 us
    ppermute x4, starting transfers between devices, advanced(): return lax.ppermute(block, ('comp', 'expert'), route)  8.35 us
    pallas_call x1, Pallas kernels, near_pass(): pl.pallas_call(near_kernel, out_shape=(array(most, width), array(most, cu...  4.61 us
    pallas_call x1, Pallas kernels, cross_pass(): pl.pallas_call(cross_kernel, out_shape=(array(most, width - cut + gates.s...  3.78 us
    pallas_call x1, Pallas kernels, far_pass(): pl.pallas_call(far_kernel, out_shape=(array(most, cut), array(most, cut),...  3.73 us
    ppermute x2, starting transfers between devices, shifted(): return lax.ppermute(block, axis, route)  3.16 us
  transfers between devices with their start and end apart: 14, of which 6 were waited for; matrix products, arithmetic and copies ran while one was open for 1% of the time, Pallas kernels for 34%

profile of v4, /device:TPU:0, one launch (start us, length us, event | category | flops | bytes accessed | tf_op | source)
XLA Modules:
  0.0 76.1 jit_solution(13136895124175318816)
XLA Ops:
  0.0 0.0 copy-start
  0.0 0.8 %bitcast_add_fusion.target = s32[2,96]{1,0:T(2,128)S(1)} fusion(s32[1,96,2]{1,2,0:T(2,128)} %param.10, s32[]{:T(128)S(6)} %axis_index.12, s32[1,96,2]{1,2,0:T(2,128)} %param.9), kind=kLoop, calls=%fused_computation.2 | loop fusion | flops 576 | bytes 2308 | tf_op jit(solution)/shard_map/add | solution.py:447
  0.8 2.4 %collective-permute-start = (s32[2,96]{1,0:T(2,128)S(1)}, s32[2,96]{1,0:T(2,128)S(1)}, u32[]{:S(2)}, u32[]{:S(2)}) collective-permute-start(s32[2,96]{1,0:T(2,128)S(1)} %bitcast_add_fusion.target), channel_id=1, source_target_pairs={{4,0},{8,4},{12,8},{0,12},{5,1},{9,5},{13,9},{1,13},{6,2},{10,6},{... | collective-permute-start | bytes 2312 | tf_op jit(solution)/shard_map/ppermute | solution.py:20
  3.2 1.0 %slice.4 = bf16[96,1536]{1,0:T(8,128)(2,1)S(1)} slice(bf16[96,3072]{1,0:T(8,128)(2,1)} %bitcast.24), slice={[0:96], [0:1536]} | slice | bytes 589824 | tf_op jit(solution)/shard_map/slice | solution.py:449
  4.2 1.8 %collective-permute-start.3 = (bf16[96,1536]{1,0:T(8,128)(2,1)S(1)}, bf16[96,1536]{1,0:T(8,128)(2,1)S(1)}, u32[]{:S(2)}, u32[]{:S(2)}) collective-permute-start(bf16[96,1536]{1,0:T(8,128)(2,1)S(1)} %slice.4), channel_id=1, source_target_pairs={{0,6},{1,7},{2,4},{3,5},{4,10},{5,11},{6,8},{7,9},{8,14},{9,15},{1... | collective-permute-start | bytes 884744 | tf_op jit(solution)/shard_map/ppermute | solution.py:34
  6.6 0.0 collective-permute-done.ahead
  6.6 0.0 copy-start.1
  6.7 1.1 %copy-done.1 = bf16[1,96,3072]{2,1,0:T(8,128)(2,1)S(1)} copy-done((bf16[1,96,3072]{2,1,0:T(8,128)(2,1)S(1)}, bf16[1,96,3072]{2,1,0:T(8,128)(2,1)}, u32[]{:S(2)}) %copy-start.1) | copy-done | bytes 589848
  7.7 0.3 shard_map.82
  8.0 0.9 %collective-permute-start.4 = (s32[2,96]{1,0:T(2,128)S(1)}, s32[2,96]{1,0:T(2,128)S(1)}, u32[]{:S(2)}, u32[]{:S(2)}) collective-permute-start(s32[2,96]{1,0:T(2,128)S(1)} %get-tuple-element.24), channel_id=1, source_target_pairs={{0,2},{1,3},{2,0},{3,1},{4,6},{5,7},{6,4},{7,5},{8,10},{9,11},{10,... | collective-permute-start | bytes 2312 | tf_op jit(solution)/shard_map/ppermute | solution.py:24
  8.9 0.0 copy-done
  8.9 1.4 %collective-permute-start.2 = (bf16[72,3072]{1,0:T(8,128)(2,1)S(1)}, bf16[72,3072]{1,0:T(8,128)(2,1)S(1)}, u32[]{:S(2)}, u32[]{:S(2)}) collective-permute-start(bf16[72,3072]{1,0:T(8,128)(2,1)S(1)} %get-tuple-element.23.after), channel_id=1, source_target_pairs={{0,5},{1,4},{2,7},{3,6},{4,9},{5,8},{6,11},{7,10},{8,13},{9,12},{1... | collective-permute-start | bytes 1327112 | tf_op jit(solution)/shard_map/ppermute | solution.py:34
  10.3 0.8 %collective-permute-start.1 = (bf16[96,3072]{1,0:T(8,128)(2,1)S(1)}, bf16[96,3072]{1,0:T(8,128)(2,1)S(1)}, u32[]{:S(2)}, u32[]{:S(2)}) collective-permute-start(bf16[96,3072]{1,0:T(8,128)(2,1)S(1)} %get-tuple-element.20), channel_id=1, source_target_pairs={{12,0},{0,4},{4,8},{8,12},{13,1},{1,5},{5,9},{9,13},{14,2},{2,6},{... | collective-permute-start | bytes 1769480 | tf_op jit(solution)/shard_map/ppermute | solution.py:20
  11.1 0.0 copy-start.2
  11.1 4.8 %shard_map.84.after.w1 = bf16[3072,2048]{1,0:T(8,128)(2,1)S(1)} custom-call(bf16[3072,2048]{1,0:T(8,128)(2,1)} %bitcast.31, bf16[72,3072]{1,0:T(8,128)(2,1)S(1)} %get-tuple-element.23.after), custom_call_target="tpu_custom_call" | custom-call | flops 1048576 | bytes 1024 | tf_op jit(solution)/shard_map/pallas_call | solution.py:285
  15.9 0.0 copy-done.2
  15.9 0.2 shard_map.88
  16.1 3.0 %collective-permute-start.5 = (bf16[72,1536]{1,0:T(8,128)(2,1)S(1)}, bf16[72,1536]{1,0:T(8,128)(2,1)S(1)}, u32[]{:S(2)}, u32[]{:S(2)}) collective-permute-start(bf16[72,1536]{1,0:T(8,128)(2,1)S(1)} %shard_map.88), channel_id=1, source_target_pairs={{0,6},{1,7},{2,4},{3,5},{4,10},{5,11},{6,8},{7,9},{8,14},{9,15},{1... | collective-permute-start | bytes 663560 | tf_op jit(solution)/shard_map/ppermute | solution.py:34
  19.2 1.9 %collective-permute-done.4.target = s32[2,96]{1,0:T(2,128)S(1)} collective-permute-done((s32[2,96]{1,0:T(2,128)S(1)}, s32[2,96]{1,0:T(2,128)S(1)}, u32[]{:S(2)}, u32[]{:S(2)}) %collective-permute-start.4) | collective-permute-done | bytes 800 | tf_op jit(solution)/shard_map/ppermute | solution.py:24
  21.1 0.6 collective-permute-done.3.crossed
  21.8 0.3 shard_map.85
  22.0 0.1 collective-permute-start.7
  22.1 0.2 shard_map.86.after
  22.3 2.1 %collective-permute-start.8 = (bf16[72,1536]{1,0:T(8,128)(2,1)S(1)}, bf16[72,1536]{1,0:T(8,128)(2,1)S(1)}, u32[]{:S(2)}, u32[]{:S(2)}) collective-permute-start(bf16[72,1536]{1,0:T(8,128)(2,1)S(1)} %shard_map.86.after), channel_id=1, source_target_pairs={{0,7},{1,6},{2,5},{3,4},{4,11},{5,10},{6,9},{7,8},{8,15},{9,14},{1... | collective-permute-start | bytes 663560 | tf_op jit(solution)/shard_map/ppermute | solution.py:34
  24.4 0.0 copy-start.3
  24.4 0.0 copy-start.4
  24.5 4.8 %shard_map.87.w2 = bf16[2048,3072]{1,0:T(8,128)(2,1)S(1)} custom-call(bf16[2048,3072]{1,0:T(8,128)(2,1)} %bitcast.30, bf16[72,1536]{1,0:T(8,128)(2,1)S(1)} %shard_map.86.after), custom_call_target="tpu_custom_call" | custom-call | flops 1048576 | bytes 1024 | tf_op jit(solution)/shard_map/pallas_call | solution.py:285
  29.3 0.0 collective-permute-done.1.own.incoming
  29.3 0.0 copy-done.3
  29.3 0.0 copy-done.4
  29.3 0.8 %shard_map.83 = (bf16[72,3072]{1,0:T(8,128)(2,1)S(1)}, f32[2,96]{1,0:T(2,128)S(1)}) custom-call(bf16[96,3072]{1,0:T(8,128)(2,1)S(1)} %collective-permute-done.1.own.incoming, s32[2,96]{1,0:T(2,128)S(1)} %bitcast_add_fusion.target, s32[2,96]{1,0:T(2,128)S(1)} %bitcast.29, f32[3,3072]{1,0:T(4,128)S(1)} %fusion.mod, bf16[4,3072]{1,0:T(4,128)(2,1)S(1)} %bitcast.28), custom_call_target="tpu_custom_call" | custom-call | flops 1048576 | bytes 1024 | tf_op jit(solution)/shard_map/pallas_call | solution.py:310
  30.1 1.1 %collective-permute-done.5.right = bf16[72,1536]{1,0:T(8,128)(2,1)S(1)} collective-permute-done((bf16[72,1536]{1,0:T(8,128)(2,1)S(1)}, bf16[72,1536]{1,0:T(8,128)(2,1)S(1)}, u32[]{:S(2)}, u32[]{:S(2)}) %collective-permute-start.5) | collective-permute-done | bytes 221216 | tf_op jit(solution)/shard_map/ppermute | solution.py:34
  31.2 3.8 %shard_map.89 = (bf16[72,1632]{1,0:T(8,128)(2,1)S(1)}, bf16[72,2048]{1,0:T(8,128)(2,1)S(1)}) custom-call(bf16[72,1536]{1,0:T(8,128)(2,1)S(1)} %get-tuple-element.26.left, bf16[72,1536]{1,0:T(8,128)(2,1)S(1)} %collective-permute-done.5.right, f32[3,3072]{1,0:T(4,128)S(1)} %fusion.mod, f32[2,96]{1,0:T(2,128)S(1)} %get-tuple-element.21.gates, ...), custom_call_target="tpu_custom_call" | custom-call | flops 1048576 | bytes 1024 | tf_op jit(solution)/shard_map/pallas_call | solution.py:323
  35.0 0.0 collective-permute-done.2.sib
  35.0 4.6 %shard_map.90 = (bf16[72,3072]{1,0:T(8,128)(2,1)S(1)}, bf16[72,1792]{1,0:T(8,128)(2,1)S(1)}, bf16[72,1280]{1,0:T(8,128)(2,1)S(1)}) custom-call(bf16[72,3072]{1,0:T(8,128)(2,1)S(1)} %get-tuple-element.22.own, bf16[72,3072]{1,0:T(8,128)(2,1)S(1)} %collective-permute-done.2.sib, f32[3,3072]{1,0:T(4,128)S(1)} %fusion.mod, ...), custom_call_target="tpu_custom_call" | custom-call | flops 1048576 | bytes 1024 | tf_op jit(solution)/shard_map/pallas_call | solution.py:368
  39.6 0.1 collective-permute-start.10
  39.7 3.9 %collective-permute-start.6 = (bf16[72,1632]{1,0:T(8,128)(2,1)S(1)}, bf16[72,1632]{1,0:T(8,128)(2,1)S(1)}, u32[]{:S(2)}, u32[]{:S(2)}) collective-permute-start(bf16[72,1632]{1,0:T(8,128)(2,1)S(1)} %get-tuple-element.27.after), channel_id=1, source_target_pairs={{0,2},{1,3},{2,0},{3,1},{4,6},{5,7},{6,4},{7,5},{8,10},{9,11},{10,... | collective-permute-start | bytes 705032 | tf_op jit(solution)/shard_map/ppermute | solution.py:24
  43.6 0.0 collective-permute-done.8.right
  43.6 0.0 collective-permute-done.7.left
  43.6 3.7 %shard_map.91 = (bf16[72,1536]{1,0:T(8,128)(2,1)S(1)}, bf16[72,1536]{1,0:T(8,128)(2,1)S(1)}, bf16[72,2048]{1,0:T(8,128)(2,1)S(1)}) custom-call(bf16[72,1536]{1,0:T(8,128)(2,1)S(1)} %collective-permute-done.7.left, bf16[72,1536]{1,0:T(8,128)(2,1)S(1)} %collective-permute-done.8.right, f32[3,3072]{1,0:T(4,128)S(1)} %fusion.mod, ...), custom_call_target="tpu_custom_call" | custom-call | flops 1048576 | bytes 1024 | tf_op jit(solution)/shard_map/pallas_call | solution.py:340
  47.4 0.1 collective-permute-start.11
  47.5 1.2 %shard_map.92 = bf16[72,1536]{1,0:T(8,128)(2,1)S(1)} custom-call(bf16[72,2048]{1,0:T(8,128)(2,1)S(1)} %get-tuple-element.30.hidden, bf16[2048,3072]{1,0:T(8,128)(2,1)S(1)} %shard_map.87.w2), custom_call_target="tpu_custom_call" | custom-call | flops 1048576 | bytes 1024 | tf_op jit(solution)/shard_map/pallas_call | solution.py:356
  48.7 2.2 %collective-permute-start.9 = (bf16[72,1536]{1,0:T(8,128)(2,1)S(1)}, bf16[72,1536]{1,0:T(8,128)(2,1)S(1)}, u32[]{:S(2)}, u32[]{:S(2)}) collective-permute-start(bf16[72,1536]{1,0:T(8,128)(2,1)S(1)} %shard_map.92), channel_id=1, source_target_pairs={{0,3},{1,2},{2,1},{3,0},{4,7},{5,6},{6,5},{7,4},{8,11},{9,10},{10,... | collective-permute-start | bytes 663560 | tf_op jit(solution)/shard_map/ppermute | solution.py:24
  50.9 8.1 %collective-permute-done.11.there = bf16[72,1536]{1,0:T(8,128)(2,1)S(1)} collective-permute-done((bf16[72,1536]{1,0:T(8,128)(2,1)S(1)}, bf16[72,1536]{1,0:T(8,128)(2,1)S(1)}, u32[]{:S(2)}, u32[]{:S(2)}) %collective-permute-start.11) | collective-permute-done | bytes 221216 | tf_op jit(solution)/shard_map/ppermute | solution.py:24
  58.9 0.0 collective-permute-done.6.y_x.carried
  59.0 0.0 collective-permute-done.10.after.y_first
  59.0 0.3 shard_map.94.after
  59.3 0.1 collective-permute-start.13
  59.4 7.0 %collective-permute-start.12 = (bf16[72,1280]{1,0:T(8,128)(2,1)S(1)}, bf16[72,1280]{1,0:T(8,128)(2,1)S(1)}, u32[]{:S(2)}, u32[]{:S(2)}) collective-permute-start(bf16[72,1280]{1,0:T(8,128)(2,1)S(1)} %shard_map.95), channel_id=1, source_target_pairs={{0,1},{1,0},{2,3},{3,2},{4,5},{5,4},{6,7},{7,6},{8,9},{9,8},{10,11... | collective-permute-start | bytes 552968 | tf_op jit(solution)/shard_map/ppermute | solution.py:24
  66.4 0.0 collective-permute-done.9.y_z
  66.4 0.5 shard_map.93.mixture
  66.9 4.5 %collective-permute-done.12.y_second = bf16[72,1280]{1,0:T(8,128)(2,1)S(1)} collective-permute-done((bf16[72,1280]{1,0:T(8,128)(2,1)S(1)}, bf16[72,1280]{1,0:T(8,128)(2,1)S(1)}, u32[]{:S(2)}, u32[]{:S(2)}) %collective-permute-start.12) | collective-permute-done | bytes 184352 | tf_op jit(solution)/shard_map/ppermute | solution.py:24
  71.5 0.3 shard_map.96.mixture
  71.8 3.3 %collective-permute-done.13.joint = bf16[96,1536]{1,0:T(8,128)(2,1)S(1)} collective-permute-done((bf16[96,1536]{1,0:T(8,128)(2,1)S(1)}, bf16[96,1536]{1,0:T(8,128)(2,1)S(1)}, u32[]{:S(2)}, u32[]{:S(2)}) %collective-permute-start.13) | collective-permute-done | bytes 294944 | tf_op jit(solution)/shard_map/ppermute | solution.py:24
  75.1 1.0 %shard_map.97 = bf16[96,3072]{1,0:T(8,128)(2,1)} custom-call(bf16[96,3072]{1,0:T(8,128)(2,1)S(1)} %collective-permute-done.1.own.incoming, f32[3,3072]{1,0:T(4,128)S(1)} %fusion.mod, f32[96,3072]{1,0:T(8,128)S(1)} %shard_map.96.mixture, bf16[96,1536]{1,0:T(8,128)(2,1)S(1)} %collective-permute-done.13.joint), custom_call_target="tpu_custom_call" | custom-call | flops 1048576 | bytes 1024 | tf_op jit(solution)/shard_map/pallas_call | solution.py:428
  (3 shorter events, 0.1 us)
Async XLA Ops:
  0.0 8.9 %copy-start = (bf16[50,3,3072]{2,0,1:T(8,128)(2,1)S(1)}, bf16[50,3,3072]{2,0,1:T(8,128)(2,1)}, u32[]{:S(2)}) copy-start(bf16[50,3,3072]{2,0,1:T(8,128)(2,1)} %param.15) | copy-start | bytes 2764804
  0.8 5.8 %collective-permute-start = (s32[2,96]{1,0:T(2,128)S(1)}, s32[2,96]{1,0:T(2,128)S(1)}, u32[]{:S(2)}, u32[]{:S(2)}) collective-permute-start(s32[2,96]{1,0:T(2,128)S(1)} %bitcast_add_fusion.target), channel_id=1, source_target_pairs={{4,0},{8,4},{12,8},{0,12},{5,1},{9,5},{13,9},{1,13},{6,2},{10,6},{... | collective-permute-start | bytes 2312 | tf_op jit(solution)/shard_map/ppermute | solution.py:20
  4.2 17.6 %collective-permute-start.3 = (bf16[96,1536]{1,0:T(8,128)(2,1)S(1)}, bf16[96,1536]{1,0:T(8,128)(2,1)S(1)}, u32[]{:S(2)}, u32[]{:S(2)}) collective-permute-start(bf16[96,1536]{1,0:T(8,128)(2,1)S(1)} %slice.4), channel_id=1, source_target_pairs={{0,6},{1,7},{2,4},{3,5},{4,10},{5,11},{6,8},{7,9},{8,14},{9,15},{1... | collective-permute-start | bytes 884744 | tf_op jit(solution)/shard_map/ppermute | solution.py:34
  6.6 1.1 %copy-start.1 = (bf16[1,96,3072]{2,1,0:T(8,128)(2,1)S(1)}, bf16[1,96,3072]{2,1,0:T(8,128)(2,1)}, u32[]{:S(2)}) copy-start(bf16[1,96,3072]{2,1,0:T(8,128)(2,1)} %param.8) | copy-start | bytes 1769476
  8.0 13.1 %collective-permute-start.4 = (s32[2,96]{1,0:T(2,128)S(1)}, s32[2,96]{1,0:T(2,128)S(1)}, u32[]{:S(2)}, u32[]{:S(2)}) collective-permute-start(s32[2,96]{1,0:T(2,128)S(1)} %get-tuple-element.24), channel_id=1, source_target_pairs={{0,2},{1,3},{2,0},{3,1},{4,6},{5,7},{6,4},{7,5},{8,10},{9,11},{10,... | collective-permute-start | bytes 2312 | tf_op jit(solution)/shard_map/ppermute | solution.py:24
  8.9 26.0 %collective-permute-start.2 = (bf16[72,3072]{1,0:T(8,128)(2,1)S(1)}, bf16[72,3072]{1,0:T(8,128)(2,1)S(1)}, u32[]{:S(2)}, u32[]{:S(2)}) collective-permute-start(bf16[72,3072]{1,0:T(8,128)(2,1)S(1)} %get-tuple-element.23.after), channel_id=1, source_target_pairs={{0,5},{1,4},{2,7},{3,6},{4,9},{5,8},{6,11},{7,10},{8,13},{9,12},{1... | collective-permute-start | bytes 1327112 | tf_op jit(solution)/shard_map/ppermute | solution.py:34
  10.3 18.9 %collective-permute-start.1 = (bf16[96,3072]{1,0:T(8,128)(2,1)S(1)}, bf16[96,3072]{1,0:T(8,128)(2,1)S(1)}, u32[]{:S(2)}, u32[]{:S(2)}) collective-permute-start(bf16[96,3072]{1,0:T(8,128)(2,1)S(1)} %get-tuple-element.20), channel_id=1, source_target_pairs={{12,0},{0,4},{4,8},{8,12},{13,1},{1,5},{5,9},{9,13},{14,2},{2,6},{... | collective-permute-start | bytes 1769480 | tf_op jit(solution)/shard_map/ppermute | solution.py:20
  11.1 4.8 %copy-start.2 = (bf16[1,96,3072]{2,1,0:T(8,128)(2,1)S(1)}, bf16[1,96,3072]{2,1,0:T(8,128)(2,1)}, u32[]{:S(2)}) copy-start(bf16[1,96,3072]{2,1,0:T(8,128)(2,1)} %param.8) | copy-start | bytes 1769476
  16.1 15.1 %collective-permute-start.5 = (bf16[72,1536]{1,0:T(8,128)(2,1)S(1)}, bf16[72,1536]{1,0:T(8,128)(2,1)S(1)}, u32[]{:S(2)}, u32[]{:S(2)}) collective-permute-start(bf16[72,1536]{1,0:T(8,128)(2,1)S(1)} %shard_map.88), channel_id=1, source_target_pairs={{0,6},{1,7},{2,4},{3,5},{4,10},{5,11},{6,8},{7,9},{8,14},{9,15},{1... | collective-permute-start | bytes 663560 | tf_op jit(solution)/shard_map/ppermute | solution.py:34
  22.0 21.6 %collective-permute-start.7 = (bf16[72,1536]{1,0:T(8,128)(2,1)S(1)}, bf16[72,1536]{1,0:T(8,128)(2,1)S(1)}, u32[]{:S(2)}, u32[]{:S(2)}) collective-permute-start(bf16[72,1536]{1,0:T(8,128)(2,1)S(1)} %get-tuple-element.25.after), channel_id=1, source_target_pairs={{0,1},{1,0},{2,3},{3,2},{4,5},{5,4},{6,7},{7,6},{8,9},{9,8},{10,11... | collective-permute-start | bytes 663560 | tf_op jit(solution)/shard_map/ppermute | solution.py:24
  22.3 21.3 %collective-permute-start.8 = (bf16[72,1536]{1,0:T(8,128)(2,1)S(1)}, bf16[72,1536]{1,0:T(8,128)(2,1)S(1)}, u32[]{:S(2)}, u32[]{:S(2)}) collective-permute-start(bf16[72,1536]{1,0:T(8,128)(2,1)S(1)} %shard_map.86.after), channel_id=1, source_target_pairs={{0,7},{1,6},{2,5},{3,4},{4,11},{5,10},{6,9},{7,8},{8,15},{9,14},{1... | collective-permute-start | bytes 663560 | tf_op jit(solution)/shard_map/ppermute | solution.py:34
  24.4 4.8 %copy-start.3 = (bf16[1,3072,4]{1,2,0:T(4,128)(2,1)S(1)}, bf16[1,3072,4]{1,2,0:T(4,128)(2,1)}, u32[]{:S(2)}) copy-start(bf16[1,3072,4]{1,2,0:T(4,128)(2,1)} %param.12) | copy-start | bytes 73732
  24.4 4.8 %copy-start.4 = (s32[1,96,2]{1,2,0:T(2,128)S(1)}, s32[1,96,2]{1,2,0:T(2,128)}, u32[]{:S(2)}) copy-start(s32[1,96,2]{1,2,0:T(2,128)} %param.9) | copy-start | bytes 2308
  39.6 19.4 %collective-permute-start.10 = (bf16[72,1792]{1,0:T(8,128)(2,1)S(1)}, bf16[72,1792]{1,0:T(8,128)(2,1)S(1)}, u32[]{:S(2)}, u32[]{:S(2)}) collective-permute-start(bf16[72,1792]{1,0:T(8,128)(2,1)S(1)} %get-tuple-element.31), channel_id=1, source_target_pairs={{0,1},{1,0},{2,3},{3,2},{4,5},{5,4},{6,7},{7,6},{8,9},{9,8},{10,11... | collective-permute-start | bytes 774152 | tf_op jit(solution)/shard_map/ppermute | solution.py:24
  39.7 19.3 %collective-permute-start.6 = (bf16[72,1632]{1,0:T(8,128)(2,1)S(1)}, bf16[72,1632]{1,0:T(8,128)(2,1)S(1)}, u32[]{:S(2)}, u32[]{:S(2)}) collective-permute-start(bf16[72,1632]{1,0:T(8,128)(2,1)S(1)} %get-tuple-element.27.after), channel_id=1, source_target_pairs={{0,2},{1,3},{2,0},{3,1},{4,6},{5,7},{6,4},{7,5},{8,10},{9,11},{10,... | collective-permute-start | bytes 705032 | tf_op jit(solution)/shard_map/ppermute | solution.py:24
  47.4 11.6 %collective-permute-start.11 = (bf16[72,1536]{1,0:T(8,128)(2,1)S(1)}, bf16[72,1536]{1,0:T(8,128)(2,1)S(1)}, u32[]{:S(2)}, u32[]{:S(2)}) collective-permute-start(bf16[72,1536]{1,0:T(8,128)(2,1)S(1)} %get-tuple-element.34), channel_id=1, source_target_pairs={{0,1},{1,0},{2,3},{3,2},{4,5},{5,4},{6,7},{7,6},{8,9},{9,8},{10,11... | collective-permute-start | bytes 663560 | tf_op jit(solution)/shard_map/ppermute | solution.py:24
  48.7 17.7 %collective-permute-start.9 = (bf16[72,1536]{1,0:T(8,128)(2,1)S(1)}, bf16[72,1536]{1,0:T(8,128)(2,1)S(1)}, u32[]{:S(2)}, u32[]{:S(2)}) collective-permute-start(bf16[72,1536]{1,0:T(8,128)(2,1)S(1)} %shard_map.92), channel_id=1, source_target_pairs={{0,3},{1,2},{2,1},{3,0},{4,7},{5,6},{6,5},{7,4},{8,11},{9,10},{10,... | collective-permute-start | bytes 663560 | tf_op jit(solution)/shard_map/ppermute | solution.py:24
  59.3 15.8 %collective-permute-start.13 = (bf16[96,1536]{1,0:T(8,128)(2,1)S(1)}, bf16[96,1536]{1,0:T(8,128)(2,1)S(1)}, u32[]{:S(2)}, u32[]{:S(2)}) collective-permute-start(bf16[96,1536]{1,0:T(8,128)(2,1)S(1)} %shard_map.94.after), channel_id=1, source_target_pairs={{0,2},{1,3},{2,0},{3,1},{4,6},{5,7},{6,4},{7,5},{8,10},{9,11},{10,... | collective-permute-start | bytes 884744 | tf_op jit(solution)/shard_map/ppermute | solution.py:24
  59.4 12.1 %collective-permute-start.12 = (bf16[72,1280]{1,0:T(8,128)(2,1)S(1)}, bf16[72,1280]{1,0:T(8,128)(2,1)S(1)}, u32[]{:S(2)}, u32[]{:S(2)}) collective-permute-start(bf16[72,1280]{1,0:T(8,128)(2,1)S(1)} %shard_map.95), channel_id=1, source_target_pairs={{0,1},{1,0},{2,3},{3,2},{4,5},{5,4},{6,7},{7,6},{8,9},{9,8},{10,11... | collective-permute-start | bytes 552968 | tf_op jit(solution)/shard_map/ppermute | solution.py:24

commit v5 on v4

--- a/solution.py
+++ b/solution.py
@@ -224,20 +224,23 @@
     out[:, cut:] = own[:, cut:] + far
 
 
-def add_kernel(target, gates, mixture, y_first, y_second, out):
-    cut = y_first.shape[1]
+def add_kernel(incoming, mod, target, gates, mixture, y_first, y_second, out_left, out_right):
     place, weight = target[...], gates[...]
-    out[:, 0:cut] = mixture[:, 0:cut] + mixed(place, weight, 1, y_first[...])
-    out[:, cut:] = mixture[:, cut:] + mixed(place, weight, 1, y_second[...])
-
-
-def last_kernel(incoming, mod, mixture, joint, out):
+    cut = out_left.shape[1]
+    first = mixed(place, weight, 1, y_first[...])
+    second = mixed(place, weight, 1, y_second[...])
+    scale = 1.0 + mod[2:3, :]
+    near = jnp.concatenate([first, second], axis=1)
+    total = incoming[...].astype(jnp.float32) + scale * (mixture[...] + near)
+    out_left[...] = total[:, 0:cut]
+    out_right[...] = total[:, cut:].astype(jnp.bfloat16)
+
+
+def last_kernel(mod, left, right, joint, out):
     cut = joint.shape[1]
-    left = mixture[:, 0:cut] + joint[...].astype(jnp.float32)
-    left = incoming[:, 0:cut].astype(jnp.float32) + (1.0 + mod[2:3, 0:cut]) * left
-    right = incoming[:, cut:].astype(jnp.float32) + (1.0 + mod[2:3, cut:]) * mixture[:, cut:]
-    out[:, 0:cut] = left.astype(jnp.bfloat16)
-    out[:, cut:] = right.astype(jnp.bfloat16)
+    value = left[...] + (1.0 + mod[2:3, 0:cut]) * joint[...].astype(jnp.float32)
+    out[:, 0:cut] = value.astype(jnp.bfloat16)
+    out[:, cut:] = right[...]
 
 
 def cost(flops):
@@ -413,26 +416,27 @@
     )(target, gates, y_own, y_x, y_z)
 
 
-def add_pass(target, gates, mixture, y_first, y_second):
+def add_pass(incoming, mod, target, gates, mixture, y_first, y_second, cut):
+    tokens, width = incoming.shape
     return pl.pallas_call(
         add_kernel,
-        out_shape=array(*mixture.shape, jnp.float32),
-        in_specs=[VMEM] * 5,
-        out_specs=VMEM,
-        compiler_params=PARAMS,
-        cost_estimate=SHORT,
-    )(target, gates, mixture, y_first, y_second)
-
-
-def last_pass(incoming, mod, mixture, joint):
+        out_shape=(array(tokens, cut, jnp.float32), array(tokens, width - cut)),
+        in_specs=[VMEM] * 7,
+        out_specs=(VMEM,) * 2,
+        compiler_params=PARAMS,
+        cost_estimate=SHORT,
+    )(incoming, mod, target, gates, mixture, y_first, y_second)
+
+
+def last_pass(mod, left, right, joint):
     return pl.pallas_call(
         last_kernel,
-        out_shape=array(*incoming.shape),
+        out_shape=array(left.shape[0], left.shape[1] + right.shape[1]),
         in_specs=[VMEM] * 4,
         out_specs=VMEM,
         compiler_params=PARAMS,
         cost_estimate=SHORT,
-    )(incoming, mod, mixture, joint)
+    )(mod, left, right, joint)
 
 
 def quad_body(states, routes, slots, timesteps, router_weight, expert_in, expert_out, modulation):
@@ -475,8 +479,10 @@
     back_second = swapped(copy_pass(s_second, joint), 1)
     joint = swapped(joint, 2)
     mixture = home_pass(target, gates, y_own, back_x, back_z)
-    mixture = add_pass(target, gates, mixture, back_first, back_second)
-    return last_pass(incoming, mod, mixture, joint)[None]
+    left, right = add_pass(
+        incoming, mod, target, gates, mixture, back_first, back_second, back_cut
+    )
+    return last_pass(mod, left, right, joint)[None]
 
 
 def gating(modulated, weight, chosen):

time: 77.3 us -> 77.1 us (level)
  no operation moved by 1% of the time
where the time goes in v5:
time: 77.1 us; the launch traced here: 76 us
  Pallas kernels  26.8 us (35%)
  starting transfers between devices  26.1 us (34%)
  waiting for transfers between devices  19.4 us (25%)
  local copies, waits for them, and re-layouts  2.11 us (3%)
  between operations  0.88 us (1%)
  other arithmetic  0.8 us (1%)
    ppermute x8, waiting for transfers between devices, swapped(): lax.ppermute(block, 'expert', [(e, e ^ mask) for e in range(lax.axis_size...  17.6 us
    ppermute x8, starting transfers between devices, swapped(): lax.ppermute(block, 'expert', [(e, e ^ mask) for e in range(lax.axis_size...  14.5 us
    pallas_call x2, Pallas kernels, load_pass(): pl.pallas_call(load_kernel, out_shape=pltpu.VMEM(weight.shape, weight.dty...  9.59 us
    ppermute x4, starting transfers between devices, advanced(): return lax.ppermute(block, ('comp', 'expert'), route)  8.35 us
    pallas_call x1, Pallas kernels, near_pass(): pl.pallas_call(near_kernel, out_shape=(array(most, width), array(most, cu...  4.61 us
    pallas_call x1, Pallas kernels, cross_pass(): pl.pallas_call(cross_kernel, out_shape=(array(most, width - cut + gates.s...  3.75 us
    pallas_call x1, Pallas kernels, far_pass(): pl.pallas_call(far_kernel, out_shape=(array(most, cut), array(most, cut),...  3.73 us
    ppermute x2, starting transfers between devices, shifted(): return lax.ppermute(block, axis, route)  3.16 us
  transfers between devices with their start and end apart: 14, of which 6 were waited for; matrix products, arithmetic and copies ran while one was open for 1% of the time, Pallas kernels for 34%

profile of v5, /device:TPU:0, one launch (start us, length us, event | category | flops | bytes accessed | tf_op | source)
XLA Modules:
  0.0 76.0 jit_solution(16224440357490722112)
XLA Ops:
  0.0 0.0 copy-start
  0.0 0.8 %bitcast_add_fusion.target = s32[2,96]{1,0:T(2,128)S(1)} fusion(s32[1,96,2]{1,2,0:T(2,128)} %param.10, s32[]{:T(128)S(6)} %axis_index.12, s32[1,96,2]{1,2,0:T(2,128)} %param.9), kind=kLoop, calls=%fused_computation.2 | loop fusion | flops 576 | bytes 2308 | tf_op jit(solution)/shard_map/add | solution.py:451
  0.8 2.4 %collective-permute-start = (s32[2,96]{1,0:T(2,128)S(1)}, s32[2,96]{1,0:T(2,128)S(1)}, u32[]{:S(2)}, u32[]{:S(2)}) collective-permute-start(s32[2,96]{1,0:T(2,128)S(1)} %bitcast_add_fusion.target), channel_id=1, source_target_pairs={{4,0},{8,4},{12,8},{0,12},{5,1},{9,5},{13,9},{1,13},{6,2},{10,6},{... | collective-permute-start | bytes 2312 | tf_op jit(solution)/shard_map/ppermute | solution.py:20
  3.2 1.0 %slice.4 = bf16[96,1536]{1,0:T(8,128)(2,1)S(1)} slice(bf16[96,3072]{1,0:T(8,128)(2,1)} %bitcast.24), slice={[0:96], [0:1536]} | slice | bytes 589824 | tf_op jit(solution)/shard_map/slice | solution.py:453
  4.2 1.8 %collective-permute-start.3 = (bf16[96,1536]{1,0:T(8,128)(2,1)S(1)}, bf16[96,1536]{1,0:T(8,128)(2,1)S(1)}, u32[]{:S(2)}, u32[]{:S(2)}) collective-permute-start(bf16[96,1536]{1,0:T(8,128)(2,1)S(1)} %slice.4), channel_id=1, source_target_pairs={{0,6},{1,7},{2,4},{3,5},{4,10},{5,11},{6,8},{7,9},{8,14},{9,15},{1... | collective-permute-start | bytes 884744 | tf_op jit(solution)/shard_map/ppermute | solution.py:34
  6.6 0.0 collective-permute-done.ahead
  6.6 0.0 copy-start.1
  6.7 1.1 %copy-done.1 = bf16[1,96,3072]{2,1,0:T(8,128)(2,1)S(1)} copy-done((bf16[1,96,3072]{2,1,0:T(8,128)(2,1)S(1)}, bf16[1,96,3072]{2,1,0:T(8,128)(2,1)}, u32[]{:S(2)}) %copy-start.1) | copy-done | bytes 589848
  7.7 0.3 shard_map.82
  8.0 0.9 %collective-permute-start.4 = (s32[2,96]{1,0:T(2,128)S(1)}, s32[2,96]{1,0:T(2,128)S(1)}, u32[]{:S(2)}, u32[]{:S(2)}) collective-permute-start(s32[2,96]{1,0:T(2,128)S(1)} %get-tuple-element.26), channel_id=1, source_target_pairs={{0,2},{1,3},{2,0},{3,1},{4,6},{5,7},{6,4},{7,5},{8,10},{9,11},{10,... | collective-permute-start | bytes 2312 | tf_op jit(solution)/shard_map/ppermute | solution.py:24
  8.9 0.0 copy-done
  8.9 1.4 %collective-permute-start.2 = (bf16[72,3072]{1,0:T(8,128)(2,1)S(1)}, bf16[72,3072]{1,0:T(8,128)(2,1)S(1)}, u32[]{:S(2)}, u32[]{:S(2)}) collective-permute-start(bf16[72,3072]{1,0:T(8,128)(2,1)S(1)} %get-tuple-element.25.after), channel_id=1, source_target_pairs={{0,5},{1,4},{2,7},{3,6},{4,9},{5,8},{6,11},{7,10},{8,13},{9,12},{1... | collective-permute-start | bytes 1327112 | tf_op jit(solution)/shard_map/ppermute | solution.py:34
  10.3 0.8 %collective-permute-start.1 = (bf16[96,3072]{1,0:T(8,128)(2,1)S(1)}, bf16[96,3072]{1,0:T(8,128)(2,1)S(1)}, u32[]{:S(2)}, u32[]{:S(2)}) collective-permute-start(bf16[96,3072]{1,0:T(8,128)(2,1)S(1)} %get-tuple-element.22), channel_id=1, source_target_pairs={{12,0},{0,4},{4,8},{8,12},{13,1},{1,5},{5,9},{9,13},{14,2},{2,6},{... | collective-permute-start | bytes 1769480 | tf_op jit(solution)/shard_map/ppermute | solution.py:20
  11.1 0.0 copy-start.2
  11.1 4.8 %shard_map.84.after.w1 = bf16[3072,2048]{1,0:T(8,128)(2,1)S(1)} custom-call(bf16[3072,2048]{1,0:T(8,128)(2,1)} %bitcast.31, bf16[72,3072]{1,0:T(8,128)(2,1)S(1)} %get-tuple-element.25.after), custom_call_target="tpu_custom_call" | custom-call | flops 1048576 | bytes 1024 | tf_op jit(solution)/shard_map/pallas_call | solution.py:288
  15.9 0.0 copy-done.2
  15.9 0.2 shard_map.88
  16.1 3.0 %collective-permute-start.5 = (bf16[72,1536]{1,0:T(8,128)(2,1)S(1)}, bf16[72,1536]{1,0:T(8,128)(2,1)S(1)}, u32[]{:S(2)}, u32[]{:S(2)}) collective-permute-start(bf16[72,1536]{1,0:T(8,128)(2,1)S(1)} %shard_map.88), channel_id=1, source_target_pairs={{0,6},{1,7},{2,4},{3,5},{4,10},{5,11},{6,8},{7,9},{8,14},{9,15},{1... | collective-permute-start | bytes 663560 | tf_op jit(solution)/shard_map/ppermute | solution.py:34
  19.2 1.9 %collective-permute-done.4.target = s32[2,96]{1,0:T(2,128)S(1)} collective-permute-done((s32[2,96]{1,0:T(2,128)S(1)}, s32[2,96]{1,0:T(2,128)S(1)}, u32[]{:S(2)}, u32[]{:S(2)}) %collective-permute-start.4) | collective-permute-done | bytes 800 | tf_op jit(solution)/shard_map/ppermute | solution.py:24
  21.1 0.6 collective-permute-done.3.crossed
  21.8 0.3 shard_map.85
  22.0 0.1 collective-permute-start.7
  22.1 0.2 shard_map.86.after
  22.3 2.1 %collective-permute-start.8 = (bf16[72,1536]{1,0:T(8,128)(2,1)S(1)}, bf16[72,1536]{1,0:T(8,128)(2,1)S(1)}, u32[]{:S(2)}, u32[]{:S(2)}) collective-permute-start(bf16[72,1536]{1,0:T(8,128)(2,1)S(1)} %shard_map.86.after), channel_id=1, source_target_pairs={{0,7},{1,6},{2,5},{3,4},{4,11},{5,10},{6,9},{7,8},{8,15},{9,14},{1... | collective-permute-start | bytes 663560 | tf_op jit(solution)/shard_map/ppermute | solution.py:34
  24.4 0.0 copy-start.5
  24.4 0.0 copy-start.6
  24.5 4.8 %shard_map.87.w2 = bf16[2048,3072]{1,0:T(8,128)(2,1)S(1)} custom-call(bf16[2048,3072]{1,0:T(8,128)(2,1)} %bitcast.30, bf16[72,1536]{1,0:T(8,128)(2,1)S(1)} %shard_map.86.after), custom_call_target="tpu_custom_call" | custom-call | flops 1048576 | bytes 1024 | tf_op jit(solution)/shard_map/pallas_call | solution.py:288
  29.3 0.0 collective-permute-done.1.own.incoming
  29.3 0.0 copy-start.3
  29.3 0.0 copy-done.5
  29.3 0.0 copy-done.6
  29.3 0.8 %shard_map.83 = (bf16[72,3072]{1,0:T(8,128)(2,1)S(1)}, f32[2,96]{1,0:T(2,128)S(1)}) custom-call(bf16[96,3072]{1,0:T(8,128)(2,1)S(1)} %collective-permute-done.1.own.incoming, s32[2,96]{1,0:T(2,128)S(1)} %bitcast_add_fusion.target, s32[2,96]{1,0:T(2,128)S(1)} %bitcast.29, f32[3,3072]{1,0:T(4,128)S(1)} %fusion.mod, bf16[4,3072]{1,0:T(4,128)(2,1)S(1)} %bitcast.28), custom_call_target="tpu_custom_call" | custom-call | flops 1048576 | bytes 1024 | tf_op jit(solution)/shard_map/pallas_call | solution.py:313
  30.1 1.1 %collective-permute-done.5.right = bf16[72,1536]{1,0:T(8,128)(2,1)S(1)} collective-permute-done((bf16[72,1536]{1,0:T(8,128)(2,1)S(1)}, bf16[72,1536]{1,0:T(8,128)(2,1)S(1)}, u32[]{:S(2)}, u32[]{:S(2)}) %collective-permute-start.5) | collective-permute-done | bytes 221216 | tf_op jit(solution)/shard_map/ppermute | solution.py:34
  31.2 3.8 %shard_map.89 = (bf16[72,1632]{1,0:T(8,128)(2,1)S(1)}, bf16[72,2048]{1,0:T(8,128)(2,1)S(1)}) custom-call(bf16[72,1536]{1,0:T(8,128)(2,1)S(1)} %get-tuple-element.28.left, bf16[72,1536]{1,0:T(8,128)(2,1)S(1)} %collective-permute-done.5.right, f32[3,3072]{1,0:T(4,128)S(1)} %fusion.mod, f32[2,96]{1,0:T(2,128)S(1)} %get-tuple-element.23.gates, ...), custom_call_target="tpu_custom_call" | custom-call | flops 1048576 | bytes 1024 | tf_op jit(solution)/shard_map/pallas_call | solution.py:326
  35.0 0.0 copy-done.3
  35.0 0.0 collective-permute-done.2.sib
  35.0 4.6 %shard_map.90 = (bf16[72,3072]{1,0:T(8,128)(2,1)S(1)}, bf16[72,1792]{1,0:T(8,128)(2,1)S(1)}, bf16[72,1280]{1,0:T(8,128)(2,1)S(1)}) custom-call(bf16[72,3072]{1,0:T(8,128)(2,1)S(1)} %get-tuple-element.24.own, bf16[72,3072]{1,0:T(8,128)(2,1)S(1)} %collective-permute-done.2.sib, f32[3,3072]{1,0:T(4,128)S(1)} %fusion.mod, ...), custom_call_target="tpu_custom_call" | custom-call | flops 1048576 | bytes 1024 | tf_op jit(solution)/shard_map/pallas_call | solution.py:371
  39.6 0.1 collective-permute-start.10
  39.7 3.9 %collective-permute-start.6 = (bf16[72,1632]{1,0:T(8,128)(2,1)S(1)}, bf16[72,1632]{1,0:T(8,128)(2,1)S(1)}, u32[]{:S(2)}, u32[]{:S(2)}) collective-permute-start(bf16[72,1632]{1,0:T(8,128)(2,1)S(1)} %get-tuple-element.29.after), channel_id=1, source_target_pairs={{0,2},{1,3},{2,0},{3,1},{4,6},{5,7},{6,4},{7,5},{8,10},{9,11},{10,... | collective-permute-start | bytes 705032 | tf_op jit(solution)/shard_map/ppermute | solution.py:24
  43.6 0.0 collective-permute-done.8.right
  43.6 0.0 collective-permute-done.7.left
  43.6 3.7 %shard_map.91 = (bf16[72,1536]{1,0:T(8,128)(2,1)S(1)}, bf16[72,1536]{1,0:T(8,128)(2,1)S(1)}, bf16[72,2048]{1,0:T(8,128)(2,1)S(1)}) custom-call(bf16[72,1536]{1,0:T(8,128)(2,1)S(1)} %collective-permute-done.7.left, bf16[72,1536]{1,0:T(8,128)(2,1)S(1)} %collective-permute-done.8.right, f32[3,3072]{1,0:T(4,128)S(1)} %fusion.mod, ...), custom_call_target="tpu_custom_call" | custom-call | flops 1048576 | bytes 1024 | tf_op jit(solution)/shard_map/pallas_call | solution.py:343
  47.3 0.1 collective-permute-start.11
  47.5 1.2 %shard_map.92 = bf16[72,1536]{1,0:T(8,128)(2,1)S(1)} custom-call(bf16[72,2048]{1,0:T(8,128)(2,1)S(1)} %get-tuple-element.32.hidden, bf16[2048,3072]{1,0:T(8,128)(2,1)S(1)} %shard_map.87.w2), custom_call_target="tpu_custom_call" | custom-call | flops 1048576 | bytes 1024 | tf_op jit(solution)/shard_map/pallas_call | solution.py:359
  48.7 2.2 %collective-permute-start.9 = (bf16[72,1536]{1,0:T(8,128)(2,1)S(1)}, bf16[72,1536]{1,0:T(8,128)(2,1)S(1)}, u32[]{:S(2)}, u32[]{:S(2)}) collective-permute-start(bf16[72,1536]{1,0:T(8,128)(2,1)S(1)} %shard_map.92), channel_id=1, source_target_pairs={{0,3},{1,2},{2,1},{3,0},{4,7},{5,6},{6,5},{7,4},{8,11},{9,10},{10,... | collective-permute-start | bytes 663560 | tf_op jit(solution)/shard_map/ppermute | solution.py:24
  50.9 8.0 %collective-permute-done.11.there = bf16[72,1536]{1,0:T(8,128)(2,1)S(1)} collective-permute-done((bf16[72,1536]{1,0:T(8,128)(2,1)S(1)}, bf16[72,1536]{1,0:T(8,128)(2,1)S(1)}, u32[]{:S(2)}, u32[]{:S(2)}) %collective-permute-start.11) | collective-permute-done | bytes 221216 | tf_op jit(solution)/shard_map/ppermute | solution.py:24
  58.9 0.0 collective-permute-done.6.y_x.carried
  58.9 0.0 collective-permute-done.10.after.y_first
  58.9 0.3 shard_map.94.after
  59.3 0.1 collective-permute-start.13
  59.4 7.2 %collective-permute-start.12 = (bf16[72,1280]{1,0:T(8,128)(2,1)S(1)}, bf16[72,1280]{1,0:T(8,128)(2,1)S(1)}, u32[]{:S(2)}, u32[]{:S(2)}) collective-permute-start(bf16[72,1280]{1,0:T(8,128)(2,1)S(1)} %shard_map.95), channel_id=1, source_target_pairs={{0,1},{1,0},{2,3},{3,2},{4,5},{5,4},{6,7},{7,6},{8,9},{9,8},{10,11... | collective-permute-start | bytes 552968 | tf_op jit(solution)/shard_map/ppermute | solution.py:24
  66.5 0.0 collective-permute-done.9.y_z
  66.5 0.0 copy-start.4
  66.5 0.5 shard_map.93.mixture
  67.1 4.6 %collective-permute-done.12.y_second = bf16[72,1280]{1,0:T(8,128)(2,1)S(1)} collective-permute-done((bf16[72,1280]{1,0:T(8,128)(2,1)S(1)}, bf16[72,1280]{1,0:T(8,128)(2,1)S(1)}, u32[]{:S(2)}, u32[]{:S(2)}) %collective-permute-start.12) | collective-permute-done | bytes 184352 | tf_op jit(solution)/shard_map/ppermute | solution.py:24
  71.6 0.0 copy-done.4
  71.6 0.4 shard_map.96
  72.0 3.1 %collective-permute-done.13.joint = bf16[96,1536]{1,0:T(8,128)(2,1)S(1)} collective-permute-done((bf16[96,1536]{1,0:T(8,128)(2,1)S(1)}, bf16[96,1536]{1,0:T(8,128)(2,1)S(1)}, u32[]{:S(2)}, u32[]{:S(2)}) %collective-permute-start.13) | collective-permute-done | bytes 294944 | tf_op jit(solution)/shard_map/ppermute | solution.py:24
  75.1 0.9 %shard_map.97 = bf16[96,3072]{1,0:T(8,128)(2,1)} custom-call(f32[3,3072]{1,0:T(4,128)S(1)} %fusion.mod, f32[96,1536]{1,0:T(8,128)S(1)} %get-tuple-element.37.left, bf16[96,1536]{1,0:T(8,128)(2,1)S(1)} %get-tuple-element.38.right, bf16[96,1536]{1,0:T(8,128)(2,1)S(1)} %collective-permute-done.13.joint), custom_call_target="tpu_custom_call" | custom-call | flops 1048576 | bytes 1024 | tf_op jit(solution)/shard_map/pallas_call | solution.py:432
  (3 shorter events, 0.1 us)
Async XLA Ops:
  0.0 8.9 %copy-start = (bf16[50,3,3072]{2,0,1:T(8,128)(2,1)S(1)}, bf16[50,3,3072]{2,0,1:T(8,128)(2,1)}, u32[]{:S(2)}) copy-start(bf16[50,3,3072]{2,0,1:T(8,128)(2,1)} %param.15) | copy-start | bytes 2764804
  0.8 5.8 %collective-permute-start = (s32[2,96]{1,0:T(2,128)S(1)}, s32[2,96]{1,0:T(2,128)S(1)}, u32[]{:S(2)}, u32[]{:S(2)}) collective-permute-start(s32[2,96]{1,0:T(2,128)S(1)} %bitcast_add_fusion.target), channel_id=1, source_target_pairs={{4,0},{8,4},{12,8},{0,12},{5,1},{9,5},{13,9},{1,13},{6,2},{10,6},{... | collective-permute-start | bytes 2312 | tf_op jit(solution)/shard_map/ppermute | solution.py:20
  4.2 17.6 %collective-permute-start.3 = (bf16[96,1536]{1,0:T(8,128)(2,1)S(1)}, bf16[96,1536]{1,0:T(8,128)(2,1)S(1)}, u32[]{:S(2)}, u32[]{:S(2)}) collective-permute-start(bf16[96,1536]{1,0:T(8,128)(2,1)S(1)} %slice.4), channel_id=1, source_target_pairs={{0,6},{1,7},{2,4},{3,5},{4,10},{5,11},{6,8},{7,9},{8,14},{9,15},{1... | collective-permute-start | bytes 884744 | tf_op jit(solution)/shard_map/ppermute | solution.py:34
  6.6 1.1 %copy-start.1 = (bf16[1,96,3072]{2,1,0:T(8,128)(2,1)S(1)}, bf16[1,96,3072]{2,1,0:T(8,128)(2,1)}, u32[]{:S(2)}) copy-start(bf16[1,96,3072]{2,1,0:T(8,128)(2,1)} %param.8) | copy-start | bytes 1769476
  8.0 13.1 %collective-permute-start.4 = (s32[2,96]{1,0:T(2,128)S(1)}, s32[2,96]{1,0:T(2,128)S(1)}, u32[]{:S(2)}, u32[]{:S(2)}) collective-permute-start(s32[2,96]{1,0:T(2,128)S(1)} %get-tuple-element.26), channel_id=1, source_target_pairs={{0,2},{1,3},{2,0},{3,1},{4,6},{5,7},{6,4},{7,5},{8,10},{9,11},{10,... | collective-permute-start | bytes 2312 | tf_op jit(solution)/shard_map/ppermute | solution.py:24
  8.9 26.0 %collective-permute-start.2 = (bf16[72,3072]{1,0:T(8,128)(2,1)S(1)}, bf16[72,3072]{1,0:T(8,128)(2,1)S(1)}, u32[]{:S(2)}, u32[]{:S(2)}) collective-permute-start(bf16[72,3072]{1,0:T(8,128)(2,1)S(1)} %get-tuple-element.25.after), channel_id=1, source_target_pairs={{0,5},{1,4},{2,7},{3,6},{4,9},{5,8},{6,11},{7,10},{8,13},{9,12},{1... | collective-permute-start | bytes 1327112 | tf_op jit(solution)/shard_map/ppermute | solution.py:34
  10.3 18.9 %collective-permute-start.1 = (bf16[96,3072]{1,0:T(8,128)(2,1)S(1)}, bf16[96,3072]{1,0:T(8,128)(2,1)S(1)}, u32[]{:S(2)}, u32[]{:S(2)}) collective-permute-start(bf16[96,3072]{1,0:T(8,128)(2,1)S(1)} %get-tuple-element.22), channel_id=1, source_target_pairs={{12,0},{0,4},{4,8},{8,12},{13,1},{1,5},{5,9},{9,13},{14,2},{2,6},{... | collective-permute-start | bytes 1769480 | tf_op jit(solution)/shard_map/ppermute | solution.py:20
  11.1 4.8 %copy-start.2 = (bf16[1,96,3072]{2,1,0:T(8,128)(2,1)S(1)}, bf16[1,96,3072]{2,1,0:T(8,128)(2,1)}, u32[]{:S(2)}) copy-start(bf16[1,96,3072]{2,1,0:T(8,128)(2,1)} %param.8) | copy-start | bytes 1769476
  16.1 15.1 %collective-permute-start.5 = (bf16[72,1536]{1,0:T(8,128)(2,1)S(1)}, bf16[72,1536]{1,0:T(8,128)(2,1)S(1)}, u32[]{:S(2)}, u32[]{:S(2)}) collective-permute-start(bf16[72,1536]{1,0:T(8,128)(2,1)S(1)} %shard_map.88), channel_id=1, source_target_pairs={{0,6},{1,7},{2,4},{3,5},{4,10},{5,11},{6,8},{7,9},{8,14},{9,15},{1... | collective-permute-start | bytes 663560 | tf_op jit(solution)/shard_map/ppermute | solution.py:34
  22.0 21.6 %collective-permute-start.7 = (bf16[72,1536]{1,0:T(8,128)(2,1)S(1)}, bf16[72,1536]{1,0:T(8,128)(2,1)S(1)}, u32[]{:S(2)}, u32[]{:S(2)}) collective-permute-start(bf16[72,1536]{1,0:T(8,128)(2,1)S(1)} %get-tuple-element.27.after), channel_id=1, source_target_pairs={{0,1},{1,0},{2,3},{3,2},{4,5},{5,4},{6,7},{7,6},{8,9},{9,8},{10,11... | collective-permute-start | bytes 663560 | tf_op jit(solution)/shard_map/ppermute | solution.py:24
  22.3 21.3 %collective-permute-start.8 = (bf16[72,1536]{1,0:T(8,128)(2,1)S(1)}, bf16[72,1536]{1,0:T(8,128)(2,1)S(1)}, u32[]{:S(2)}, u32[]{:S(2)}) collective-permute-start(bf16[72,1536]{1,0:T(8,128)(2,1)S(1)} %shard_map.86.after), channel_id=1, source_target_pairs={{0,7},{1,6},{2,5},{3,4},{4,11},{5,10},{6,9},{7,8},{8,15},{9,14},{1... | collective-permute-start | bytes 663560 | tf_op jit(solution)/shard_map/ppermute | solution.py:34
  24.4 4.9 %copy-start.5 = (bf16[1,3072,4]{1,2,0:T(4,128)(2,1)S(1)}, bf16[1,3072,4]{1,2,0:T(4,128)(2,1)}, u32[]{:S(2)}) copy-start(bf16[1,3072,4]{1,2,0:T(4,128)(2,1)} %param.12) | copy-start | bytes 73732
  24.4 4.9 %copy-start.6 = (s32[1,96,2]{1,2,0:T(2,128)S(1)}, s32[1,96,2]{1,2,0:T(2,128)}, u32[]{:S(2)}) copy-start(s32[1,96,2]{1,2,0:T(2,128)} %param.9) | copy-start | bytes 2308
  29.3 5.7 %copy-start.3 = (bf16[96,3072]{1,0:T(8,128)(2,1)}, bf16[96,3072]{1,0:T(8,128)(2,1)S(1)}, u32[]{:S(2)}) copy-start(bf16[96,3072]{1,0:T(8,128)(2,1)S(1)} %collective-permute-done.1.own.incoming) | copy-start | bytes 1769476
  39.6 19.3 %collective-permute-start.10 = (bf16[72,1792]{1,0:T(8,128)(2,1)S(1)}, bf16[72,1792]{1,0:T(8,128)(2,1)S(1)}, u32[]{:S(2)}, u32[]{:S(2)}) collective-permute-start(bf16[72,1792]{1,0:T(8,128)(2,1)S(1)} %get-tuple-element.33), channel_id=1, source_target_pairs={{0,1},{1,0},{2,3},{3,2},{4,5},{5,4},{6,7},{7,6},{8,9},{9,8},{10,11... | collective-permute-start | bytes 774152 | tf_op jit(solution)/shard_map/ppermute | solution.py:24
  39.7 19.2 %collective-permute-start.6 = (bf16[72,1632]{1,0:T(8,128)(2,1)S(1)}, bf16[72,1632]{1,0:T(8,128)(2,1)S(1)}, u32[]{:S(2)}, u32[]{:S(2)}) collective-permute-start(bf16[72,1632]{1,0:T(8,128)(2,1)S(1)} %get-tuple-element.29.after), channel_id=1, source_target_pairs={{0,2},{1,3},{2,0},{3,1},{4,6},{5,7},{6,4},{7,5},{8,10},{9,11},{10,... | collective-permute-start | bytes 705032 | tf_op jit(solution)/shard_map/ppermute | solution.py:24
  47.3 11.6 %collective-permute-start.11 = (bf16[72,1536]{1,0:T(8,128)(2,1)S(1)}, bf16[72,1536]{1,0:T(8,128)(2,1)S(1)}, u32[]{:S(2)}, u32[]{:S(2)}) collective-permute-start(bf16[72,1536]{1,0:T(8,128)(2,1)S(1)} %get-tuple-element.36), channel_id=1, source_target_pairs={{0,1},{1,0},{2,3},{3,2},{4,5},{5,4},{6,7},{7,6},{8,9},{9,8},{10,11... | collective-permute-start | bytes 663560 | tf_op jit(solution)/shard_map/ppermute | solution.py:24
  48.7 17.8 %collective-permute-start.9 = (bf16[72,1536]{1,0:T(8,128)(2,1)S(1)}, bf16[72,1536]{1,0:T(8,128)(2,1)S(1)}, u32[]{:S(2)}, u32[]{:S(2)}) collective-permute-start(bf16[72,1536]{1,0:T(8,128)(2,1)S(1)} %shard_map.92), channel_id=1, source_target_pairs={{0,3},{1,2},{2,1},{3,0},{4,7},{5,6},{6,5},{7,4},{8,11},{9,10},{10,... | collective-permute-start | bytes 663560 | tf_op jit(solution)/shard_map/ppermute | solution.py:24
  59.3 15.8 %collective-permute-start.13 = (bf16[96,1536]{1,0:T(8,128)(2,1)S(1)}, bf16[96,1536]{1,0:T(8,128)(2,1)S(1)}, u32[]{:S(2)}, u32[]{:S(2)}) collective-permute-start(bf16[96,1536]{1,0:T(8,128)(2,1)S(1)} %shard_map.94.after), channel_id=1, source_target_pairs={{0,2},{1,3},{2,0},{3,1},{4,6},{5,7},{6,4},{7,5},{8,10},{9,11},{10,... | collective-permute-start | bytes 884744 | tf_op jit(solution)/shard_map/ppermute | solution.py:24
  59.4 12.3 %collective-permute-start.12 = (bf16[72,1280]{1,0:T(8,128)(2,1)S(1)}, bf16[72,1280]{1,0:T(8,128)(2,1)S(1)}, u32[]{:S(2)}, u32[]{:S(2)}) collective-permute-start(bf16[72,1280]{1,0:T(8,128)(2,1)S(1)} %shard_map.95), channel_id=1, source_target_pairs={{0,1},{1,0},{2,3},{3,2},{4,5},{5,4},{6,7},{7,6},{8,9},{9,8},{10,11... | collective-permute-start | bytes 552968 | tf_op jit(solution)/shard_map/ppermute | solution.py:24
  66.5 5.1 %copy-start.4 = (bf16[96,3072]{1,0:T(8,128)(2,1)S(1)}, bf16[96,3072]{1,0:T(8,128)(2,1)}, u32[]{:S(2)}) copy-start(bf16[96,3072]{1,0:T(8,128)(2,1)} %copy-done.3) | copy-start | bytes 1769476
